TPU v7x, 512 devices: a whole 4x4x16 slice. The times are simulated.
512 devices in a mesh: row: 16 (over x, y), col: 32 (over z, core).
Axes of the slice: x: 4, y: 4, z: 16, core: 2. Of those that a mesh axis runs over, the one named last changes fastest.
Arguments:
- covariates: bfloat16 [131072, 4096], P('row', 'col'), may hold values from -64 to 64
- labels: int32 [131072], P('row'), may hold values from 0 to 15
- weights: float32 [16, 4096], P(None, 'col'), may hold values from -0.0234375 to 0.0234375
- sample_index: int32 [65536], P('row'), may hold values from 0 to 131071, as said below
Outputs:
- gradient: float32 [16, 4096], P(None, 'col')
- newton_step: float32 [16, 4096], P(None, 'col')
Inputs may be any that keep to these rules, and one draw needn't show every extreme that they name: The 4096 entries sample_index[b * 4096] to sample_index[(b + 1) * 4096 - 1] name users b * 8192 to (b + 1) * 8192 - 1; repeats may occur.
All inputs are finite; a program needn't handle non-finite values.
Results may differ from a plain program's by a relative error of at most 0.0039.
Values may be sent and summed in bfloat16 or wider, within the bound.
No kernel may reach another device: no remote copies, remote signals or barrier semaphores. Data moves between devices by JAX's collectives and lax.ppermute only.
A program may use at most 64 MiB of HBM per device.

v0:
```python
import jax
import jax.numpy as jnp
from jax import lax
from jax.sharding import PartitionSpec as P

ITERS = 2


RIDGE_WEIGHT = 0.004


def class_shares(logits):
    exponent = jnp.exp(logits)
    return exponent / jnp.sum(exponent, axis=0, keepdims=True)


def body(covariates, labels, weights, sample_index):
    user_rows = covariates.shape[0]
    col_width = covariates.shape[1]
    row_count = lax.axis_size("row")
    sub_rows_dev = sample_index.shape[0]
    first_user = lax.axis_index("row") * user_rows
    own_width = col_width // row_count
    own_start = lax.axis_index("row") * own_width
    rounded_weights = weights.astype(jnp.bfloat16)
    within = sample_index - first_user
    sub_rows = jnp.take(covariates, within, axis=0)
    partial_value = lax.dot_general(
        rounded_weights, covariates, (((1,), (1,)), ((), ())), preferred_element_type=jnp.float32
    )
    logits = lax.psum(partial_value, "col")
    shares = class_shares(logits)
    classes = lax.broadcasted_iota(jnp.int32, shares.shape, 0)
    indicator = (labels[None, :] == classes).astype(jnp.float32)
    misfit = (shares - indicator).astype(jnp.bfloat16)
    sub_shares = jnp.take(shares, within, axis=1)
    grad_term = jnp.dot(misfit, covariates, preferred_element_type=jnp.float32)
    gradient = lax.psum(grad_term, "row") / (user_rows * row_count) + RIDGE_WEIGHT * weights
    sub_total = sub_rows_dev * row_count

    def own_columns(vector):
        return lax.dynamic_slice_in_dim(vector, own_start, own_width, 1)

    def local_inner(first_vec, second_vec):
        return jnp.sum(own_columns(first_vec) * own_columns(second_vec))

    residual = -gradient
    direction = residual
    newton_step = jnp.zeros_like(residual)
    norm_now = lax.psum(local_inner(residual, residual), ("row", "col"))
    for iteration in range(ITERS):
        rounded = direction.astype(jnp.bfloat16)
        partial_response = lax.dot_general(
            rounded, sub_rows, (((1,), (1,)), ((), ())), preferred_element_type=jnp.float32
        )
        response = lax.psum(partial_response, "col")
        centred = response - jnp.sum(sub_shares * response, axis=0, keepdims=True)
        weighted = (sub_shares * centred).astype(jnp.bfloat16)
        summed = lax.psum(jnp.dot(weighted, sub_rows, preferred_element_type=jnp.float32), "row")
        image = summed / sub_total + RIDGE_WEIGHT * direction
        curve = lax.psum(local_inner(direction, image), ("row", "col"))
        step_size = norm_now / curve
        newton_step = newton_step + step_size * direction
        residual = residual - step_size * image
        if iteration + 1 < ITERS:
            norm_new = lax.psum(local_inner(residual, residual), ("row", "col"))
            direction = residual + norm_new / norm_now * direction
            norm_now = norm_new
    return (gradient, newton_step)


def solution(mesh):
    in_specs = (P("row", "col"), P("row"), P(None, "col"), P("row"))
    out_specs = (P(None, "col"), P(None, "col"))
    return jax.shard_map(body, mesh=mesh, in_specs=in_specs, out_specs=out_specs, check_vma=False)
```

profile of v0, /device:TPU:1, one launch (start us, length us, event | category | flops | bytes accessed | tf_op | source)
XLA Modules:
  0.0 1073.0 jit_solution(5783098514605044032)
XLA Ops:
  7.2 0.0 copy-start
  7.2 0.0 copy-start.3
  7.2 0.0 all-reduce.5.cloned.1.call-start
  7.2 1.5 copy-done
  8.8 2.2 fusion.24
  10.9 0.0 all-reduce.5.cloned.1.call-update
  11.0 0.0 all-reduce.7.cloned.1.call-start
  11.0 0.0 copy-done.3
  11.0 0.0 copy-start.5
  11.0 14.9 %gather_fusion.1 = bf16[4096,128]{1,0:T(8,128)(2,1)} fusion(bf16[8192,128]{1,0:T(8,128)(2,1)S(1)} %copy-done, s32[4096]{0:T(1024)S(1)} %fusion.16), kind=kCustom, calls=%fused_computation.1 | custom fusion | bytes 2113536 | tf_op jit(solution)/shard_map/jit(_take)/gather | solution.py:27
  26.0 0.0 copy-start.4
  26.0 198.4 %all-reduce.5.cloned.1.call-done = f32[16,8192]{1,0:T(8,128)} async-done(((f32[16,8192]{1,0:T(8,128)}), f32[16,8192]{1,0:T(8,128)}) %all-reduce.5.cloned.1.call-update) | async-done | bytes 524304 | tf_op jit(solution)/shard_map/psum | solution.py:31
  224.4 1.2 exponential_reduce_fusion
  225.5 1.2 exponential_divide_fusion
  226.7 0.0 copy-done.5
  226.7 0.4 fusion
  227.1 33.8 %psum.71 = f32[16,128]{1,0:T(8,128)S(1)} all-reduce(f32[16,128]{1,0:T(8,128)S(1)} %fusion), channel_id=1, replica_groups=mesh['row'=16,'col'=32] {'row'}, use_global_device_ids=true, to_apply=%region_2.3 | all-reduce | flops 2048 | bytes 16384 | tf_op jit(solution)/shard_map/psum | solution.py:38
  260.9 0.0 copy-done.4
  261.0 0.0 copy-start.2
  261.0 2.6 fusion.22
  263.6 0.0 all-reduce.7.cloned.1.call-update
  263.6 0.0 all-reduce.9.cloned.1.call-start
  263.7 2.6 copy.6
  266.3 0.0 copy-start.1
  266.3 16.4 %gather_fusion = f32[4096,16]{1,0:T(8,128)} fusion(f32[16,8192]{0,1:T(8,128)} %copy.6, s32[4096]{0:T(1024)S(1)} %fusion.16), kind=kCustom, calls=%fused_computation | custom fusion | bytes 540672 | tf_op jit(solution)/shard_map/jit(_take)/gather | solution.py:36
  282.6 2.2 copy.7
  284.8 187.2 %all-reduce.7.cloned.1.call-done = f32[16,4096]{1,0:T(8,128)} async-done(((f32[16,4096]{1,0:T(8,128)}), f32[16,4096]{1,0:T(8,128)}) %all-reduce.7.cloned.1.call-update) | async-done | bytes 262160 | tf_op jit(solution)/shard_map/psum | solution.py:56
  472.0 1.0 fusion.1
  473.0 0.0 copy-done.1
  473.0 1.7 fusion.8
  474.7 33.8 %psum.74 = f32[16,128]{1,0:T(8,128)S(1)} all-reduce(f32[16,128]{1,0:T(8,128)S(1)} %fusion.8), channel_id=1, replica_groups=mesh['row'=16,'col'=32] {'row'}, use_global_device_ids=true, to_apply=%region_7.8 | all-reduce | flops 2048 | bytes 16384 | tf_op jit(solution)/shard_map/psum | solution.py:59
  508.5 0.8 multiply_reduce_fusion.1
  509.2 105.0 %all-reduce = (f32[]{:T(128)}, f32[]{:T(128)}) all-reduce(f32[]{:T(128)} %get-tuple-element.3, f32[]{:T(128)} %get-tuple-element.2), channel_id=1, replica_groups=mesh['row'=16,'col'=32] {'row','col'}, use_global_device_ids=true, to_apply=%region_4.5 | all-reduce | flops 2 | bytes 16 | tf_op jit(solution)/shard_map/psum | solution.py:50
  615.5 0.7 multiply_reduce_fusion
  616.2 102.3 %psum.76 = f32[]{:T(128)} all-reduce(f32[]{:T(128)} %multiply_reduce_fusion), channel_id=1, replica_groups=mesh['row'=16,'col'=32] {'row','col'}, use_global_device_ids=true, to_apply=%region_11.12 | all-reduce | flops 1 | bytes 8 | tf_op jit(solution)/shard_map/psum | solution.py:66
  719.8 1.6 fusion.20
  721.4 0.0 all-reduce.9.cloned.1.call-update
  721.4 200.9 %all-reduce.9.cloned.1.call-done = f32[16,4096]{1,0:T(8,128)} async-done(((f32[16,4096]{1,0:T(8,128)}), f32[16,4096]{1,0:T(8,128)}) %all-reduce.9.cloned.1.call-update) | async-done | bytes 262160 | tf_op jit(solution)/shard_map/psum | solution.py:56
  922.3 1.0 fusion.3
  923.3 1.7 fusion.6
  925.0 33.8 %psum.78 = f32[16,128]{1,0:T(8,128)S(1)} all-reduce(f32[16,128]{1,0:T(8,128)S(1)} %fusion.6), channel_id=1, replica_groups=mesh['row'=16,'col'=32] {'row'}, use_global_device_ids=true, to_apply=%region_14.15 | all-reduce | flops 2048 | bytes 16384 | tf_op jit(solution)/shard_map/psum | solution.py:59
  958.8 0.8 fusion.19
  959.5 105.0 %psum.79 = f32[]{:T(128)} all-reduce(f32[]{:T(128)} %fusion.19), channel_id=1, replica_groups=mesh['row'=16,'col'=32] {'row','col'}, use_global_device_ids=true, to_apply=%region_16.17 | all-reduce | flops 1 | bytes 8 | tf_op jit(solution)/shard_map/psum | solution.py:61
  1065.9 0.0 copy-done.2
  1065.9 0.6 multiply_add_fusion
  (6 shorter events, 0.0 us)
Async XLA Ops:
  7.2 1.6 copy-start
  7.2 3.8 copy-start.3
  7.2 217.2 %all-reduce.5.cloned.1.call-start = ((), (), s32[]{:S(2)}) async-start(), calls=%async_computation | async-start | bytes 1048576 | tf_op jit(solution)/shard_map/psum | solution.py:31
  11.0 461.0 %all-reduce.7.cloned.1.call-start = ((), (), s32[]{:S(2)}) async-start(), calls=%async_computation.1 | async-start | bytes 524288 | tf_op jit(solution)/shard_map/psum | solution.py:56
  11.0 215.7 %copy-start.5 = (s32[8192]{0:T(1024)S(1)}, s32[8192]{0:T(1024)}, u32[]{:S(2)}) copy-start(s32[8192]{0:T(1024)} %param.5) | copy-start | bytes 98308
  26.0 235.0 %copy-start.4 = (f32[16,128]{1,0:T(8,128)S(1)}, f32[16,128]{1,0:T(8,128)}, u32[]{:S(2)}) copy-start(f32[16,128]{1,0:T(8,128)} %param.6) | copy-start | bytes 24580
  261.0 804.9 %copy-start.2 = (f32[16,128]{1,0:T(8,128)}, f32[16,128]{1,0:T(8,128)S(1)}, u32[]{:S(2)}) copy-start(f32[16,128]{1,0:T(8,128)S(1)} %get-tuple-element.7) | copy-start | bytes 24580
  263.6 658.7 %all-reduce.9.cloned.1.call-start = ((), (), s32[]{:S(2)}) async-start(), calls=%async_computation.2 | async-start | bytes 524288 | tf_op jit(solution)/shard_map/psum | solution.py:56
  266.3 206.7 %copy-start.1 = (bf16[4096,128]{1,0:T(8,128)(2,1)S(1)}, bf16[4096,128]{1,0:T(8,128)(2,1)}, u32[]{:S(2)}) copy-start(bf16[4096,128]{1,0:T(8,128)(2,1)} %gather_fusion.1) | copy-start | bytes 3145732
Sparse Core Ops, SparseCore 0:
  11.1 213.2 all-reduce.4
  263.8 208.1 all-reduce.6
  721.5 200.7 all-reduce.8
where the time goes:
time: 1070 us
  waiting for transfers between devices  586 us (55%)
  blocking collectives  414 us (39%)
  local copies, waits for them, and re-layouts  37.6 us (4%)
  between operations  17.8 us (2%)
    psum x2, waiting for transfers between devices, body(): response = lax.psum(partial_response, 'col')  388 us
    psum x1, waiting for transfers between devices, body(): logits = lax.psum(partial_value, 'col')  198 us
    psum x1, blocking collectives, body(): norm_now = lax.psum(local_inner(residual, residual), ('row', 'col'))  105 us
    psum x1, blocking collectives, body(): curve = lax.psum(local_inner(direction, image), ('row', 'col'))  105 us
    psum x1, blocking collectives, body(): norm_new = lax.psum(local_inner(residual, residual), ('row', 'col'))  102 us
    psum x2, blocking collectives, body(): lax.psum(jnp.dot(weighted, sub_rows, preferred_element_type=jnp.float32),...  67.6 us
    psum x1, blocking collectives, body(): lax.psum(grad_term, 'row') / (user_rows * row_count)  33.8 us
  transfers between devices with their start and end apart: 3, of which 3 were waited for; matrix products, arithmetic and copies ran while one was open for 3% of the time, Pallas kernels for 0%

commit v1 on v0

v1 whole, which is shorter than its diff:
```python
import jax
import jax.numpy as jnp
from jax import lax
from jax.sharding import Mesh, PartitionSpec as P

RIDGE_WEIGHT = 0.004


def class_shares(logits):
    exponent = jnp.exp(logits)
    return exponent / jnp.sum(exponent, axis=0, keepdims=True)


def swap(block, axis):
    return lax.all_to_all(block, axis, 0, 0, tiled=True)


def spread(block, axis):
    return swap(jnp.broadcast_to(block[None], (lax.axis_size(axis),) + block.shape), axis)


def total(block, axis):
    return jnp.sum(spread(block, axis), axis=0)


def body(covariates, labels, weights, sample_index):
    user_rows, col_width = covariates.shape
    row_count, depth, cores = lax.axis_size("row"), lax.axis_size("z"), lax.axis_size("c")
    row, level, core = lax.axis_index("row"), lax.axis_index("z"), lax.axis_index("c")
    users = user_rows * row_count
    sub_total = sample_index.shape[0] * row_count
    half = user_rows // cores
    own = half // depth
    first_own = core * half + level * own
    classes = weights.shape[0]

    other = lax.dynamic_slice_in_dim(covariates, (1 - core) * half, half, 0)
    other = lax.ppermute(other, "c", [(0, 1), (1, 0)])
    mine = lax.dynamic_slice_in_dim(covariates, core * half, half, 0)
    wide = jnp.where(core == 0, jnp.concatenate([mine, other], 1), jnp.concatenate([other, mine], 1))
    wide_weights = lax.all_gather(weights, "c", axis=1, tiled=True)

    position = row * user_rows + first_own + jnp.arange(own, dtype=jnp.int32)
    count = jnp.sum((sample_index[:, None] == position[None, :]).astype(jnp.float32), axis=0)

    def pieces(values):
        return values.reshape(classes, depth, own).transpose(1, 0, 2)

    def reduce_users(values):
        return jnp.sum(swap(pieces(values).astype(jnp.bfloat16), "z").astype(jnp.float32), axis=0)

    def back_to_columns(block):
        gathered = spread(block.astype(jnp.bfloat16), "z").transpose(1, 0, 2).reshape(classes, half)
        part = jnp.dot(gathered, wide, preferred_element_type=jnp.float32)
        part = jnp.sum(lax.all_gather(part, "c", axis=0), axis=0)
        return total(part, "row")

    def respond(vector):
        return lax.dot_general(
            vector.astype(jnp.bfloat16), wide, (((1,), (1,)), ((), ())), preferred_element_type=jnp.float32
        )

    partial_value = lax.dot_general(
        weights.astype(jnp.bfloat16), covariates, (((1,), (1,)), ((), ())), preferred_element_type=jnp.float32
    )
    both = lax.all_gather(partial_value.astype(jnp.bfloat16), "c", axis=0)
    both = lax.dynamic_slice_in_dim(both, core * half, half, 2).astype(jnp.float32)
    logits = reduce_users(jnp.sum(both, axis=0))
    shares = class_shares(logits)
    own_labels = lax.dynamic_slice_in_dim(labels, first_own, own, 0)
    indicator = own_labels[None, :] == lax.broadcasted_iota(jnp.int32, shares.shape, 0)
    misfit = shares - indicator.astype(jnp.float32)
    gradient = back_to_columns(misfit) / users + RIDGE_WEIGHT * wide_weights

    residual = -gradient
    response = reduce_users(respond(residual))
    centred = response - jnp.sum(shares * response, axis=0, keepdims=True)
    image = back_to_columns(count * shares * centred) / sub_total + RIDGE_WEIGHT * residual

    scalars = jnp.stack([jnp.sum(residual * residual), jnp.sum(residual * image), jnp.sum(image * image)])
    scalars = total(jnp.pad(scalars, (0, 125))[None], "z")[0]
    image_response = reduce_users(respond(image))
    norm_0, curve_0, image_norm = scalars[0], scalars[1], scalars[2]
    step_0 = norm_0 / curve_0
    beta = jnp.maximum(image_norm / curve_0 * step_0 - 1.0, 0.0)
    residual_1 = residual - step_0 * image
    direction_1 = residual_1 + beta * residual
    response_1 = (1.0 + beta) * response - step_0 * image_response
    centred_1 = response_1 - jnp.sum(shares * response_1, axis=0, keepdims=True)
    spread_1 = jnp.sum(count * shares * centred_1 * centred_1)
    last = jnp.stack([jnp.sum(residual_1 * residual_1), jnp.sum(direction_1 * direction_1), spread_1])
    last = total(jnp.pad(last, (0, 125))[None], "z")
    last = total(last, ("row", "c"))[0]
    copies = row_count * cores
    norm_1, square_1 = last[0] / copies, last[1] / copies
    curve_1 = last[2] / sub_total + RIDGE_WEIGHT * square_1
    newton_step = step_0 * residual + norm_1 / curve_1 * direction_1

    def own_columns(block):
        return lax.dynamic_slice_in_dim(block, core * col_width, col_width, 1)

    return (own_columns(gradient), own_columns(newton_step))


def solution(mesh):
    cores = 2
    rows, cols = mesh.devices.shape
    fine = Mesh(mesh.devices.reshape(rows, cols // cores, cores), ("row", "z", "c"))
    in_specs = (P("row", ("z", "c")), P("row"), P(None, ("z", "c")), P("row"))
    out_specs = (P(None, ("z", "c")), P(None, ("z", "c")))
    return jax.shard_map(body, mesh=fine, in_specs=in_specs, out_specs=out_specs, check_vma=False)
```

time: 1070 us -> 201 us (0.19)
  waiting for transfers between devices: 586 us -> 59.8 us
  blocking collectives: 414 us -> 65.1 us
  starting transfers between devices: 0.12 us -> 44.8 us
  local copies, waits for them, and re-layouts: 37.6 us -> 8.92 us
  between operations: 17.8 us -> 5.65 us
    psum x3 -> x0, waiting for transfers between devices: 586 us -> none  [the longest x2 388 us: body(): response = lax.psum(partial_response, 'col')]
    psum x6 -> x0, blocking collectives: 414 us -> none  [the longest x1 105 us: body(): norm_now = lax.psum(local_inner(residual, residual), ('row', 'col'))]
    all_to_all x0 -> x7, waiting for transfers between devices: none -> 59.8 us  [swap(): return lax.all_to_all(block, axis, 0, 0, tiled=True)]
    all_to_all x0 -> x3, blocking collectives: none -> 43.6 us  [swap(): return lax.all_to_all(block, axis, 0, 0, tiled=True)]
    all_to_all x0 -> x7, starting transfers between devices: none -> 42.2 us  [swap(): return lax.all_to_all(block, axis, 0, 0, tiled=True)]
    gather x3 -> x0, local copies, waits for them, and re-layouts: 33.4 us -> none  [the longest x2 18.5 us: body(): sub_shares = jnp.take(shares, within, axis=1)]
    all_gather x0 -> x4, blocking collectives: none -> 21.4 us  [the longest x2 10.6 us: back_to_columns(): part = jnp.sum(lax.all_gather(part, 'c', axis=0), axis=0)]
  transfers between devices with their start and end apart: 3 -> 8, of which waited for: 3 -> 7; matrix products, arithmetic and copies ran while one was open for 3% -> 4% of each run, Pallas kernels for 0% -> 0%
where the time goes in v1:
time: 201 us; the launch traced here: 200 us
  blocking collectives  65.1 us (32%)
  waiting for transfers between devices  59.8 us (30%)
  starting transfers between devices  44.8 us (22%)
  other arithmetic  11.1 us (6%)
  local copies, waits for them, and re-layouts  8.92 us (4%)
  between operations  5.65 us (3%)
  matrix products  4.45 us (2%)
    all_to_all x7, waiting for transfers between devices, swap(): return lax.all_to_all(block, axis, 0, 0, tiled=True)  59.8 us
    all_to_all x3, blocking collectives, swap(): return lax.all_to_all(block, axis, 0, 0, tiled=True)  43.6 us
    all_to_all x7, starting transfers between devices, swap(): return lax.all_to_all(block, axis, 0, 0, tiled=True)  42.2 us
    all_gather x2, blocking collectives, back_to_columns(): part = jnp.sum(lax.all_gather(part, 'c', axis=0), axis=0)  10.6 us
    all_gather x1, blocking collectives, body(): both = lax.all_gather(partial_value.astype(jnp.bfloat16), 'c', axis=0)  8.7 us
  transfers between devices with their start and end apart: 8, of which 7 were waited for; matrix products, arithmetic and copies ran while one was open for 4% of the time, Pallas kernels for 0%

profile of v1, /device:TPU:1, one launch (start us, length us, event | category | flops | bytes accessed | tf_op | source)
XLA Modules:
  0.0 199.8 jit_solution(5296459045223915805)
XLA Ops:
  0.6 0.0 copy-start
  0.6 2.4 %convolution_convert_fusion = bf16[16,8192]{1,0:T(8,128)(2,1)S(1)} fusion(bf16[8192,128]{1,0:T(8,128)(2,1)} %param.4, f32[16,128]{1,0:T(8,128)} %param.6), kind=kOutput, calls=%fused_computation | convolution fusion | flops 33687552 | bytes 2367488 | tf_op jit(solution)/shard_map/dot_general | solution.py:63
  3.0 8.7 %all-gather = bf16[32,8192]{1,0:T(8,128)(2,1)S(1)} all-gather(bf16[16,8192]{1,0:T(8,128)(2,1)S(1)} %convolution_convert_fusion), channel_id=2, replica_groups=mesh['row'=16,'z'=16,'c'=2] {'c'}, dimensions={0}, use_global_device_ids=true | all-gather | bytes 786432 | tf_op jit(solution)/shard_map/all_gather | solution.py:66
  11.8 0.7 copy.20
  12.5 9.5 %all-to-all-start = ((bf16[16,16,256]{2,1,0:T(8,128)(2,1)}), bf16[16,16,256]{2,1,0:T(8,128)(2,1)S(1)}, u32[]{:S(2)}, u32[]{:S(2)}) async-start(bf16[16,16,256]{2,1,0:T(8,128)(2,1)} %copy.20), calls=%async_computation | async-start | bytes 262144 | tf_op jit(solution)/shard_map/all_to_all | solution.py:15
  22.1 0.0 copy-done
  22.1 1.1 constant_dynamic-slice_fusion.2
  23.2 2.5 %collective-permute-start = (bf16[4096,128]{1,0:T(8,128)(2,1)}, bf16[4096,128]{1,0:T(8,128)(2,1)S(1)}, u32[]{:S(2)}, u32[]{:S(2)}) collective-permute-start(bf16[4096,128]{1,0:T(8,128)(2,1)} %get-tuple-element.10), channel_id=1, source_target_pairs={{0,1},{1,0},{2,3},{3,2},{4,5},{5,4},{6,7},{7,6},{8,9},{9,8},{10,11... | collective-permute-start | bytes 3145736 | tf_op jit(solution)/shard_map/ppermute | solution.py:38
  25.8 0.8 dynamic_slice.19
  26.5 7.7 %all-to-all-done = bf16[16,16,256]{2,1,0:T(8,128)(2,1)S(1)} async-done(((bf16[16,16,256]{2,1,0:T(8,128)(2,1)}), bf16[16,16,256]{2,1,0:T(8,128)(2,1)S(1)}, u32[]{:S(2)}, u32[]{:S(2)}) %all-to-all-start) | async-done | bytes 131104 | tf_op jit(solution)/shard_map/all_to_all | solution.py:15
  34.3 0.7 broadcast_in_dim.14
  34.9 6.5 %all-to-all-start.1 = ((bf16[16,16,256]{2,1,0:T(8,128)(2,1)}), bf16[16,16,256]{2,1,0:T(8,128)(2,1)S(1)}, u32[]{:S(2)}, u32[]{:S(2)}) async-start(bf16[16,16,256]{2,1,0:T(8,128)(2,1)} %broadcast_in_dim.14), calls=%async_computation.1 | async-start | bytes 262144 | tf_op jit(solution)/shard_map/all_to_all | solution.py:15
  41.4 12.0 %all-to-all-done.1 = bf16[16,16,256]{2,1,0:T(8,128)(2,1)S(1)} async-done(((bf16[16,16,256]{2,1,0:T(8,128)(2,1)}), bf16[16,16,256]{2,1,0:T(8,128)(2,1)S(1)}, u32[]{:S(2)}, u32[]{:S(2)}) %all-to-all-start.1) | async-done | bytes 131104 | tf_op jit(solution)/shard_map/all_to_all | solution.py:15
  53.4 0.0 collective-permute-done
  53.4 0.0 copy-start.1
  53.4 1.0 copy-done.1
  54.4 2.1 %maximum_select_fusion = bf16[4096,256]{1,0:T(8,128)(2,1)S(1)} fusion(bf16[4096,128]{1,0:T(8,128)(2,1)} %copy-done.1, bf16[4096,128]{1,0:T(8,128)(2,1)S(1)} %get-tuple-element.9, pred[]{:T(512)S(6)} %eq.30), kind=kLoop, calls=%fused_computation.4 | loop fusion | flops 9437184 | bytes 4194305 | tf_op jit(solution)/shard_map/jit(_where)/select_n | solution.py:40
  56.5 0.0 copy-start.2
  56.6 0.4 fusion.10
  56.9 0.0 copy-start.3
  56.9 5.3 %all-gather.1 = f32[32,256]{1,0:T(8,128)S(1)} all-gather(f32[16,256]{1,0:T(8,128)S(1)} %fusion.10), channel_id=3, replica_groups=mesh['row'=16,'z'=16,'c'=2] {'c'}, dimensions={0}, use_global_device_ids=true | all-gather | bytes 49152 | tf_op jit(solution)/shard_map/all_gather | solution.py:55
  62.3 0.7 broadcast_in_dim.15
  63.0 6.8 %all-to-all-start.2 = ((f32[16,16,256]{2,1,0:T(8,128)}), f32[16,16,256]{2,1,0:T(8,128)S(1)}, u32[]{:S(2)}, u32[]{:S(2)}) async-start(f32[16,16,256]{2,1,0:T(8,128)} %broadcast_in_dim.15), calls=%async_computation.2 | async-start | bytes 524288 | tf_op jit(solution)/shard_map/all_to_all | solution.py:15
  69.7 0.0 copy-done.2
  69.7 2.1 %all_gather.25 = f32[16,256]{1,0:T(8,128)S(1)} all-gather(f32[16,128]{1,0:T(8,128)S(1)} %copy-done.2), channel_id=1, replica_groups=mesh['row'=16,'z'=16,'c'=2] {'c'}, dimensions={1}, use_global_device_ids=true | all-gather | bytes 24576 | tf_op jit(solution)/shard_map/all_gather | solution.py:41
  71.9 5.5 %all-to-all-done.2 = f32[16,16,256]{2,1,0:T(8,128)S(1)} async-done(((f32[16,16,256]{2,1,0:T(8,128)}), f32[16,16,256]{2,1,0:T(8,128)S(1)}, u32[]{:S(2)}, u32[]{:S(2)}) %all-to-all-start.2) | async-done | bytes 262176 | tf_op jit(solution)/shard_map/all_to_all | solution.py:15
  77.4 0.6 convolution_convert_fusion.2
  78.0 0.7 copy.36
  78.7 3.5 %all-to-all-start.3 = ((bf16[16,16,256]{2,1,0:T(8,128)(2,1)}), bf16[16,16,256]{2,1,0:T(8,128)(2,1)S(1)}, u32[]{:S(2)}, u32[]{:S(2)}) async-start(bf16[16,16,256]{2,1,0:T(8,128)(2,1)} %bitcast.47), calls=%async_computation.3 | async-start | bytes 262144 | tf_op jit(solution)/shard_map/all_to_all | solution.py:15
  82.2 0.0 copy-done.3
  82.2 1.9 convert_reduce_fusion
  84.1 10.1 %all-to-all-done.3 = bf16[16,16,256]{2,1,0:T(8,128)(2,1)S(1)} async-done(((bf16[16,16,256]{2,1,0:T(8,128)(2,1)}), bf16[16,16,256]{2,1,0:T(8,128)(2,1)S(1)}, u32[]{:S(2)}, u32[]{:S(2)}) %all-to-all-start.3) | async-done | bytes 131104 | tf_op jit(solution)/shard_map/all_to_all | solution.py:15
  94.3 16.9 %all_to_all.50 = bf16[16,16,256]{2,1,0:T(8,128)(2,1)S(1)} all-to-all(bf16[16,16,256]{2,1,0:T(8,128)(2,1)S(1)} %broadcast_in_dim.16), channel_id=1, replica_groups=mesh['row'=16,'z'=16,'c'=2] {'z'}, dimensions={0} | all-to-all | bytes 262144 | tf_op jit(solution)/shard_map/all_to_all | solution.py:15
  111.1 0.4 fusion.11
  111.5 5.3 %all-gather.2 = f32[32,256]{1,0:T(8,128)S(1)} all-gather(f32[16,256]{1,0:T(8,128)S(1)} %fusion.11), channel_id=4, replica_groups=mesh['row'=16,'z'=16,'c'=2] {'c'}, dimensions={0}, use_global_device_ids=true | all-gather | bytes 49152 | tf_op jit(solution)/shard_map/all_gather | solution.py:55
  116.9 11.7 %all_to_all.51 = f32[16,16,256]{2,1,0:T(8,128)S(1)} all-to-all(f32[16,16,256]{2,1,0:T(8,128)S(1)} %broadcast_in_dim.17), channel_id=1, replica_groups=mesh['row'=16,'z'=16,'c'=2] {'row'}, dimensions={0} | all-to-all | bytes 524288 | tf_op jit(solution)/shard_map/all_to_all | solution.py:15
  128.5 0.7 multiply_reduce_fusion.4
  129.2 2.1 %select_maximum_fusion.2 = f32[128]{0:T(128)S(1)} fusion(f32[1]{0:T(128)} %bitcast.9, f32[1]{0:T(128)} %bitcast.8, f32[1]{0:T(128)} %bitcast.4), kind=kLoop, calls=%fused_computation.42 | loop fusion | flops 768 | bytes 524 | tf_op jit(solution)/shard_map/stack | solution.py:80
  131.3 0.6 broadcast_in_dim.18
  131.9 3.5 %all-to-all-start.6 = ((f32[16,1,128]{2,1,0:T(1,128)}), f32[16,1,128]{2,1,0:T(1,128)S(1)}, u32[]{:S(2)}, u32[]{:S(2)}) async-start(f32[16,1,128]{2,1,0:T(1,128)} %broadcast_in_dim.18), calls=%async_computation.6 | async-start | bytes 16384 | tf_op jit(solution)/shard_map/all_to_all | solution.py:15
  135.4 0.6 convolution_convert_fusion.1
  136.0 0.7 copy.35
  136.7 9.8 %all-to-all-done.6 = f32[16,1,128]{2,1,0:T(1,128)S(1)} async-done(((f32[16,1,128]{2,1,0:T(1,128)}), f32[16,1,128]{2,1,0:T(1,128)S(1)}, u32[]{:S(2)}, u32[]{:S(2)}) %all-to-all-start.6) | async-done | bytes 8224 | tf_op jit(solution)/shard_map/all_to_all | solution.py:15
  146.5 3.5 %all-to-all-start.7 = ((bf16[16,16,256]{2,1,0:T(8,128)(2,1)}), bf16[16,16,256]{2,1,0:T(8,128)(2,1)S(1)}, u32[]{:S(2)}, u32[]{:S(2)}) async-start(bf16[16,16,256]{2,1,0:T(8,128)(2,1)} %bitcast.45), calls=%async_computation.7 | async-start | bytes 262144 | tf_op jit(solution)/shard_map/all_to_all | solution.py:15
  150.0 0.7 fusion.9
  153.4 0.6 multiply_reduce_fusion.1
  154.1 7.9 %all-to-all-done.7 = bf16[16,16,256]{2,1,0:T(8,128)(2,1)S(1)} async-done(((bf16[16,16,256]{2,1,0:T(8,128)(2,1)}), bf16[16,16,256]{2,1,0:T(8,128)(2,1)S(1)}, u32[]{:S(2)}, u32[]{:S(2)}) %all-to-all-start.7) | async-done | bytes 131104 | tf_op jit(solution)/shard_map/all_to_all | solution.py:15
  162.0 0.7 fusion
  162.7 2.1 %select_maximum_fusion = f32[128]{0:T(128)S(1)} fusion(f32[1]{0:T(128)} %bitcast.17, f32[1]{0:T(128)} %bitcast.15, f32[1]{0:T(128)} %bitcast.13), kind=kLoop, calls=%fused_computation.40 | loop fusion | flops 768 | bytes 524 | tf_op jit(solution)/shard_map/stack | solution.py:91
  164.8 15.1 %all_to_all.52 = f32[16,1,128]{2,1,0:T(1,128)S(1)} all-to-all(f32[16,1,128]{2,1,0:T(1,128)S(1)} %broadcast_in_dim.19), channel_id=1, replica_groups=mesh['row'=16,'z'=16,'c'=2] {'z'}, dimensions={0} | all-to-all | bytes 16384 | tf_op jit(solution)/shard_map/all_to_all | solution.py:15
  179.9 0.6 broadcast_in_dim.20
  180.5 9.0 %all-to-all-start.9 = ((f32[32,1,128]{2,1,0:T(1,128)}), f32[32,1,128]{2,1,0:T(1,128)S(1)}, u32[]{:S(2)}, u32[]{:S(2)}) async-start(f32[32,1,128]{2,1,0:T(1,128)} %broadcast_in_dim.20), calls=%async_computation.9 | async-start | bytes 32768 | tf_op jit(solution)/shard_map/all_to_all | solution.py:15
  189.5 6.9 %all-to-all-done.9 = f32[32,1,128]{2,1,0:T(1,128)S(1)} async-done(((f32[32,1,128]{2,1,0:T(1,128)}), f32[32,1,128]{2,1,0:T(1,128)S(1)}, u32[]{:S(2)}, u32[]{:S(2)}) %all-to-all-start.9) | async-done | bytes 16416 | tf_op jit(solution)/shard_map/all_to_all | solution.py:15
  196.5 0.7 fusion.8
  199.2 0.6 fusion.1
  (24 shorter events, 0.4 us)
Async XLA Ops:
  0.6 21.4 %copy-start = (bf16[8192,128]{1,0:T(8,128)(2,1)S(1)}, bf16[8192,128]{1,0:T(8,128)(2,1)}, u32[]{:S(2)}) copy-start(bf16[8192,128]{1,0:T(8,128)(2,1)} %param.4) | copy-start | bytes 6291460
  12.5 21.7 %all-to-all-start = ((bf16[16,16,256]{2,1,0:T(8,128)(2,1)}), bf16[16,16,256]{2,1,0:T(8,128)(2,1)S(1)}, u32[]{:S(2)}, u32[]{:S(2)}) async-start(bf16[16,16,256]{2,1,0:T(8,128)(2,1)} %copy.20), calls=%async_computation | async-start | bytes 262144 | tf_op jit(solution)/shard_map/all_to_all | solution.py:15
  23.2 30.2 %collective-permute-start = (bf16[4096,128]{1,0:T(8,128)(2,1)}, bf16[4096,128]{1,0:T(8,128)(2,1)S(1)}, u32[]{:S(2)}, u32[]{:S(2)}) collective-permute-start(bf16[4096,128]{1,0:T(8,128)(2,1)} %get-tuple-element.10), channel_id=1, source_target_pairs={{0,1},{1,0},{2,3},{3,2},{4,5},{5,4},{6,7},{7,6},{8,9},{9,8},{10,11... | collective-permute-start | bytes 3145736 | tf_op jit(solution)/shard_map/ppermute | solution.py:38
  34.9 18.5 %all-to-all-start.1 = ((bf16[16,16,256]{2,1,0:T(8,128)(2,1)}), bf16[16,16,256]{2,1,0:T(8,128)(2,1)S(1)}, u32[]{:S(2)}, u32[]{:S(2)}) async-start(bf16[16,16,256]{2,1,0:T(8,128)(2,1)} %broadcast_in_dim.14), calls=%async_computation.1 | async-start | bytes 262144 | tf_op jit(solution)/shard_map/all_to_all | solution.py:15
  53.4 1.0 copy-start.1
  56.5 13.2 %copy-start.2 = (f32[16,128]{1,0:T(8,128)S(1)}, f32[16,128]{1,0:T(8,128)}, u32[]{:S(2)}) copy-start(f32[16,128]{1,0:T(8,128)} %param.6) | copy-start | bytes 24580
  56.9 25.3 %copy-start.3 = (s32[4096]{0:T(1024)S(1)}, s32[4096]{0:T(1024)}, u32[]{:S(2)}) copy-start(s32[4096]{0:T(1024)} %param.7) | copy-start | bytes 49156
  63.0 14.3 %all-to-all-start.2 = ((f32[16,16,256]{2,1,0:T(8,128)}), f32[16,16,256]{2,1,0:T(8,128)S(1)}, u32[]{:S(2)}, u32[]{:S(2)}) async-start(f32[16,16,256]{2,1,0:T(8,128)} %broadcast_in_dim.15), calls=%async_computation.2 | async-start | bytes 524288 | tf_op jit(solution)/shard_map/all_to_all | solution.py:15
  78.7 15.5 %all-to-all-start.3 = ((bf16[16,16,256]{2,1,0:T(8,128)(2,1)}), bf16[16,16,256]{2,1,0:T(8,128)(2,1)S(1)}, u32[]{:S(2)}, u32[]{:S(2)}) async-start(bf16[16,16,256]{2,1,0:T(8,128)(2,1)} %bitcast.47), calls=%async_computation.3 | async-start | bytes 262144 | tf_op jit(solution)/shard_map/all_to_all | solution.py:15
  131.9 14.6 %all-to-all-start.6 = ((f32[16,1,128]{2,1,0:T(1,128)}), f32[16,1,128]{2,1,0:T(1,128)S(1)}, u32[]{:S(2)}, u32[]{:S(2)}) async-start(f32[16,1,128]{2,1,0:T(1,128)} %broadcast_in_dim.18), calls=%async_computation.6 | async-start | bytes 16384 | tf_op jit(solution)/shard_map/all_to_all | solution.py:15
  146.5 15.4 %all-to-all-start.7 = ((bf16[16,16,256]{2,1,0:T(8,128)(2,1)}), bf16[16,16,256]{2,1,0:T(8,128)(2,1)S(1)}, u32[]{:S(2)}, u32[]{:S(2)}) async-start(bf16[16,16,256]{2,1,0:T(8,128)(2,1)} %bitcast.45), calls=%async_computation.7 | async-start | bytes 262144 | tf_op jit(solution)/shard_map/all_to_all | solution.py:15
  180.5 15.9 %all-to-all-start.9 = ((f32[32,1,128]{2,1,0:T(1,128)}), f32[32,1,128]{2,1,0:T(1,128)S(1)}, u32[]{:S(2)}, u32[]{:S(2)}) async-start(f32[32,1,128]{2,1,0:T(1,128)} %broadcast_in_dim.20), calls=%async_computation.9 | async-start | bytes 32768 | tf_op jit(solution)/shard_map/all_to_all | solution.py:15

commit v2 on v1

v2 whole, which is shorter than its diff:
```python
import functools

import jax
import jax.numpy as jnp
from jax import lax
from jax.experimental import pallas as pl
from jax.experimental.pallas import tpu as pltpu
from jax.sharding import Mesh, PartitionSpec as P

RIDGE_WEIGHT = 0.004
F32, BF16 = jnp.float32, jnp.bfloat16
LANES = 128
PIECES = 3
CORES = 2


def kernel_call(body, out_shape, *operands):
    return pl.pallas_call(
        body,
        out_shape=out_shape,
        in_specs=[pl.BlockSpec(memory_space=pltpu.VMEM)] * len(operands),
        out_specs=jax.tree.map(lambda _: pl.BlockSpec(memory_space=pltpu.VMEM), out_shape),
        compiler_params=pltpu.CompilerParams(vmem_limit_bytes=24 * 1024 * 1024),
    )(*operands)


def times_transposed(left, right):
    return lax.dot_general(left, right, (((1,), (1,)), ((), ())), preferred_element_type=F32)


def arrived(ref):
    total = ref[0].astype(F32)
    for sender in range(1, ref.shape[0]):
        total = total + ref[sender].astype(F32)
    return total


def repeat(ref, block):
    for receiver in range(ref.shape[0]):
        ref[receiver] = block


def shares_sum(shares, block):
    return jnp.sum(shares * block, axis=0, keepdims=True)


def whole(block):
    return jnp.sum(jnp.sum(block, axis=1, keepdims=True), axis=0, keepdims=True)


def logits_kernel(weights, rows, mine, other):
    core = lax.axis_index("c")
    depth = mine.shape[0]
    rounded = weights[...].astype(BF16)
    for level in range(depth):
        mine[level] = times_transposed(rounded, rows[core * depth + level])
        other[level] = times_transposed(rounded, rows[(1 - core) * depth + level])


def add_kernel(mine, other, both):
    both[...] = mine[...] + other[...]


def misfit_kernel(came, labels, shares, sent):
    depth = came.shape[0]
    place = lax.axis_index("c") * depth + lax.axis_index("z")
    exponent = jnp.exp(arrived(came))
    share = exponent / jnp.sum(exponent, axis=0, keepdims=True)
    shares[...] = share
    indicator = labels[pl.ds(place, 1), :] == lax.broadcasted_iota(jnp.int32, share.shape, 0)
    repeat(sent, (share - indicator.astype(F32)).astype(BF16))


def columns_kernel(came, rows, others, part):
    core = lax.axis_index("c")
    depth, width = came.shape[0], rows.shape[2]
    own = jnp.zeros((part.shape[0], width), F32)
    far = jnp.zeros((part.shape[0], width), F32)
    for level in range(depth):
        own = own + jnp.dot(came[level], rows[core * depth + level], preferred_element_type=F32)
        far = far + jnp.dot(came[level], others[level], preferred_element_type=F32)
    part[:, :width] = own
    part[:, width:] = far


def pair_kernel(parts, sent):
    core = lax.axis_index("c")
    mine, far = parts[core], parts[1 - core]
    width = mine.shape[1] // CORES
    repeat(sent, mine + jnp.concatenate([far[:, width:], far[:, :width]], axis=1))


def respond(vector, rows, others, sent):
    core = lax.axis_index("c")
    depth, width = others.shape[0], rows.shape[2]
    own, far = vector[:, :width].astype(BF16), vector[:, width:].astype(BF16)
    for level in range(depth):
        value = times_transposed(own, rows[core * depth + level]) + times_transposed(far, others[level])
        sent[level, :, : value.shape[1]] = value.astype(BF16)


def gradient_kernel(users, came, weights, far_weights, rows, others, gradient, residual, sent):
    width = weights.shape[1]
    value = arrived(came) / users + RIDGE_WEIGHT * jnp.concatenate([weights[...], far_weights[...]], axis=1)
    gradient[...] = value[:, :width]
    residual[...] = -value
    respond(-value, rows, others, sent)


def weigh_kernel(came, shares, count, response, sent):
    value = arrived(came)
    response[...] = value
    share = shares[...]
    repeat(sent, (count[...] * (share * (value - shares_sum(share, value)))).astype(BF16))


def image_kernel(sub_total, came, residual, rows, others, image, sent):
    start = residual[...]
    value = arrived(came) / sub_total + RIDGE_WEIGHT * start
    image[...] = value
    respond(value, rows, others, sent)
    place = lax.broadcasted_iota(jnp.int32, (start.shape[0], LANES), 0)
    tile = jnp.zeros(place.shape, F32)
    for which, product in enumerate((start * start, start * value, value * value)):
        left = whole(product)
        for piece in range(PIECES):
            head = left.astype(BF16).astype(F32)
            tile = jnp.where(place == which * PIECES + piece, head, tile)
            left = left - head
    tile = tile.astype(BF16)
    for level in range(sent.shape[0]):
        sent[level, :, value.shape[1] :] = tile


def direction_kernel(came, response, shares, count, residual, image, base, direction, sent):
    got = arrived(came)
    width = base.shape[1]
    image_response, tile = got[:, : count.shape[1]], got[:, count.shape[1] :]

    def scalar(which):
        return sum(tile[which * PIECES + piece : which * PIECES + piece + 1, :1] for piece in range(PIECES))

    norm, curve, image_norm = scalar(0), scalar(1), scalar(2)
    step = norm / curve
    beta = jnp.maximum(image_norm / curve * step - 1.0, 0.0)
    start = residual[...]
    after = start - step * image[...]
    second = after + beta * start
    base[...] = step * start[:, :width]
    direction[...] = second[:, :width]
    share = shares[...]
    value = (1.0 + beta) * response[...] - step * image_response
    centred = value - shares_sum(share, value)
    lane = lax.broadcasted_iota(jnp.int32, (1, LANES), 1)
    line = jnp.where(lane == 0, whole(after * after), whole(second * second))
    line = jnp.where(lane < 2, line, whole(count[...] * (share * (centred * centred))))
    repeat(sent, line)


def relay_kernel(came, sent):
    repeat(sent, arrived(came))


def step_kernel(sub_total, copies, came, base, direction, newton_step):
    line = arrived(came)
    norm, square, spread = line[:, 0:1] / copies, line[:, 1:2] / copies, line[:, 2:3]
    curve = spread / sub_total + RIDGE_WEIGHT * square
    newton_step[...] = base[...] + norm / curve * direction[...]


def swap(block, axis):
    return lax.all_to_all(block, axis, 0, 0, tiled=True)


def array(*shape, dtype=F32):
    return jax.ShapeDtypeStruct(shape, dtype)


def body(covariates, labels, weights, sample_index):
    user_rows, width = covariates.shape
    classes = weights.shape[0]
    row_count, depth = lax.axis_size("row"), lax.axis_size("z")
    row, level, core = lax.axis_index("row"), lax.axis_index("z"), lax.axis_index("c")
    users = user_rows * row_count
    sub_total = sample_index.shape[0] * row_count
    half = user_rows // CORES
    own = half // depth
    wide = CORES * width
    pair = [(0, 1), (1, 0)]
    rows = covariates.reshape(CORES * depth, own, width)
    labels = labels.reshape(CORES * depth, own)
    blocks = (depth, classes, own)

    mine, other = kernel_call(logits_kernel, (array(*blocks), array(*blocks)), weights, rows)
    logits = kernel_call(add_kernel, array(*blocks), mine, lax.ppermute(other, "c", pair))
    logits, covariates, weights, sample_index = lax.optimization_barrier(
        (logits, covariates, weights, sample_index)
    )
    came = swap(logits, "z")
    others = lax.dynamic_slice_in_dim(covariates, (1 - core) * half, half, 0)
    others = lax.ppermute(others, "c", pair).reshape(depth, own, width)
    far_weights = lax.ppermute(weights, "c", pair)
    position = row * user_rows + core * half + level * own + jnp.arange(own, dtype=jnp.int32)
    count = jnp.sum((sample_index[:, None] == position[None, :]).astype(F32), axis=0)[None]
    came, others, far_weights, count = lax.optimization_barrier((came, others, far_weights, count))

    shares, sent = kernel_call(misfit_kernel, (array(classes, own), array(*blocks, dtype=BF16)), came, labels)

    def back_to_columns(sent):
        part = kernel_call(columns_kernel, array(classes, wide), swap(sent, "z"), rows, others)
        parts = lax.all_gather(part, "c", axis=0)
        return swap(kernel_call(pair_kernel, array(row_count, classes, wide), parts), "row")

    gradient, residual, sent = kernel_call(
        functools.partial(gradient_kernel, users),
        (array(classes, width), array(classes, wide), array(*blocks, dtype=BF16)),
        back_to_columns(sent), weights, far_weights, rows, others,
    )
    response, sent = kernel_call(
        weigh_kernel, (array(classes, own), array(*blocks, dtype=BF16)), swap(sent, "z"), shares, count
    )
    image, sent = kernel_call(
        functools.partial(image_kernel, sub_total),
        (array(classes, wide), array(depth, classes, own + LANES, dtype=BF16)),
        back_to_columns(sent), residual, rows, others,
    )
    base, direction, sent = kernel_call(
        direction_kernel,
        (array(classes, width), array(classes, width), array(depth, 1, LANES)),
        swap(sent, "z"), response, shares, count, residual, image,
    )
    sent = kernel_call(relay_kernel, array(row_count * CORES, 1, LANES), swap(sent, "z"))
    newton_step = kernel_call(
        functools.partial(step_kernel, sub_total, row_count * CORES),
        array(classes, width),
        swap(sent, ("row", "c")), base, direction,
    )
    return gradient, newton_step


def solution(mesh):
    rows, cols = mesh.devices.shape
    fine = Mesh(mesh.devices.reshape(rows, cols // CORES, CORES), ("row", "z", "c"))
    in_specs = (P("row", ("z", "c")), P("row"), P(None, ("z", "c")), P("row"))
    out_specs = (P(None, ("z", "c")), P(None, ("z", "c")))
    return jax.shard_map(body, mesh=fine, in_specs=in_specs, out_specs=out_specs, check_vma=False)
```

time: 201 us -> 184 us (0.915)
  blocking collectives: 65.1 us -> 139 us
  waiting for transfers between devices: 59.8 us -> 11 us
  starting transfers between devices: 44.8 us -> 23.1 us
  other arithmetic: 11.1 us -> 1.88 us
  local copies, waits for them, and re-layouts: 8.92 us -> 3.37 us
  between operations: 5.65 us -> 0.78 us
  Pallas kernels: 0 us -> 4.85 us
  matrix products: 4.45 us -> 0 us
    all_to_all x3 -> x8, blocking collectives: 43.6 us -> 128 us  [swap(): return lax.all_to_all(block, axis, 0, 0, tiled=True)]
    all_to_all x7 -> x1, waiting for transfers between devices: 59.8 us -> 9.91 us  [swap(): return lax.all_to_all(block, axis, 0, 0, tiled=True)]
    all_to_all x7 -> x1, starting transfers between devices: 42.2 us -> 9.55 us  [swap(): return lax.all_to_all(block, axis, 0, 0, tiled=True)]
    ppermute x1 -> x3, starting transfers between devices: 2.55 us -> 13.5 us  [the longest x1 8.92 us: body(): lax.ppermute(other, 'c', pair)]
    all_gather x4 -> x2, blocking collectives: 21.4 us -> 10.5 us  [back_to_columns(): parts = lax.all_gather(part, 'c', axis=0)]
    pallas_call x0 -> x13, Pallas kernels: none -> 4.85 us  [kernel_call(): pl.pallas_call(body, out_shape=out_shape, in_specs=[pl.BlockSpec(memory_s...]
    dot_general x5 -> x0, matrix products: 4.45 us -> none  [the longest x1 2.4 us: body(): lax.dot_general(weights.astype(jnp.bfloat16), covariates, (((1,), (1,)),...]
    another operation x2 -> x0, other arithmetic: 4.11 us -> none  [the longest x1 2.06 us: body(): jnp.stack([jnp.sum(residual_1 * residual_1), jnp.sum(direction_1 * direct...]
  transfers between devices with their start and end apart: 8 -> 4, of which waited for: 7 -> 2; matrix products, arithmetic and copies ran while one was open for 4% -> 1% of each run, Pallas kernels for 0% -> 0%
where the time goes in v2:
time: 184 us; the launch traced here: 183 us
  blocking collectives  139 us (76%)
  starting transfers between devices  23.1 us (13%)
  waiting for transfers between devices  11 us (6%)
  Pallas kernels  4.85 us (3%)
  local copies, waits for them, and re-layouts  3.37 us (2%)
  other arithmetic  1.88 us (1%)
    all_to_all x8, blocking collectives, swap(): return lax.all_to_all(block, axis, 0, 0, tiled=True)  128 us
    all_gather x2, blocking collectives, back_to_columns(): parts = lax.all_gather(part, 'c', axis=0)  10.5 us
    all_to_all x1, waiting for transfers between devices, swap(): return lax.all_to_all(block, axis, 0, 0, tiled=True)  9.91 us
    all_to_all x1, starting transfers between devices, swap(): return lax.all_to_all(block, axis, 0, 0, tiled=True)  9.55 us
    ppermute x1, starting transfers between devices, body(): lax.ppermute(other, 'c', pair)  8.92 us
    pallas_call x13, Pallas kernels, kernel_call(): pl.pallas_call(body, out_shape=out_shape, in_specs=[pl.BlockSpec(memory_s...  4.85 us
  transfers between devices with their start and end apart: 4, of which 2 were waited for; matrix products, arithmetic and copies ran while one was open for 1% of the time, Pallas kernels for 0%

profile of v2, /device:TPU:1, one launch (start us, length us, event | category | flops | bytes accessed | tf_op | source)
XLA Modules:
  0.0 183.5 jit_solution(5912533639384337994)
XLA Ops:
  0.6 0.0 copy-start
  0.6 1.6 copy-done
  2.2 0.0 copy-start.2
  2.2 0.7 copy-done.2
  2.9 0.0 copy-start.1
  2.9 0.6 shard_map.59
  3.6 0.0 copy-start.4
  3.6 0.0 copy-start.3
  3.6 0.0 copy-start.5
  3.6 8.9 %collective-permute-start = (f32[16,16,256]{2,1,0:T(8,128)S(1)}, f32[16,16,256]{2,1,0:T(8,128)S(1)}, u32[]{:S(2)}, u32[]{:S(2)}) collective-permute-start(f32[16,16,256]{2,1,0:T(8,128)S(1)} %get-tuple-element.25), channel_id=1, source_target_pairs={{0,1},{1,0},{2,3},{3,2},{4,5},{5,4},{6,7},{7,6},{8,9},{9,8},{10,11... | collective-permute-start | bytes 786440 | tf_op jit(solution)/shard_map/ppermute | solution.py:195
  12.5 1.1 collective-permute-done.other
  13.7 0.7 shard_map.60
  14.4 0.0 copy-done.1
  14.4 1.1 constant_dynamic-slice_fusion
  15.5 2.3 %collective-permute-start.1 = (bf16[4096,128]{1,0:T(8,128)(2,1)}, bf16[4096,128]{1,0:T(8,128)(2,1)S(1)}, u32[]{:S(2)}, u32[]{:S(2)}) collective-permute-start(bf16[4096,128]{1,0:T(8,128)(2,1)} %constant_dynamic-slice_fusion), channel_id=1, source_target_pairs={{0,1},{1,0},{2,3},{3,2},{4,5},{5,4},{6,7},{7,6},{8,9},{9,8},{10,11... | collective-permute-start | bytes 3145736 | tf_op jit(solution)/shard_map/ppermute | solution.py:201
  17.7 9.6 %all-to-all-start = ((f32[16,16,256]{2,1,0:T(8,128)}), f32[16,16,256]{2,1,0:T(8,128)S(1)}, u32[]{:S(2)}, u32[]{:S(2)}) async-start(f32[16,16,256]{2,1,0:T(8,128)} %shard_map.60), calls=%async_computation | async-start | bytes 524288 | tf_op jit(solution)/shard_map/all_to_all | solution.py:172
  27.3 0.0 copy-done.4
  27.4 0.0 copy-done.3
  27.4 2.3 %collective-permute-start.2 = (f32[16,128]{1,0:T(8,128)S(1)}, f32[16,128]{1,0:T(8,128)S(1)}, u32[]{:S(2)}, u32[]{:S(2)}) collective-permute-start(f32[16,128]{1,0:T(8,128)S(1)} %copy-done.3), channel_id=1, source_target_pairs={{0,1},{1,0},{2,3},{3,2},{4,5},{5,4},{6,7},{7,6},{8,9},{9,8},{10,11... | collective-permute-start | bytes 24584 | tf_op jit(solution)/shard_map/ppermute | solution.py:202
  29.7 0.0 copy-done.5
  29.7 1.9 %convert_reduce_fusion = f32[256]{0:T(256)S(1)} fusion(s32[256]{0:T(256)S(1)} %iota_add_fusion, s32[4096]{0:T(1024)S(1)} %copy-done.5), kind=kLoop, calls=%fused_computation | loop fusion | flops 3145472 | bytes 18432 | tf_op jit(solution)/shard_map/reduce_sum | solution.py:204
  31.6 0.0 collective-permute-done.2.far_weights
  31.6 9.9 %all-to-all-done.came = f32[16,16,256]{2,1,0:T(8,128)S(1)} async-done(((f32[16,16,256]{2,1,0:T(8,128)}), f32[16,16,256]{2,1,0:T(8,128)S(1)}, u32[]{:S(2)}, u32[]{:S(2)}) %all-to-all-start) | async-done | bytes 262176 | tf_op jit(solution)/shard_map/all_to_all | solution.py:172
  41.5 0.0 collective-permute-done.1
  41.6 21.8 %all_to_all.45.came = bf16[16,16,256]{2,1,0:T(8,128)(2,1)S(1)} all-to-all(bf16[16,16,256]{2,1,0:T(8,128)(2,1)S(1)} %get-tuple-element.31), channel_id=1, replica_groups=mesh['row'=16,'z'=16,'c'=2] {'z'}, dimensions={0} | all-to-all | bytes 262144 | tf_op jit(solution)/shard_map/all_to_all | solution.py:172
  63.4 0.4 shard_map.62
  63.8 5.2 %all-gather = f32[32,256]{1,0:T(8,128)S(1)} all-gather(f32[16,256]{1,0:T(8,128)S(1)} %shard_map.62), channel_id=2, replica_groups=mesh['row'=16,'z'=16,'c'=2] {'c'}, dimensions={0}, use_global_device_ids=true | all-gather | bytes 49152 | tf_op jit(solution)/shard_map/all_gather | solution.py:211
  69.0 14.1 %all_to_all.46.came = f32[16,16,256]{2,1,0:T(8,128)S(1)} all-to-all(f32[16,16,256]{2,1,0:T(8,128)S(1)} %shard_map.63), channel_id=1, replica_groups=mesh['row'=16,'z'=16,'c'=2] {'row'}, dimensions={0} | all-to-all | bytes 524288 | tf_op jit(solution)/shard_map/all_to_all | solution.py:172
  83.2 0.9 shard_map.64
  84.0 15.3 %all_to_all.47.came = bf16[16,16,256]{2,1,0:T(8,128)(2,1)S(1)} all-to-all(bf16[16,16,256]{2,1,0:T(8,128)(2,1)S(1)} %get-tuple-element.35), channel_id=1, replica_groups=mesh['row'=16,'z'=16,'c'=2] {'z'}, dimensions={0} | all-to-all | bytes 262144 | tf_op jit(solution)/shard_map/all_to_all | solution.py:172
  99.3 16.9 %all_to_all.48.came = bf16[16,16,256]{2,1,0:T(8,128)(2,1)S(1)} all-to-all(bf16[16,16,256]{2,1,0:T(8,128)(2,1)S(1)} %get-tuple-element.38), channel_id=1, replica_groups=mesh['row'=16,'z'=16,'c'=2] {'z'}, dimensions={0} | all-to-all | bytes 262144 | tf_op jit(solution)/shard_map/all_to_all | solution.py:172
  116.2 0.4 shard_map.66
  116.6 5.3 %all-gather.1 = f32[32,256]{1,0:T(8,128)S(1)} all-gather(f32[16,256]{1,0:T(8,128)S(1)} %shard_map.66), channel_id=3, replica_groups=mesh['row'=16,'z'=16,'c'=2] {'c'}, dimensions={0}, use_global_device_ids=true | all-gather | bytes 49152 | tf_op jit(solution)/shard_map/all_gather | solution.py:211
  121.9 11.7 %all_to_all.49.came = f32[16,16,256]{2,1,0:T(8,128)S(1)} all-to-all(f32[16,16,256]{2,1,0:T(8,128)S(1)} %shard_map.67), channel_id=1, replica_groups=mesh['row'=16,'z'=16,'c'=2] {'row'}, dimensions={0} | all-to-all | bytes 524288 | tf_op jit(solution)/shard_map/all_to_all | solution.py:172
  133.6 0.7 shard_map.68
  134.2 15.2 %all_to_all.50.came = bf16[16,16,384]{2,1,0:T(8,128)(2,1)S(1)} all-to-all(bf16[16,16,384]{2,1,0:T(8,128)(2,1)S(1)} %get-tuple-element.40), channel_id=1, replica_groups=mesh['row'=16,'z'=16,'c'=2] {'z'}, dimensions={0} | all-to-all | bytes 393216 | tf_op jit(solution)/shard_map/all_to_all | solution.py:172
  149.4 0.2 shard_map.69
  149.6 18.4 %all_to_all.51.came = f32[16,1,128]{2,1,0:T(1,128)S(1)} all-to-all(f32[16,1,128]{2,1,0:T(1,128)S(1)} %get-tuple-element.43), channel_id=1, replica_groups=mesh['row'=16,'z'=16,'c'=2] {'z'}, dimensions={0} | all-to-all | bytes 16384 | tf_op jit(solution)/shard_map/all_to_all | solution.py:172
  168.0 14.6 %all_to_all.52.came = f32[32,1,128]{2,1,0:T(1,128)S(1)} all-to-all(f32[32,1,128]{2,1,0:T(1,128)S(1)} %shard_map.70), channel_id=1, replica_groups=mesh['row'=16,'z'=16,'c'=2] {'row','c'}, dimensions={0} | all-to-all | bytes 32768 | tf_op jit(solution)/shard_map/all_to_all | solution.py:172
  182.7 0.8 shard_map.71
  (7 shorter events, 0.2 us)
Async XLA Ops:
  0.6 1.6 copy-start
  2.2 0.7 copy-start.2
  2.9 11.5 %copy-start.1 = (bf16[8192,128]{1,0:T(8,128)(2,1)S(1)}, bf16[8192,128]{1,0:T(8,128)(2,1)}, u32[]{:S(2)}) copy-start(bf16[8192,128]{1,0:T(8,128)(2,1)} %param.4) | copy-start | bytes 6291460
  3.6 23.7 %copy-start.4 = (s32[8192]{0:T(1024)S(1)}, s32[8192]{0:T(1024)}, u32[]{:S(2)}) copy-start(s32[8192]{0:T(1024)} %param.5) | copy-start | bytes 98308
  3.6 23.8 %copy-start.3 = (f32[16,128]{1,0:T(8,128)S(1)}, f32[16,128]{1,0:T(8,128)}, u32[]{:S(2)}) copy-start(f32[16,128]{1,0:T(8,128)} %weights.2) | copy-start | bytes 24580
  3.6 26.1 %copy-start.5 = (s32[4096]{0:T(1024)S(1)}, s32[4096]{0:T(1024)}, u32[]{:S(2)}) copy-start(s32[4096]{0:T(1024)} %param.7) | copy-start | bytes 49156
  3.6 10.1 %collective-permute-start = (f32[16,16,256]{2,1,0:T(8,128)S(1)}, f32[16,16,256]{2,1,0:T(8,128)S(1)}, u32[]{:S(2)}, u32[]{:S(2)}) collective-permute-start(f32[16,16,256]{2,1,0:T(8,128)S(1)} %get-tuple-element.25), channel_id=1, source_target_pairs={{0,1},{1,0},{2,3},{3,2},{4,5},{5,4},{6,7},{7,6},{8,9},{9,8},{10,11... | collective-permute-start | bytes 786440 | tf_op jit(solution)/shard_map/ppermute | solution.py:195
  15.5 26.1 %collective-permute-start.1 = (bf16[4096,128]{1,0:T(8,128)(2,1)}, bf16[4096,128]{1,0:T(8,128)(2,1)S(1)}, u32[]{:S(2)}, u32[]{:S(2)}) collective-permute-start(bf16[4096,128]{1,0:T(8,128)(2,1)} %constant_dynamic-slice_fusion), channel_id=1, source_target_pairs={{0,1},{1,0},{2,3},{3,2},{4,5},{5,4},{6,7},{7,6},{8,9},{9,8},{10,11... | collective-permute-start | bytes 3145736 | tf_op jit(solution)/shard_map/ppermute | solution.py:201
  17.7 23.8 %all-to-all-start = ((f32[16,16,256]{2,1,0:T(8,128)}), f32[16,16,256]{2,1,0:T(8,128)S(1)}, u32[]{:S(2)}, u32[]{:S(2)}) async-start(f32[16,16,256]{2,1,0:T(8,128)} %shard_map.60), calls=%async_computation | async-start | bytes 524288 | tf_op jit(solution)/shard_map/all_to_all | solution.py:172
  27.4 4.2 %collective-permute-start.2 = (f32[16,128]{1,0:T(8,128)S(1)}, f32[16,128]{1,0:T(8,128)S(1)}, u32[]{:S(2)}, u32[]{:S(2)}) collective-permute-start(f32[16,128]{1,0:T(8,128)S(1)} %copy-done.3), channel_id=1, source_target_pairs={{0,1},{1,0},{2,3},{3,2},{4,5},{5,4},{6,7},{7,6},{8,9},{9,8},{10,11... | collective-permute-start | bytes 24584 | tf_op jit(solution)/shard_map/ppermute | solution.py:202

commit v3 on v2

v3 whole, which is shorter than its diff:
```python
import functools

import jax
import jax.numpy as jnp
from jax import lax
from jax.experimental import pallas as pl
from jax.experimental.pallas import tpu as pltpu
from jax.sharding import Mesh, PartitionSpec as P

RIDGE_WEIGHT = 0.004
F32, BF16 = jnp.float32, jnp.bfloat16
LANES, SUBLANES = 128, 8
PIECES = 3
CORES = 2
GROUPS = 4
TOP, REACH = 32767.0, 768.0


def kernel_call(body, out_shape, *operands):
    return pl.pallas_call(
        body,
        out_shape=out_shape,
        in_specs=[pl.BlockSpec(memory_space=pltpu.VMEM)] * len(operands),
        out_specs=jax.tree.map(lambda _: pl.BlockSpec(memory_space=pltpu.VMEM), out_shape),
        compiler_params=pltpu.CompilerParams(vmem_limit_bytes=24 * 1024 * 1024),
    )(*operands)


def times_transposed(left, right):
    return lax.dot_general(left, right, (((1,), (1,)), ((), ())), preferred_element_type=F32)


def arrived(ref):
    total = ref[0].astype(F32)
    for sender in range(1, ref.shape[0]):
        total = total + ref[sender].astype(F32)
    return total


def repeat(ref, block):
    for receiver in range(ref.shape[0]):
        ref[receiver] = block


def shares_sum(shares, block):
    return jnp.sum(shares * block, axis=0, keepdims=True)


def whole(block):
    return jnp.sum(jnp.sum(block, axis=1, keepdims=True), axis=0, keepdims=True)


def send_other_kernel(weights_hbm, rows_hbm, other, weights, rows, weights_sem, row_sems):
    depth = other.shape[0]
    first = (1 - lax.axis_index("c")) * depth
    head = pltpu.make_async_copy(weights_hbm, weights, weights_sem)
    head.start()
    step = depth // GROUPS
    copies = []
    for group in range(GROUPS):
        here = pl.ds(group * step, step)
        copies.append(
            pltpu.make_async_copy(rows_hbm.at[pl.ds(first + group * step, step)], rows.at[here], row_sems.at[group])
        )
        copies[-1].start()
    head.wait()
    rounded = weights[...].astype(BF16)
    for group in range(GROUPS):
        copies[group].wait()
        for level in range(group * step, (group + 1) * step):
            other[level] = times_transposed(rounded, rows[level])


def keep_kernel(user_rows, weights, rows, index, mine, count):
    depth, _, own = mine.shape
    core = lax.axis_index("c")
    place = core * depth + lax.axis_index("z")
    rounded = weights[...].astype(BF16)
    for level in range(depth):
        mine[level] = times_transposed(rounded, rows[core * depth + level])
    offset = index[...] - (lax.axis_index("row") * user_rows + place * own)
    low, high = offset & (LANES - 1), offset >> 7
    low_place = lax.broadcasted_iota(jnp.int32, (LANES, LANES), 0)
    high_place = lax.broadcasted_iota(jnp.int32, (SUBLANES, LANES), 0)
    drawn = jnp.zeros((SUBLANES, LANES), F32)
    for line in range(index.shape[0]):
        is_low = (low[line : line + 1] == low_place).astype(F32).astype(BF16)
        is_high = (high[line : line + 1] == high_place).astype(F32).astype(BF16)
        drawn = drawn + times_transposed(is_high, is_low)
    for part in range(own // LANES):
        count[:, part * LANES : (part + 1) * LANES] = drawn[part : part + 1]


def code_kernel(mine, other, sent):
    for level in range(mine.shape[0]):
        value = mine[level] + other[level]
        value = value - value[-1:]
        largest = jnp.max(jnp.abs(value), axis=0, keepdims=True)
        scale = jnp.minimum(jnp.floor(largest * (TOP / REACH)) + 1.0, TOP)
        code = jnp.floor(value * (TOP * TOP / REACH / scale) + 0.5)
        code = jnp.clip(code, -TOP, TOP)
        last = lax.broadcasted_iota(jnp.int32, value.shape, 0) == value.shape[0] - 1
        sent[level] = jnp.where(last, scale, code).astype(jnp.int32).astype(jnp.int16)


def misfit_kernel(came, labels, shares, sent):
    depth, classes, own = came.shape
    logits = jnp.zeros((classes, own), F32)
    for sender in range(depth):
        code = came[sender].astype(jnp.int32).astype(F32)
        logits = logits + code * (code[-1:] * (REACH / TOP / TOP))
    kind = lax.broadcasted_iota(jnp.int32, logits.shape, 0)
    logits = jnp.where(kind == classes - 1, 0.0, logits)
    exponent = jnp.exp(logits - jnp.max(logits, axis=0, keepdims=True))
    share = exponent / jnp.sum(exponent, axis=0, keepdims=True)
    shares[...] = share
    lines = own // LANES
    first = (lax.axis_index("c") * depth + lax.axis_index("z")) * lines
    label = jnp.concatenate([labels[pl.ds(first + line, 1), :] for line in range(lines)], axis=1)
    repeat(sent, (share - (label == kind).astype(F32)).astype(BF16))


def columns(came, rows):
    core = lax.axis_index("c")
    depth = came.shape[0]
    sums = []
    for owner in (core, 1 - core):
        first = (owner * CORES + core) * depth
        total = jnp.dot(came[0], rows[first], preferred_element_type=F32)
        for level in range(1, depth):
            total = total + jnp.dot(came[level], rows[first + level], preferred_element_type=F32)
        sums.append(total)
    return sums


def misfit_columns_kernel(ridge, came, rows, weights, part):
    own, far = columns(came, rows)
    width = own.shape[1]
    part[:, :width] = own + ridge * weights[...]
    part[:, width:] = far


def image_columns_kernel(came, rows, part):
    own, far = columns(came, rows)
    width = own.shape[1]
    part[:, :width] = own
    part[:, width:] = far


def pair_kernel(parts, sent):
    core = lax.axis_index("c")
    mine, far = parts[core], parts[1 - core]
    width = mine.shape[1] // CORES
    both = mine + jnp.concatenate([far[:, width:], far[:, :width]], axis=1)
    repeat(sent, both.astype(sent.dtype))


def respond(vector, rows, depth):
    core = lax.axis_index("c")
    width = rows.shape[2]
    own, far = vector[:, :width].astype(BF16), vector[:, width:].astype(BF16)
    for level in range(depth):
        near = times_transposed(own, rows[(core * CORES + core) * depth + level])
        yield near + times_transposed(far, rows[((1 - core) * CORES + core) * depth + level])


def gradient_kernel(users, came, rows, gradient, residual, sent):
    width = gradient.shape[1]
    value = arrived(came) / users
    gradient[...] = value[:, :width]
    residual[...] = -value
    for level, answer in enumerate(respond(-value, rows, sent.shape[0])):
        sent[level] = answer.astype(BF16)


def weigh_kernel(came, shares, count, response, sent):
    value = arrived(came)
    response[...] = value
    share = shares[...]
    repeat(sent, (count[...] * (share * (value - shares_sum(share, value)))).astype(BF16))


def image_kernel(sub_total, came, residual, rows, image, sent):
    start = residual[...]
    value = arrived(came) / sub_total + RIDGE_WEIGHT * start
    image[...] = value
    _, classes, own = sent.shape
    lane = lax.broadcasted_iota(jnp.int32, (1, own), 1)
    line = jnp.zeros(lane.shape, F32)
    for which, product in enumerate((start * start, start * value, value * value)):
        left = whole(product)
        for piece in range(PIECES):
            head = left.astype(BF16).astype(F32)
            line = jnp.where(lane == which * PIECES + piece, head, line)
            left = left - head
    last = lax.broadcasted_iota(jnp.int32, (classes, own), 0) == classes - 1
    for level, answer in enumerate(respond(value, rows, sent.shape[0])):
        sent[level] = jnp.where(last, line, answer - answer[-1:]).astype(BF16)


def direction_kernel(came, response, shares, count, residual, image, base, direction, sent):
    got = arrived(came)
    classes, own = got.shape
    width = base.shape[1]
    line = got[-1:]
    lane = lax.broadcasted_iota(jnp.int32, line.shape, 1)

    def scalar(which):
        pieces = jnp.logical_and(lane >= which * PIECES, lane < (which + 1) * PIECES)
        return jnp.sum(jnp.where(pieces, line, 0.0), axis=1, keepdims=True)

    norm, curve, image_norm = scalar(0), scalar(1), scalar(2)
    step = norm / curve
    beta = jnp.maximum(image_norm / curve * step - 1.0, 0.0)
    start = residual[...]
    after = start - step * image[...]
    second = after + beta * start
    base[...] = step * start[:, :width]
    direction[...] = second[:, :width]
    image_response = jnp.where(lax.broadcasted_iota(jnp.int32, got.shape, 0) == classes - 1, 0.0, got)
    share = shares[...]
    value = (1.0 + beta) * response[...] - step * image_response
    centred = value - shares_sum(share, value)
    lane = lax.broadcasted_iota(jnp.int32, (1, LANES), 1)
    line = jnp.where(lane == 0, whole(after * after), whole(second * second))
    line = jnp.where(lane < 2, line, whole(count[...] * (share * (centred * centred))))
    repeat(sent, line)


def relay_kernel(came, sent):
    repeat(sent, arrived(came))


def step_kernel(sub_total, copies, came, base, direction, newton_step):
    line = arrived(came)
    norm, square, spread = line[:, 0:1] / copies, line[:, 1:2] / copies, line[:, 2:3]
    curve = spread / sub_total + RIDGE_WEIGHT * square
    newton_step[...] = base[...] + norm / curve * direction[...]


def swap(block, axis):
    return lax.all_to_all(block, axis, 0, 0, tiled=True)


def array(*shape, dtype=F32):
    return jax.ShapeDtypeStruct(shape, dtype)


def body(covariates, labels, weights, sample_index):
    user_rows, width = covariates.shape
    classes = weights.shape[0]
    row_count, depth = lax.axis_size("row"), lax.axis_size("z")
    users = user_rows * row_count
    sub_total = sample_index.shape[0] * row_count
    own = user_rows // CORES // depth
    wide = CORES * width
    blocks = (depth, classes, own)
    rows = covariates.reshape(CORES * depth, own, width)
    labels = labels.reshape(-1, LANES)
    sample_index = sample_index.reshape(-1, LANES)

    pair_rows = lax.all_gather(rows, "c", axis=0, tiled=True)
    other = pl.pallas_call(
        send_other_kernel,
        out_shape=array(*blocks),
        in_specs=[pl.BlockSpec(memory_space=pl.ANY)] * 2,
        out_specs=pl.BlockSpec(memory_space=pltpu.VMEM),
        scratch_shapes=[
            pltpu.VMEM(weights.shape, F32),
            pltpu.VMEM((depth, own, width), BF16),
            pltpu.SemaphoreType.DMA,
            pltpu.SemaphoreType.DMA((GROUPS,)),
        ],
    )(weights, rows)
    other = lax.ppermute(other, "c", [(0, 1), (1, 0)])
    mine, count = kernel_call(
        functools.partial(keep_kernel, user_rows), (array(*blocks), array(1, own)), weights, rows, sample_index
    )
    sent = kernel_call(code_kernel, array(*blocks, dtype=jnp.int16), mine, other)
    shares, sent = kernel_call(
        misfit_kernel, (array(classes, own), array(*blocks, dtype=BF16)), swap(sent, "z"), labels
    )

    def add_pair(part, dtype):
        parts = lax.all_gather(part, "c", axis=0)
        return swap(kernel_call(pair_kernel, array(row_count, classes, wide, dtype=dtype), parts), "row")

    ridge = RIDGE_WEIGHT * users / row_count
    part = kernel_call(
        functools.partial(misfit_columns_kernel, ridge), array(classes, wide), swap(sent, "z"), pair_rows, weights
    )
    gradient, residual, sent = kernel_call(
        functools.partial(gradient_kernel, users),
        (array(classes, width), array(classes, wide), array(*blocks, dtype=BF16)),
        add_pair(part, F32), pair_rows,
    )
    response, sent = kernel_call(
        weigh_kernel, (array(classes, own), array(*blocks, dtype=BF16)), swap(sent, "z"), shares, count
    )
    part = kernel_call(image_columns_kernel, array(classes, wide), swap(sent, "z"), pair_rows)
    image, sent = kernel_call(
        functools.partial(image_kernel, sub_total),
        (array(classes, wide), array(*blocks, dtype=BF16)),
        add_pair(part, BF16), residual, pair_rows,
    )
    base, direction, sent = kernel_call(
        direction_kernel,
        (array(classes, width), array(classes, width), array(depth, 1, LANES)),
        swap(sent, "z"), response, shares, count, residual, image,
    )
    sent = kernel_call(relay_kernel, array(row_count * CORES, 1, LANES), swap(sent, "z"))
    newton_step = kernel_call(
        functools.partial(step_kernel, sub_total, row_count * CORES),
        array(classes, width),
        swap(sent, ("row", "c")), base, direction,
    )
    return gradient, newton_step


def solution(mesh):
    rows, cols = mesh.devices.shape
    fine = Mesh(mesh.devices.reshape(rows, cols // CORES, CORES), ("row", "z", "c"))
    in_specs = (P("row", ("z", "c")), P("row"), P(None, ("z", "c")), P("row"))
    out_specs = (P(None, ("z", "c")), P(None, ("z", "c")))
    return jax.shard_map(body, mesh=fine, in_specs=in_specs, out_specs=out_specs, check_vma=False)
```

time: 184 us -> 187 us (1.016)
  starting transfers between devices: 23.1 us -> 8.82 us
  blocking collectives: 139 us -> 153 us
  between operations: 0.78 us -> 14.1 us
  waiting for transfers between devices: 11 us -> 1.08 us
  Pallas kernels: 4.85 us -> 7.04 us
  other arithmetic: 1.88 us -> 0 us
    all_to_all x8 -> x9, blocking collectives: 128 us -> 142 us  [swap(): return lax.all_to_all(block, axis, 0, 0, tiled=True)]
    all_to_all x1 -> x0, waiting for transfers between devices: 9.91 us -> none  [swap(): return lax.all_to_all(block, axis, 0, 0, tiled=True)]
    all_to_all x1 -> x0, starting transfers between devices: 9.55 us -> none  [swap(): return lax.all_to_all(block, axis, 0, 0, tiled=True)]
    ppermute x3 -> x1, starting transfers between devices: 13.5 us -> 8.79 us  [body(): other = lax.ppermute(other, 'c', [(0, 1), (1, 0)])]
    pallas_call x0 -> x1, Pallas kernels: none -> 2.45 us  [body(): pl.pallas_call(send_other_kernel, out_shape=array(*blocks), in_specs=[pl....]
    reduce_sum x1 -> x0, other arithmetic: 1.87 us -> none  [body(): jnp.sum((sample_index[:, None] == position[None, :]).astype(F32), axis=0)]
  transfers between devices with their start and end apart: 4 -> 2, of which waited for: 2 -> 1; matrix products, arithmetic and copies ran while one was open for 1% -> 0% of each run, Pallas kernels for 0% -> 2%
where the time goes in v3:
time: 187 us; the launch traced here: 186 us
  blocking collectives  153 us (82%)
  between operations  14.1 us (8%)
  starting transfers between devices  8.82 us (5%)
  Pallas kernels  7.04 us (4%)
  local copies, waits for them, and re-layouts  2.21 us (1%)
    all_to_all x9, blocking collectives, swap(): return lax.all_to_all(block, axis, 0, 0, tiled=True)  142 us
    all_gather x2, blocking collectives, add_pair(): parts = lax.all_gather(part, 'c', axis=0)  10.6 us
    ppermute x1, starting transfers between devices, body(): other = lax.ppermute(other, 'c', [(0, 1), (1, 0)])  8.79 us
    pallas_call x13, Pallas kernels, kernel_call(): pl.pallas_call(body, out_shape=out_shape, in_specs=[pl.BlockSpec(memory_s...  4.59 us
  transfers between devices with their start and end apart: 2, of which 1 were waited for; matrix products, arithmetic and copies ran while one was open for 0% of the time, Pallas kernels for 2%

profile of v3, /device:TPU:1, one launch (start us, length us, event | category | flops | bytes accessed | tf_op | source)
XLA Modules:
  0.0 186.0 jit_solution(10962040933705063562)
XLA Ops:
  7.2 0.0 copy-start.2
  7.2 0.0 copy-start.3
  7.2 0.0 copy-start.5
  7.2 0.0 copy-start.4
  7.2 0.0 all-gather.4.cloned.1.call-start
  7.2 0.7 all-gather.4.cloned.1.call-update
  7.9 2.5 %shard_map.60 = f32[16,16,256]{2,1,0:T(8,128)} custom-call(f32[16,128]{1,0:T(8,128)} %weights.3, bf16[32,256,128]{2,1,0:T(8,128)(2,1)} %bitcast.6), custom_call_target="tpu_custom_call" | custom-call | tf_op jit(solution)/shard_map/pallas_call | solution.py:263
  10.4 8.8 %collective-permute-start = (f32[16,16,256]{2,1,0:T(8,128)}, f32[16,16,256]{2,1,0:T(8,128)S(1)}, u32[]{:S(2)}, u32[]{:S(2)}) collective-permute-start(f32[16,16,256]{2,1,0:T(8,128)} %shard_map.60), channel_id=1, source_target_pairs={{0,1},{1,0},{2,3},{3,2},{4,5},{5,4},{6,7},{7,6},{8,9},{9,8},{10,11... | collective-permute-start | bytes 786440 | tf_op jit(solution)/shard_map/ppermute | solution.py:275
  19.2 0.0 copy-done.2
  19.2 0.0 copy-done.3
  19.2 0.0 copy-done.5
  19.2 0.9 shard_map.59
  20.1 0.4 collective-permute-done.other
  20.5 0.2 shard_map.61
  20.7 21.5 %all_to_all.45.came = s16[16,16,256]{2,1,0:T(8,128)(2,1)S(1)} all-to-all(s16[16,16,256]{2,1,0:T(8,128)(2,1)S(1)} %shard_map.61), channel_id=1, replica_groups=mesh['row'=16,'z'=16,'c'=2] {'z'}, dimensions={0} | all-to-all | bytes 262144 | tf_op jit(solution)/shard_map/all_to_all | solution.py:242
  42.2 0.0 copy-done.4
  42.2 0.1 shard_map.62
  42.3 18.3 %all_to_all.46.came = bf16[16,16,256]{2,1,0:T(8,128)(2,1)S(1)} all-to-all(bf16[16,16,256]{2,1,0:T(8,128)(2,1)S(1)} %get-tuple-element.17), channel_id=1, replica_groups=mesh['row'=16,'z'=16,'c'=2] {'z'}, dimensions={0} | all-to-all | bytes 262144 | tf_op jit(solution)/shard_map/all_to_all | solution.py:242
  60.5 0.0 all-gather.4.cloned.1.call-done.rows
  60.5 0.0 copy-start
  60.5 2.2 %copy-done = bf16[64,256,128]{2,1,0:T(8,128)(2,1)S(1)} copy-done((bf16[64,256,128]{2,1,0:T(8,128)(2,1)S(1)}, bf16[64,256,128]{2,1,0:T(8,128)(2,1)}, u32[]{:S(2)}) %copy-start) | copy-done | bytes 4194328
  62.7 0.0 copy-start.1
  62.7 0.4 shard_map.63
  63.1 5.3 %all-gather = f32[32,256]{1,0:T(8,128)S(1)} all-gather(f32[16,256]{1,0:T(8,128)S(1)} %shard_map.63), channel_id=2, replica_groups=mesh['row'=16,'z'=16,'c'=2] {'c'}, dimensions={0}, use_global_device_ids=true | all-gather | bytes 49152 | tf_op jit(solution)/shard_map/all_gather | solution.py:285
  68.5 14.1 %all_to_all.47.came = f32[16,16,256]{2,1,0:T(8,128)S(1)} all-to-all(f32[16,16,256]{2,1,0:T(8,128)S(1)} %shard_map.64), channel_id=1, replica_groups=mesh['row'=16,'z'=16,'c'=2] {'row'}, dimensions={0} | all-to-all | bytes 524288 | tf_op jit(solution)/shard_map/all_to_all | solution.py:242
  82.6 0.0 copy-done.1
  82.6 0.8 shard_map.65
  83.5 15.3 %all_to_all.48.came = bf16[16,16,256]{2,1,0:T(8,128)(2,1)S(1)} all-to-all(bf16[16,16,256]{2,1,0:T(8,128)(2,1)S(1)} %get-tuple-element.19), channel_id=1, replica_groups=mesh['row'=16,'z'=16,'c'=2] {'z'}, dimensions={0} | all-to-all | bytes 262144 | tf_op jit(solution)/shard_map/all_to_all | solution.py:242
  98.8 16.9 %all_to_all.49.came = bf16[16,16,256]{2,1,0:T(8,128)(2,1)S(1)} all-to-all(bf16[16,16,256]{2,1,0:T(8,128)(2,1)S(1)} %get-tuple-element.22), channel_id=1, replica_groups=mesh['row'=16,'z'=16,'c'=2] {'z'}, dimensions={0} | all-to-all | bytes 262144 | tf_op jit(solution)/shard_map/all_to_all | solution.py:242
  115.7 0.4 shard_map.67
  116.0 5.3 %all-gather.1 = f32[32,256]{1,0:T(8,128)S(1)} all-gather(f32[16,256]{1,0:T(8,128)S(1)} %shard_map.67), channel_id=3, replica_groups=mesh['row'=16,'z'=16,'c'=2] {'c'}, dimensions={0}, use_global_device_ids=true | all-gather | bytes 49152 | tf_op jit(solution)/shard_map/all_gather | solution.py:285
  121.4 10.8 %all_to_all.50.came = bf16[16,16,256]{2,1,0:T(8,128)(2,1)S(1)} all-to-all(bf16[16,16,256]{2,1,0:T(8,128)(2,1)S(1)} %shard_map.68), channel_id=1, replica_groups=mesh['row'=16,'z'=16,'c'=2] {'row'}, dimensions={0} | all-to-all | bytes 262144 | tf_op jit(solution)/shard_map/all_to_all | solution.py:242
  132.1 0.7 shard_map.69
  132.8 14.9 %all_to_all.51.came = bf16[16,16,256]{2,1,0:T(8,128)(2,1)S(1)} all-to-all(bf16[16,16,256]{2,1,0:T(8,128)(2,1)S(1)} %get-tuple-element.24), channel_id=1, replica_groups=mesh['row'=16,'z'=16,'c'=2] {'z'}, dimensions={0} | all-to-all | bytes 262144 | tf_op jit(solution)/shard_map/all_to_all | solution.py:242
  147.6 0.2 shard_map.70
  147.9 16.2 %all_to_all.52.came = f32[16,1,128]{2,1,0:T(1,128)S(1)} all-to-all(f32[16,1,128]{2,1,0:T(1,128)S(1)} %get-tuple-element.27), channel_id=1, replica_groups=mesh['row'=16,'z'=16,'c'=2] {'z'}, dimensions={0} | all-to-all | bytes 16384 | tf_op jit(solution)/shard_map/all_to_all | solution.py:242
  164.1 14.2 %all_to_all.53.came = f32[32,1,128]{2,1,0:T(1,128)S(1)} all-to-all(f32[32,1,128]{2,1,0:T(1,128)S(1)} %shard_map.71), channel_id=1, replica_groups=mesh['row'=16,'z'=16,'c'=2] {'row','c'}, dimensions={0} | all-to-all | bytes 32768 | tf_op jit(solution)/shard_map/all_to_all | solution.py:242
  178.3 0.8 shard_map.72
  (4 shorter events, 0.1 us)
Async XLA Ops:
  7.2 12.0 %copy-start.2 = (bf16[8192,128]{1,0:T(8,128)(2,1)S(1)}, bf16[8192,128]{1,0:T(8,128)(2,1)}, u32[]{:S(2)}) copy-start(bf16[8192,128]{1,0:T(8,128)(2,1)} %param.4) | copy-start | bytes 6291460
  7.2 12.0 %copy-start.3 = (f32[16,128]{1,0:T(8,128)S(1)}, f32[16,128]{1,0:T(8,128)}, u32[]{:S(2)}) copy-start(f32[16,128]{1,0:T(8,128)} %weights.3) | copy-start | bytes 24580
  7.2 12.0 %copy-start.5 = (s32[4096]{0:T(1024)S(1)}, s32[4096]{0:T(1024)}, u32[]{:S(2)}) copy-start(s32[4096]{0:T(1024)} %param.7) | copy-start | bytes 49156
  7.2 35.0 %copy-start.4 = (s32[8192]{0:T(1024)S(1)}, s32[8192]{0:T(1024)}, u32[]{:S(2)}) copy-start(s32[8192]{0:T(1024)} %param.5) | copy-start | bytes 98308
  7.2 53.3 %all-gather.4.cloned.1.call-start = ((), (), s32[]{:S(2)}) async-start(), calls=%async_computation.9 | async-start | bytes 6291456 | tf_op jit(solution)/shard_map/all_gather | solution.py:262
  10.4 10.1 %collective-permute-start = (f32[16,16,256]{2,1,0:T(8,128)}, f32[16,16,256]{2,1,0:T(8,128)S(1)}, u32[]{:S(2)}, u32[]{:S(2)}) collective-permute-start(f32[16,16,256]{2,1,0:T(8,128)} %shard_map.60), channel_id=1, source_target_pairs={{0,1},{1,0},{2,3},{3,2},{4,5},{5,4},{6,7},{7,6},{8,9},{9,8},{10,11... | collective-permute-start | bytes 786440 | tf_op jit(solution)/shard_map/ppermute | solution.py:275
  60.5 2.2 %copy-start = (bf16[64,256,128]{2,1,0:T(8,128)(2,1)S(1)}, bf16[64,256,128]{2,1,0:T(8,128)(2,1)}, u32[]{:S(2)}) copy-start(bf16[64,256,128]{2,1,0:T(8,128)(2,1)} %all-gather.4.cloned.1.call-done.rows) | copy-start | bytes 12582916
  62.7 19.9 %copy-start.1 = (bf16[64,256,128]{2,1,0:T(8,128)(2,1)S(1)}, bf16[64,256,128]{2,1,0:T(8,128)(2,1)}, u32[]{:S(2)}) copy-start(bf16[64,256,128]{2,1,0:T(8,128)(2,1)} %all-gather.4.cloned.1.call-done.rows) | copy-start | bytes 12582916
Sparse Core Ops, SparseCore 0:
  10.1 30.8 all-gather.3

commit v4 on v3

--- a/solution.py
+++ b/solution.py
@@ -12,7 +12,6 @@
 LANES, SUBLANES = 128, 8
 PIECES = 3
 CORES = 2
-GROUPS = 4
 TOP, REACH = 32767.0, 768.0
 
 
@@ -50,34 +49,9 @@
     return jnp.sum(jnp.sum(block, axis=1, keepdims=True), axis=0, keepdims=True)
 
 
-def send_other_kernel(weights_hbm, rows_hbm, other, weights, rows, weights_sem, row_sems):
-    depth = other.shape[0]
-    first = (1 - lax.axis_index("c")) * depth
-    head = pltpu.make_async_copy(weights_hbm, weights, weights_sem)
-    head.start()
-    step = depth // GROUPS
-    copies = []
-    for group in range(GROUPS):
-        here = pl.ds(group * step, step)
-        copies.append(
-            pltpu.make_async_copy(rows_hbm.at[pl.ds(first + group * step, step)], rows.at[here], row_sems.at[group])
-        )
-        copies[-1].start()
-    head.wait()
-    rounded = weights[...].astype(BF16)
-    for group in range(GROUPS):
-        copies[group].wait()
-        for level in range(group * step, (group + 1) * step):
-            other[level] = times_transposed(rounded, rows[level])
-
-
-def keep_kernel(user_rows, weights, rows, index, mine, count):
-    depth, _, own = mine.shape
-    core = lax.axis_index("c")
-    place = core * depth + lax.axis_index("z")
-    rounded = weights[...].astype(BF16)
-    for level in range(depth):
-        mine[level] = times_transposed(rounded, rows[core * depth + level])
+def count_kernel(user_rows, depth, index, count):
+    own = count.shape[1]
+    place = lax.axis_index("c") * depth + lax.axis_index("z")
     offset = index[...] - (lax.axis_index("row") * user_rows + place * own)
     low, high = offset & (LANES - 1), offset >> 7
     low_place = lax.broadcasted_iota(jnp.int32, (LANES, LANES), 0)
@@ -91,9 +65,11 @@
         count[:, part * LANES : (part + 1) * LANES] = drawn[part : part + 1]
 
 
-def code_kernel(mine, other, sent):
-    for level in range(mine.shape[0]):
-        value = mine[level] + other[level]
+def code_kernel(pair_weights, rows, sent):
+    depth = sent.shape[0]
+    rounded = [pair_weights[core].astype(BF16) for core in range(CORES)]
+    for level in range(depth):
+        value = sum(times_transposed(rounded[core], rows[core * depth + level]) for core in range(CORES))
         value = value - value[-1:]
         largest = jnp.max(jnp.abs(value), axis=0, keepdims=True)
         scale = jnp.minimum(jnp.floor(largest * (TOP / REACH)) + 1.0, TOP)
@@ -125,7 +101,7 @@
     depth = came.shape[0]
     sums = []
     for owner in (core, 1 - core):
-        first = (owner * CORES + core) * depth
+        first = owner * depth
         total = jnp.dot(came[0], rows[first], preferred_element_type=F32)
         for level in range(1, depth):
             total = total + jnp.dot(came[level], rows[first + level], preferred_element_type=F32)
@@ -140,19 +116,27 @@
     part[:, width:] = far
 
 
-def image_columns_kernel(came, rows, part):
-    own, far = columns(came, rows)
-    width = own.shape[1]
-    part[:, :width] = own
-    part[:, width:] = far
+def image_columns_kernel(came, rows, sent):
+    repeat(sent, jnp.concatenate(columns(came, rows), axis=1).astype(BF16))
 
 
 def pair_kernel(parts, sent):
     core = lax.axis_index("c")
-    mine, far = parts[core], parts[1 - core]
-    width = mine.shape[1] // CORES
-    both = mine + jnp.concatenate([far[:, width:], far[:, :width]], axis=1)
-    repeat(sent, both.astype(sent.dtype))
+    repeat(sent, parts[core] + turned(parts[1 - core]))
+
+
+def turned(block):
+    width = block.shape[1] // CORES
+    return jnp.concatenate([block[:, width:], block[:, :width]], axis=1)
+
+
+def arrived_pair(ref):
+    core = lax.axis_index("c")
+    near, far = ref[core].astype(F32), ref[1 - core].astype(F32)
+    for row in range(1, ref.shape[0] // CORES):
+        near = near + ref[row * CORES + core].astype(F32)
+        far = far + ref[row * CORES + 1 - core].astype(F32)
+    return near + turned(far)
 
 
 def respond(vector, rows, depth):
@@ -160,8 +144,8 @@
     width = rows.shape[2]
     own, far = vector[:, :width].astype(BF16), vector[:, width:].astype(BF16)
     for level in range(depth):
-        near = times_transposed(own, rows[(core * CORES + core) * depth + level])
-        yield near + times_transposed(far, rows[((1 - core) * CORES + core) * depth + level])
+        near = times_transposed(own, rows[core * depth + level])
+        yield near + times_transposed(far, rows[(1 - core) * depth + level])
 
 
 def gradient_kernel(users, came, rows, gradient, residual, sent):
@@ -182,7 +166,7 @@
 
 def image_kernel(sub_total, came, residual, rows, image, sent):
     start = residual[...]
-    value = arrived(came) / sub_total + RIDGE_WEIGHT * start
+    value = arrived_pair(came) / sub_total + RIDGE_WEIGHT * start
     image[...] = value
     _, classes, own = sent.shape
     lane = lax.broadcasted_iota(jnp.int32, (1, own), 1)
@@ -259,49 +243,35 @@
     labels = labels.reshape(-1, LANES)
     sample_index = sample_index.reshape(-1, LANES)
 
-    pair_rows = lax.all_gather(rows, "c", axis=0, tiled=True)
-    other = pl.pallas_call(
-        send_other_kernel,
-        out_shape=array(*blocks),
-        in_specs=[pl.BlockSpec(memory_space=pl.ANY)] * 2,
-        out_specs=pl.BlockSpec(memory_space=pltpu.VMEM),
-        scratch_shapes=[
-            pltpu.VMEM(weights.shape, F32),
-            pltpu.VMEM((depth, own, width), BF16),
-            pltpu.SemaphoreType.DMA,
-            pltpu.SemaphoreType.DMA((GROUPS,)),
-        ],
-    )(weights, rows)
-    other = lax.ppermute(other, "c", [(0, 1), (1, 0)])
-    mine, count = kernel_call(
-        functools.partial(keep_kernel, user_rows), (array(*blocks), array(1, own)), weights, rows, sample_index
-    )
-    sent = kernel_call(code_kernel, array(*blocks, dtype=jnp.int16), mine, other)
+    pair_rows = swap(rows, "c")
+    pair_weights = lax.all_gather(weights, "c", axis=0)
+    count = kernel_call(functools.partial(count_kernel, user_rows, depth), array(1, own), sample_index)
+    sent = kernel_call(code_kernel, array(*blocks, dtype=jnp.int16), pair_weights, pair_rows)
     shares, sent = kernel_call(
         misfit_kernel, (array(classes, own), array(*blocks, dtype=BF16)), swap(sent, "z"), labels
     )
-
-    def add_pair(part, dtype):
-        parts = lax.all_gather(part, "c", axis=0)
-        return swap(kernel_call(pair_kernel, array(row_count, classes, wide, dtype=dtype), parts), "row")
 
     ridge = RIDGE_WEIGHT * users / row_count
     part = kernel_call(
         functools.partial(misfit_columns_kernel, ridge), array(classes, wide), swap(sent, "z"), pair_rows, weights
     )
+    parts = lax.all_gather(part, "c", axis=0)
+    sent = kernel_call(pair_kernel, array(row_count, classes, wide), parts)
     gradient, residual, sent = kernel_call(
         functools.partial(gradient_kernel, users),
         (array(classes, width), array(classes, wide), array(*blocks, dtype=BF16)),
-        add_pair(part, F32), pair_rows,
+        swap(sent, "row"), pair_rows,
     )
     response, sent = kernel_call(
         weigh_kernel, (array(classes, own), array(*blocks, dtype=BF16)), swap(sent, "z"), shares, count
     )
-    part = kernel_call(image_columns_kernel, array(classes, wide), swap(sent, "z"), pair_rows)
+    sent = kernel_call(
+        image_columns_kernel, array(row_count * CORES, classes, wide, dtype=BF16), swap(sent, "z"), pair_rows
+    )
     image, sent = kernel_call(
         functools.partial(image_kernel, sub_total),
         (array(classes, wide), array(*blocks, dtype=BF16)),
-        add_pair(part, BF16), residual, pair_rows,
+        swap(sent, ("row", "c")), residual, pair_rows,
     )
     base, direction, sent = kernel_call(
         direction_kernel,

time: 187 us -> 173 us (0.925)
  between operations: 14.1 us -> 0.7 us
  blocking collectives: 153 us -> 140 us
  waiting for transfers between devices: 1.08 us -> 11.5 us
  starting transfers between devices: 8.82 us -> 14.2 us
  local copies, waits for them, and re-layouts: 2.21 us -> 0.01 us
    all_to_all x0 -> x2, starting transfers between devices: none -> 14.2 us  [swap(): return lax.all_to_all(block, axis, 0, 0, tiled=True)]
    all_to_all x0 -> x2, waiting for transfers between devices: none -> 11.5 us  [swap(): return lax.all_to_all(block, axis, 0, 0, tiled=True)]
    all_to_all x9 -> x8, blocking collectives: 142 us -> 133 us  [swap(): return lax.all_to_all(block, axis, 0, 0, tiled=True)]
    ppermute x1 -> x0, starting transfers between devices: 8.79 us -> none  [body(): other = lax.ppermute(other, 'c', [(0, 1), (1, 0)])]
    all_gather x2, blocking collectives: 10.6 us -> 7.63 us  [the longest x1 5.32 us: body(): parts = lax.all_gather(part, 'c', axis=0)]
    pallas_call x1 -> x0, Pallas kernels: 2.45 us -> none  [body(): pl.pallas_call(send_other_kernel, out_shape=array(*blocks), in_specs=[pl....]
    unnamed x12 -> x6, local copies, waits for them, and re-layouts: 2.21 us -> 0.01 us
    pallas_call x13 -> x12, Pallas kernels: 4.59 us -> 5.31 us  [kernel_call(): pl.pallas_call(body, out_shape=out_shape, in_specs=[pl.BlockSpec(memory_s...]
  transfers between devices with their start and end apart: 2 -> 2, of which waited for: 1 -> 2; matrix products, arithmetic and copies ran while one was open for 0% -> 0% of each run, Pallas kernels for 2% -> 0%
where the time goes in v4:
time: 173 us; the launch traced here: 172 us
  blocking collectives  140 us (81%)
  starting transfers between devices  14.2 us (8%)
  waiting for transfers between devices  11.5 us (7%)
  Pallas kernels  5.31 us (3%)
    all_to_all x8, blocking collectives, swap(): return lax.all_to_all(block, axis, 0, 0, tiled=True)  133 us
    all_to_all x2, starting transfers between devices, swap(): return lax.all_to_all(block, axis, 0, 0, tiled=True)  14.2 us
    all_to_all x2, waiting for transfers between devices, swap(): return lax.all_to_all(block, axis, 0, 0, tiled=True)  11.5 us
    all_gather x1, blocking collectives, body(): parts = lax.all_gather(part, 'c', axis=0)  5.32 us
    pallas_call x12, Pallas kernels, kernel_call(): pl.pallas_call(body, out_shape=out_shape, in_specs=[pl.BlockSpec(memory_s...  5.31 us
  transfers between devices with their start and end apart: 2, of which 2 were waited for; matrix products, arithmetic and copies ran while one was open for 0% of the time, Pallas kernels for 0%

profile of v4, /device:TPU:1, one launch (start us, length us, event | category | flops | bytes accessed | tf_op | source)
XLA Modules:
  0.0 171.9 jit_solution(6708742752419479512)
XLA Ops:
  0.6 0.0 copy-start
  0.6 10.6 %all-to-all-start = ((bf16[32,256,128]{2,1,0:T(8,128)(2,1)}), bf16[32,256,128]{2,1,0:T(8,128)(2,1)S(1)}, u32[]{:S(2)}, u32[]{:S(2)}) async-start(bf16[32,256,128]{2,1,0:T(8,128)(2,1)} %bitcast.9), calls=%async_computation | async-start | bytes 4194304 | tf_op jit(solution)/shard_map/all_to_all | solution.py:226
  11.3 0.0 copy-done
  11.3 0.0 copy-start.1
  11.3 2.3 %all-gather = f32[32,128]{1,0:T(8,128)S(1)} all-gather(f32[16,128]{1,0:T(8,128)S(1)} %copy-done), channel_id=2, replica_groups=mesh['row'=16,'z'=16,'c'=2] {'c'}, dimensions={0}, use_global_device_ids=true | all-gather | bytes 24576 | tf_op jit(solution)/shard_map/all_gather | solution.py:247
  13.6 0.2 all-to-all-done.rows
  13.8 0.7 shard_map.59
  14.5 21.5 %all_to_all.50.came = s16[16,16,256]{2,1,0:T(8,128)(2,1)S(1)} all-to-all(s16[16,16,256]{2,1,0:T(8,128)(2,1)S(1)} %shard_map.59), channel_id=1, replica_groups=mesh['row'=16,'z'=16,'c'=2] {'z'}, dimensions={0} | all-to-all | bytes 262144 | tf_op jit(solution)/shard_map/all_to_all | solution.py:226
  36.0 0.0 copy-done.1
  36.0 0.1 shard_map.60
  36.1 18.3 %all_to_all.51.came = bf16[16,16,256]{2,1,0:T(8,128)(2,1)S(1)} all-to-all(bf16[16,16,256]{2,1,0:T(8,128)(2,1)S(1)} %get-tuple-element.14), channel_id=1, replica_groups=mesh['row'=16,'z'=16,'c'=2] {'z'}, dimensions={0} | all-to-all | bytes 262144 | tf_op jit(solution)/shard_map/all_to_all | solution.py:226
  54.3 0.4 shard_map.61
  54.7 0.0 copy-start.2
  54.7 5.3 %all-gather.1 = f32[32,256]{1,0:T(8,128)S(1)} all-gather(f32[16,256]{1,0:T(8,128)S(1)} %shard_map.61), channel_id=3, replica_groups=mesh['row'=16,'z'=16,'c'=2] {'c'}, dimensions={0}, use_global_device_ids=true | all-gather | bytes 49152 | tf_op jit(solution)/shard_map/all_gather | solution.py:258
  60.0 14.1 %all_to_all.52.came = f32[16,16,256]{2,1,0:T(8,128)S(1)} all-to-all(f32[16,16,256]{2,1,0:T(8,128)S(1)} %shard_map.62), channel_id=1, replica_groups=mesh['row'=16,'z'=16,'c'=2] {'row'}, dimensions={0} | all-to-all | bytes 524288 | tf_op jit(solution)/shard_map/all_to_all | solution.py:226
  74.2 1.3 shard_map.63
  75.5 3.5 %all-to-all-start.4 = ((bf16[16,16,256]{2,1,0:T(8,128)(2,1)}), bf16[16,16,256]{2,1,0:T(8,128)(2,1)S(1)}, u32[]{:S(2)}, u32[]{:S(2)}) async-start(bf16[16,16,256]{2,1,0:T(8,128)(2,1)} %get-tuple-element.16), calls=%async_computation.4 | async-start | bytes 262144 | tf_op jit(solution)/shard_map/all_to_all | solution.py:226
  79.0 0.0 copy-done.2
  79.0 0.7 shard_map.64.count
  79.7 11.3 %all-to-all-done.4.came = bf16[16,16,256]{2,1,0:T(8,128)(2,1)S(1)} async-done(((bf16[16,16,256]{2,1,0:T(8,128)(2,1)}), bf16[16,16,256]{2,1,0:T(8,128)(2,1)S(1)}, u32[]{:S(2)}, u32[]{:S(2)}) %all-to-all-start.4) | async-done | bytes 131104 | tf_op jit(solution)/shard_map/all_to_all | solution.py:226
  91.0 16.9 %all_to_all.53.came = bf16[16,16,256]{2,1,0:T(8,128)(2,1)S(1)} all-to-all(bf16[16,16,256]{2,1,0:T(8,128)(2,1)S(1)} %get-tuple-element.18), channel_id=1, replica_groups=mesh['row'=16,'z'=16,'c'=2] {'z'}, dimensions={0} | all-to-all | bytes 262144 | tf_op jit(solution)/shard_map/all_to_all | solution.py:226
  107.9 0.4 shard_map.66
  108.3 17.2 %all_to_all.54.came = bf16[32,16,256]{2,1,0:T(8,128)(2,1)S(1)} all-to-all(bf16[32,16,256]{2,1,0:T(8,128)(2,1)S(1)} %shard_map.66), channel_id=1, replica_groups=mesh['row'=16,'z'=16,'c'=2] {'row','c'}, dimensions={0} | all-to-all | bytes 524288 | tf_op jit(solution)/shard_map/all_to_all | solution.py:226
  125.5 0.7 shard_map.67
  126.2 15.0 %all_to_all.55.came = bf16[16,16,256]{2,1,0:T(8,128)(2,1)S(1)} all-to-all(bf16[16,16,256]{2,1,0:T(8,128)(2,1)S(1)} %get-tuple-element.20), channel_id=1, replica_groups=mesh['row'=16,'z'=16,'c'=2] {'z'}, dimensions={0} | all-to-all | bytes 262144 | tf_op jit(solution)/shard_map/all_to_all | solution.py:226
  141.2 0.2 shard_map.68
  141.4 17.6 %all_to_all.56.came = f32[16,1,128]{2,1,0:T(1,128)S(1)} all-to-all(f32[16,1,128]{2,1,0:T(1,128)S(1)} %get-tuple-element.23), channel_id=1, replica_groups=mesh['row'=16,'z'=16,'c'=2] {'z'}, dimensions={0} | all-to-all | bytes 16384 | tf_op jit(solution)/shard_map/all_to_all | solution.py:226
  159.0 12.0 %all_to_all.57.came = f32[32,1,128]{2,1,0:T(1,128)S(1)} all-to-all(f32[32,1,128]{2,1,0:T(1,128)S(1)} %shard_map.69), channel_id=1, replica_groups=mesh['row'=16,'z'=16,'c'=2] {'row','c'}, dimensions={0} | all-to-all | bytes 32768 | tf_op jit(solution)/shard_map/all_to_all | solution.py:226
  171.0 0.8 shard_map.70
  (3 shorter events, 0.1 us)
Async XLA Ops:
  0.6 10.7 %copy-start = (f32[16,128]{1,0:T(8,128)S(1)}, f32[16,128]{1,0:T(8,128)}, u32[]{:S(2)}) copy-start(f32[16,128]{1,0:T(8,128)} %weights.1) | copy-start | bytes 24580
  0.6 13.1 %all-to-all-start = ((bf16[32,256,128]{2,1,0:T(8,128)(2,1)}), bf16[32,256,128]{2,1,0:T(8,128)(2,1)S(1)}, u32[]{:S(2)}, u32[]{:S(2)}) async-start(bf16[32,256,128]{2,1,0:T(8,128)(2,1)} %bitcast.9), calls=%async_computation | async-start | bytes 4194304 | tf_op jit(solution)/shard_map/all_to_all | solution.py:226
  11.3 24.7 %copy-start.1 = (s32[8192]{0:T(1024)S(1)}, s32[8192]{0:T(1024)}, u32[]{:S(2)}) copy-start(s32[8192]{0:T(1024)} %param.5) | copy-start | bytes 98308
  54.7 24.3 %copy-start.2 = (s32[4096]{0:T(1024)S(1)}, s32[4096]{0:T(1024)}, u32[]{:S(2)}) copy-start(s32[4096]{0:T(1024)} %param.7) | copy-start | bytes 49156
  75.5 15.5 %all-to-all-start.4 = ((bf16[16,16,256]{2,1,0:T(8,128)(2,1)}), bf16[16,16,256]{2,1,0:T(8,128)(2,1)S(1)}, u32[]{:S(2)}, u32[]{:S(2)}) async-start(bf16[16,16,256]{2,1,0:T(8,128)(2,1)} %get-tuple-element.16), calls=%async_computation.4 | async-start | bytes 262144 | tf_op jit(solution)/shard_map/all_to_all | solution.py:226

commit v5 on v4

--- a/solution.py
+++ b/solution.py
@@ -12,6 +12,7 @@
 LANES, SUBLANES = 128, 8
 PIECES = 3
 CORES = 2
+GROUPS = 4
 TOP, REACH = 32767.0, 768.0
 
 
@@ -49,10 +50,31 @@
     return jnp.sum(jnp.sum(block, axis=1, keepdims=True), axis=0, keepdims=True)
 
 
-def count_kernel(user_rows, depth, index, count):
-    own = count.shape[1]
-    place = lax.axis_index("c") * depth + lax.axis_index("z")
-    offset = index[...] - (lax.axis_index("row") * user_rows + place * own)
+def parcel_kernel(weights, rows_hbm, parcel_hbm, rounded, weights_sem, row_sems):
+    half = rows_hbm.shape[0] // CORES
+    first = (1 - lax.axis_index("c")) * half
+    step = half // GROUPS
+    copies = []
+    for group in range(GROUPS):
+        source = rows_hbm.at[pl.ds(first + group * step, step)]
+        target = parcel_hbm.at[pl.ds(group * step, step)]
+        copies.append(pltpu.make_async_copy(source, target, row_sems.at[group]))
+        copies[-1].start()
+    rounded[...] = weights[...].astype(BF16)
+    copies.append(pltpu.make_async_copy(rounded, parcel_hbm.at[pl.ds(half, weights.shape[0])], weights_sem))
+    copies[-1].start()
+    for copy in copies:
+        copy.wait()
+
+
+def keep_kernel(weights, rows, index, mine, count):
+    depth, _, own = mine.shape
+    core = lax.axis_index("c")
+    place = core * depth + lax.axis_index("z")
+    rounded = weights[...].astype(BF16)
+    for level in range(depth):
+        mine[level] = times_transposed(rounded, rows[core * depth + level])
+    offset = index[...] - (lax.axis_index("row") * (CORES * depth * own) + place * own)
     low, high = offset & (LANES - 1), offset >> 7
     low_place = lax.broadcasted_iota(jnp.int32, (LANES, LANES), 0)
     high_place = lax.broadcasted_iota(jnp.int32, (SUBLANES, LANES), 0)
@@ -65,17 +87,17 @@
         count[:, part * LANES : (part + 1) * LANES] = drawn[part : part + 1]
 
 
-def code_kernel(pair_weights, rows, sent):
-    depth = sent.shape[0]
-    rounded = [pair_weights[core].astype(BF16) for core in range(CORES)]
+def code_kernel(mine, parcel, sent):
+    depth, classes, own = mine.shape
+    rounded = parcel[depth * own :]
     for level in range(depth):
-        value = sum(times_transposed(rounded[core], rows[core * depth + level]) for core in range(CORES))
+        value = mine[level] + times_transposed(rounded, parcel[level * own : (level + 1) * own])
         value = value - value[-1:]
         largest = jnp.max(jnp.abs(value), axis=0, keepdims=True)
         scale = jnp.minimum(jnp.floor(largest * (TOP / REACH)) + 1.0, TOP)
         code = jnp.floor(value * (TOP * TOP / REACH / scale) + 0.5)
         code = jnp.clip(code, -TOP, TOP)
-        last = lax.broadcasted_iota(jnp.int32, value.shape, 0) == value.shape[0] - 1
+        last = lax.broadcasted_iota(jnp.int32, value.shape, 0) == classes - 1
         sent[level] = jnp.where(last, scale, code).astype(jnp.int32).astype(jnp.int16)
 
 
@@ -96,28 +118,26 @@
     repeat(sent, (share - (label == kind).astype(F32)).astype(BF16))
 
 
-def columns(came, rows):
-    core = lax.axis_index("c")
-    depth = came.shape[0]
-    sums = []
-    for owner in (core, 1 - core):
-        first = owner * depth
-        total = jnp.dot(came[0], rows[first], preferred_element_type=F32)
-        for level in range(1, depth):
-            total = total + jnp.dot(came[level], rows[first + level], preferred_element_type=F32)
-        sums.append(total)
-    return sums
-
-
-def misfit_columns_kernel(ridge, came, rows, weights, part):
-    own, far = columns(came, rows)
+def columns(came, rows, parcel):
+    core = lax.axis_index("c")
+    depth, _, own = came.shape
+    near = jnp.dot(came[0], rows[core * depth], preferred_element_type=F32)
+    far = jnp.dot(came[0], parcel[:own], preferred_element_type=F32)
+    for level in range(1, depth):
+        near = near + jnp.dot(came[level], rows[core * depth + level], preferred_element_type=F32)
+        far = far + jnp.dot(came[level], parcel[level * own : (level + 1) * own], preferred_element_type=F32)
+    return near, far
+
+
+def misfit_columns_kernel(ridge, came, rows, parcel, weights, part):
+    own, far = columns(came, rows, parcel)
     width = own.shape[1]
     part[:, :width] = own + ridge * weights[...]
     part[:, width:] = far
 
 
-def image_columns_kernel(came, rows, sent):
-    repeat(sent, jnp.concatenate(columns(came, rows), axis=1).astype(BF16))
+def image_columns_kernel(came, rows, parcel, sent):
+    repeat(sent, jnp.concatenate(columns(came, rows, parcel), axis=1).astype(BF16))
 
 
 def pair_kernel(parts, sent):
@@ -139,21 +159,19 @@
     return near + turned(far)
 
 
-def respond(vector, rows, depth):
-    core = lax.axis_index("c")
-    width = rows.shape[2]
+def respond(vector, rows, parcel, depth):
+    core = lax.axis_index("c")
+    _, users, width = rows.shape
     own, far = vector[:, :width].astype(BF16), vector[:, width:].astype(BF16)
     for level in range(depth):
         near = times_transposed(own, rows[core * depth + level])
-        yield near + times_transposed(far, rows[(1 - core) * depth + level])
-
-
-def gradient_kernel(users, came, rows, gradient, residual, sent):
-    width = gradient.shape[1]
-    value = arrived(came) / users
-    gradient[...] = value[:, :width]
-    residual[...] = -value
-    for level, answer in enumerate(respond(-value, rows, sent.shape[0])):
+        yield near + times_transposed(far, parcel[level * users : (level + 1) * users])
+
+
+def gradient_kernel(users, came, rows, parcel, residual, sent):
+    value = arrived(came) / -users
+    residual[...] = value
+    for level, answer in enumerate(respond(value, rows, parcel, sent.shape[0])):
         sent[level] = answer.astype(BF16)
 
 
@@ -164,7 +182,7 @@
     repeat(sent, (count[...] * (share * (value - shares_sum(share, value)))).astype(BF16))
 
 
-def image_kernel(sub_total, came, residual, rows, image, sent):
+def image_kernel(sub_total, came, residual, rows, parcel, image, sent):
     start = residual[...]
     value = arrived_pair(came) / sub_total + RIDGE_WEIGHT * start
     image[...] = value
@@ -178,7 +196,7 @@
             line = jnp.where(lane == which * PIECES + piece, head, line)
             left = left - head
     last = lax.broadcasted_iota(jnp.int32, (classes, own), 0) == classes - 1
-    for level, answer in enumerate(respond(value, rows, sent.shape[0])):
+    for level, answer in enumerate(respond(value, rows, parcel, sent.shape[0])):
         sent[level] = jnp.where(last, line, answer - answer[-1:]).astype(BF16)
 
 
@@ -215,7 +233,8 @@
     repeat(sent, arrived(came))
 
 
-def step_kernel(sub_total, copies, came, base, direction, newton_step):
+def step_kernel(sub_total, copies, came, residual, base, direction, gradient, newton_step):
+    gradient[...] = -residual[:, : gradient.shape[1]]
     line = arrived(came)
     norm, square, spread = line[:, 0:1] / copies, line[:, 1:2] / copies, line[:, 2:3]
     curve = spread / sub_total + RIDGE_WEIGHT * square
@@ -243,35 +262,45 @@
     labels = labels.reshape(-1, LANES)
     sample_index = sample_index.reshape(-1, LANES)
 
-    pair_rows = swap(rows, "c")
-    pair_weights = lax.all_gather(weights, "c", axis=0)
-    count = kernel_call(functools.partial(count_kernel, user_rows, depth), array(1, own), sample_index)
-    sent = kernel_call(code_kernel, array(*blocks, dtype=jnp.int16), pair_weights, pair_rows)
+    parcel = pl.pallas_call(
+        parcel_kernel,
+        out_shape=array(user_rows // CORES + classes, width, dtype=BF16),
+        in_specs=[pl.BlockSpec(memory_space=pltpu.VMEM), pl.BlockSpec(memory_space=pl.ANY)],
+        out_specs=pl.BlockSpec(memory_space=pl.ANY),
+        scratch_shapes=[
+            pltpu.VMEM(weights.shape, BF16),
+            pltpu.SemaphoreType.DMA,
+            pltpu.SemaphoreType.DMA((GROUPS,)),
+        ],
+    )(weights, covariates)
+    parcel = lax.ppermute(parcel, "c", [(0, 1), (1, 0)])
+    mine, count = kernel_call(keep_kernel, (array(*blocks), array(1, own)), weights, rows, sample_index)
+    sent = kernel_call(code_kernel, array(*blocks, dtype=jnp.int16), mine, parcel)
     shares, sent = kernel_call(
         misfit_kernel, (array(classes, own), array(*blocks, dtype=BF16)), swap(sent, "z"), labels
     )
 
     ridge = RIDGE_WEIGHT * users / row_count
     part = kernel_call(
-        functools.partial(misfit_columns_kernel, ridge), array(classes, wide), swap(sent, "z"), pair_rows, weights
+        functools.partial(misfit_columns_kernel, ridge), array(classes, wide), swap(sent, "z"), rows, parcel, weights
     )
     parts = lax.all_gather(part, "c", axis=0)
     sent = kernel_call(pair_kernel, array(row_count, classes, wide), parts)
-    gradient, residual, sent = kernel_call(
+    residual, sent = kernel_call(
         functools.partial(gradient_kernel, users),
-        (array(classes, width), array(classes, wide), array(*blocks, dtype=BF16)),
-        swap(sent, "row"), pair_rows,
+        (array(classes, wide), array(*blocks, dtype=BF16)),
+        swap(sent, "row"), rows, parcel,
     )
     response, sent = kernel_call(
         weigh_kernel, (array(classes, own), array(*blocks, dtype=BF16)), swap(sent, "z"), shares, count
     )
     sent = kernel_call(
-        image_columns_kernel, array(row_count * CORES, classes, wide, dtype=BF16), swap(sent, "z"), pair_rows
+        image_columns_kernel, array(row_count * CORES, classes, wide, dtype=BF16), swap(sent, "z"), rows, parcel
     )
     image, sent = kernel_call(
         functools.partial(image_kernel, sub_total),
         (array(classes, wide), array(*blocks, dtype=BF16)),
-        swap(sent, ("row", "c")), residual, pair_rows,
+        swap(sent, ("row", "c")), residual, rows, parcel,
     )
     base, direction, sent = kernel_call(
         direction_kernel,
@@ -279,12 +308,11 @@
         swap(sent, "z"), response, shares, count, residual, image,
     )
     sent = kernel_call(relay_kernel, array(row_count * CORES, 1, LANES), swap(sent, "z"))
-    newton_step = kernel_call(
+    return kernel_call(
         functools.partial(step_kernel, sub_total, row_count * CORES),
-        array(classes, width),
-        swap(sent, ("row", "c")), base, direction,
-    )
-    return gradient, newton_step
+        (array(classes, width), array(classes, width)),
+        swap(sent, ("row", "c")), residual, base, direction,
+    )
 
 
 def solution(mesh):

time: 173 us -> 203 us (1.17)
  Pallas kernels: 5.31 us -> 38.5 us
  blocking collectives: 140 us -> 153 us
  waiting for transfers between devices: 11.5 us -> 1.53 us
  starting transfers between devices: 14.2 us -> 8.79 us
    pallas_call x0 -> x1, Pallas kernels: none -> 33.8 us  [body(): pl.pallas_call(parcel_kernel, out_shape=array(user_rows // CORES + classe...]
    all_to_all x8 -> x9, blocking collectives: 133 us -> 148 us  [swap(): return lax.all_to_all(block, axis, 0, 0, tiled=True)]
    all_to_all x2 -> x0, starting transfers between devices: 14.2 us -> none  [swap(): return lax.all_to_all(block, axis, 0, 0, tiled=True)]
    all_to_all x2 -> x0, waiting for transfers between devices: 11.5 us -> none  [swap(): return lax.all_to_all(block, axis, 0, 0, tiled=True)]
    ppermute x0 -> x1, starting transfers between devices: none -> 8.79 us  [body(): parcel = lax.ppermute(parcel, 'c', [(0, 1), (1, 0)])]
    all_gather x1 -> x0, blocking collectives: 2.31 us -> none  [body(): pair_weights = lax.all_gather(weights, 'c', axis=0)]
  transfers between devices with their start and end apart: 2 -> 1, of which waited for: 2 -> 1; matrix products, arithmetic and copies ran while one was open for 0% -> 0% of each run, Pallas kernels for 0% -> 0%
where the time goes in v5:
time: 203 us
  blocking collectives  153 us (75%)
  Pallas kernels  38.5 us (19%)
  starting transfers between devices  8.79 us (4%)
    all_to_all x9, blocking collectives, swap(): return lax.all_to_all(block, axis, 0, 0, tiled=True)  148 us
    pallas_call x1, Pallas kernels, body(): pl.pallas_call(parcel_kernel, out_shape=array(user_rows // CORES + classe...  33.8 us
    ppermute x1, starting transfers between devices, body(): parcel = lax.ppermute(parcel, 'c', [(0, 1), (1, 0)])  8.79 us
    all_gather x1, blocking collectives, body(): parts = lax.all_gather(part, 'c', axis=0)  5.19 us
    pallas_call x12, Pallas kernels, kernel_call(): pl.pallas_call(body, out_shape=out_shape, in_specs=[pl.BlockSpec(memory_s...  4.7 us
  transfers between devices with their start and end apart: 1, of which 1 were waited for; matrix products, arithmetic and copies ran while one was open for 0% of the time, Pallas kernels for 0%

profile of v5, /device:TPU:1, one launch (start us, length us, event | category | flops | bytes accessed | tf_op | source)
XLA Modules:
  0.0 202.6 jit_solution(13064703319422157317)
XLA Ops:
  0.6 0.0 copy-start.1
  0.6 0.0 copy-start
  0.6 0.0 copy-start.3
  0.7 33.8 %shard_map.60 = bf16[4112,128]{1,0:T(8,128)(2,1)} custom-call(f32[16,128]{1,0:T(8,128)} %weights.5, bf16[8192,128]{1,0:T(8,128)(2,1)} %rows_hbm.1), custom_call_target="tpu_custom_call" | custom-call | tf_op jit(solution)/shard_map/pallas_call | solution.py:265
  34.4 8.8 %collective-permute-start = (bf16[4112,128]{1,0:T(8,128)(2,1)}, bf16[4112,128]{1,0:T(8,128)(2,1)S(1)}, u32[]{:S(2)}, u32[]{:S(2)}) collective-permute-start(bf16[4112,128]{1,0:T(8,128)(2,1)} %shard_map.60), channel_id=1, source_target_pairs={{0,1},{1,0},{2,3},{3,2},{4,5},{5,4},{6,7},{7,6},{8,9},{9,8},{10,11... | collective-permute-start | bytes 3158024 | tf_op jit(solution)/shard_map/ppermute | solution.py:276
  43.2 0.0 copy-done.1
  43.2 0.0 copy-done
  43.2 0.0 copy-done.3
  43.2 0.9 shard_map.59
  44.2 0.0 copy-start.2
  44.2 1.5 collective-permute-done.parcel
  45.7 0.4 shard_map.61
  46.1 21.5 %all_to_all.45.came = s16[16,16,256]{2,1,0:T(8,128)(2,1)S(1)} all-to-all(s16[16,16,256]{2,1,0:T(8,128)(2,1)S(1)} %shard_map.61), channel_id=1, replica_groups=mesh['row'=16,'z'=16,'c'=2] {'z'}, dimensions={0} | all-to-all | bytes 262144 | tf_op jit(solution)/shard_map/all_to_all | solution.py:245
  67.6 0.0 copy-done.2
  67.6 0.1 shard_map.62
  67.7 18.3 %all_to_all.46.came = bf16[16,16,256]{2,1,0:T(8,128)(2,1)S(1)} all-to-all(bf16[16,16,256]{2,1,0:T(8,128)(2,1)S(1)} %get-tuple-element.16), channel_id=1, replica_groups=mesh['row'=16,'z'=16,'c'=2] {'z'}, dimensions={0} | all-to-all | bytes 262144 | tf_op jit(solution)/shard_map/all_to_all | solution.py:245
  86.0 0.4 shard_map.63
  86.4 5.2 %all-gather = f32[32,256]{1,0:T(8,128)S(1)} all-gather(f32[16,256]{1,0:T(8,128)S(1)} %shard_map.63), channel_id=2, replica_groups=mesh['row'=16,'z'=16,'c'=2] {'c'}, dimensions={0}, use_global_device_ids=true | all-gather | bytes 49152 | tf_op jit(solution)/shard_map/all_gather | solution.py:287
  91.6 14.1 %all_to_all.47.came = f32[16,16,256]{2,1,0:T(8,128)S(1)} all-to-all(f32[16,16,256]{2,1,0:T(8,128)S(1)} %shard_map.64), channel_id=1, replica_groups=mesh['row'=16,'z'=16,'c'=2] {'row'}, dimensions={0} | all-to-all | bytes 524288 | tf_op jit(solution)/shard_map/all_to_all | solution.py:245
  105.7 0.6 shard_map.65
  106.4 15.3 %all_to_all.48.came = bf16[16,16,256]{2,1,0:T(8,128)(2,1)S(1)} all-to-all(bf16[16,16,256]{2,1,0:T(8,128)(2,1)S(1)} %get-tuple-element.17), channel_id=1, replica_groups=mesh['row'=16,'z'=16,'c'=2] {'z'}, dimensions={0} | all-to-all | bytes 262144 | tf_op jit(solution)/shard_map/all_to_all | solution.py:245
  121.7 16.9 %all_to_all.49.came = bf16[16,16,256]{2,1,0:T(8,128)(2,1)S(1)} all-to-all(bf16[16,16,256]{2,1,0:T(8,128)(2,1)S(1)} %get-tuple-element.20), channel_id=1, replica_groups=mesh['row'=16,'z'=16,'c'=2] {'z'}, dimensions={0} | all-to-all | bytes 262144 | tf_op jit(solution)/shard_map/all_to_all | solution.py:245
  138.6 0.4 shard_map.67
  139.0 17.2 %all_to_all.50.came = bf16[32,16,256]{2,1,0:T(8,128)(2,1)S(1)} all-to-all(bf16[32,16,256]{2,1,0:T(8,128)(2,1)S(1)} %shard_map.67), channel_id=1, replica_groups=mesh['row'=16,'z'=16,'c'=2] {'row','c'}, dimensions={0} | all-to-all | bytes 524288 | tf_op jit(solution)/shard_map/all_to_all | solution.py:245
  156.2 0.7 shard_map.68
  156.9 15.0 %all_to_all.51.came = bf16[16,16,256]{2,1,0:T(8,128)(2,1)S(1)} all-to-all(bf16[16,16,256]{2,1,0:T(8,128)(2,1)S(1)} %get-tuple-element.22), channel_id=1, replica_groups=mesh['row'=16,'z'=16,'c'=2] {'z'}, dimensions={0} | all-to-all | bytes 262144 | tf_op jit(solution)/shard_map/all_to_all | solution.py:245
  171.9 0.2 shard_map.69
  172.1 17.5 %all_to_all.52.came = f32[16,1,128]{2,1,0:T(1,128)S(1)} all-to-all(f32[16,1,128]{2,1,0:T(1,128)S(1)} %get-tuple-element.25), channel_id=1, replica_groups=mesh['row'=16,'z'=16,'c'=2] {'z'}, dimensions={0} | all-to-all | bytes 16384 | tf_op jit(solution)/shard_map/all_to_all | solution.py:245
  189.7 12.0 %all_to_all.53.came = f32[32,1,128]{2,1,0:T(1,128)S(1)} all-to-all(f32[32,1,128]{2,1,0:T(1,128)S(1)} %shard_map.70), channel_id=1, replica_groups=mesh['row'=16,'z'=16,'c'=2] {'row','c'}, dimensions={0} | all-to-all | bytes 32768 | tf_op jit(solution)/shard_map/all_to_all | solution.py:245
  201.7 0.8 shard_map.71
  (3 shorter events, 0.1 us)
Async XLA Ops:
  0.6 42.6 %copy-start.1 = (f32[16,128]{1,0:T(8,128)S(1)}, f32[16,128]{1,0:T(8,128)}, u32[]{:S(2)}) copy-start(f32[16,128]{1,0:T(8,128)} %weights.5) | copy-start | bytes 24580
  0.6 42.6 %copy-start = (bf16[8192,128]{1,0:T(8,128)(2,1)S(1)}, bf16[8192,128]{1,0:T(8,128)(2,1)}, u32[]{:S(2)}) copy-start(bf16[8192,128]{1,0:T(8,128)(2,1)} %rows_hbm.1) | copy-start | bytes 6291460
  0.6 42.6 %copy-start.3 = (s32[4096]{0:T(1024)S(1)}, s32[4096]{0:T(1024)}, u32[]{:S(2)}) copy-start(s32[4096]{0:T(1024)} %param.7) | copy-start | bytes 49156
  34.4 11.3 %collective-permute-start = (bf16[4112,128]{1,0:T(8,128)(2,1)}, bf16[4112,128]{1,0:T(8,128)(2,1)S(1)}, u32[]{:S(2)}, u32[]{:S(2)}) collective-permute-start(bf16[4112,128]{1,0:T(8,128)(2,1)} %shard_map.60), channel_id=1, source_target_pairs={{0,1},{1,0},{2,3},{3,2},{4,5},{5,4},{6,7},{7,6},{8,9},{9,8},{10,11... | collective-permute-start | bytes 3158024 | tf_op jit(solution)/shard_map/ppermute | solution.py:276
  44.2 23.4 %copy-start.2 = (s32[8192]{0:T(1024)S(1)}, s32[8192]{0:T(1024)}, u32[]{:S(2)}) copy-start(s32[8192]{0:T(1024)} %param.5) | copy-start | bytes 98308

commit v6 on v5

--- a/solution.py
+++ b/solution.py
@@ -50,20 +50,25 @@
     return jnp.sum(jnp.sum(block, axis=1, keepdims=True), axis=0, keepdims=True)
 
 
-def parcel_kernel(weights, rows_hbm, parcel_hbm, rounded, weights_sem, row_sems):
-    half = rows_hbm.shape[0] // CORES
+def parcel_kernel(weights, rows_hbm, parcel_hbm, rounded, staged, weights_sem, in_sems, out_sems):
+    half = staged.shape[0]
     first = (1 - lax.axis_index("c")) * half
     step = half // GROUPS
-    copies = []
+    ins, outs = [], []
     for group in range(GROUPS):
-        source = rows_hbm.at[pl.ds(first + group * step, step)]
-        target = parcel_hbm.at[pl.ds(group * step, step)]
-        copies.append(pltpu.make_async_copy(source, target, row_sems.at[group]))
-        copies[-1].start()
+        here = staged.at[pl.ds(group * step, step)]
+        ins.append(
+            pltpu.make_async_copy(rows_hbm.at[pl.ds(first + group * step, step)], here, in_sems.at[group])
+        )
+        outs.append(pltpu.make_async_copy(here, parcel_hbm.at[pl.ds(group * step, step)], out_sems.at[group]))
+        ins[-1].start()
     rounded[...] = weights[...].astype(BF16)
-    copies.append(pltpu.make_async_copy(rounded, parcel_hbm.at[pl.ds(half, weights.shape[0])], weights_sem))
-    copies[-1].start()
-    for copy in copies:
+    outs.append(pltpu.make_async_copy(rounded, parcel_hbm.at[pl.ds(half, weights.shape[0])], weights_sem))
+    outs[-1].start()
+    for group in range(GROUPS):
+        ins[group].wait()
+        outs[group].start()
+    for copy in outs:
         copy.wait()
 
 
@@ -269,7 +274,9 @@
         out_specs=pl.BlockSpec(memory_space=pl.ANY),
         scratch_shapes=[
             pltpu.VMEM(weights.shape, BF16),
+            pltpu.VMEM((user_rows // CORES, width), BF16),
             pltpu.SemaphoreType.DMA,
+            pltpu.SemaphoreType.DMA((GROUPS,)),
             pltpu.SemaphoreType.DMA((GROUPS,)),
         ],
     )(weights, covariates)

time: 203 us -> 172 us (0.85)
  Pallas kernels: 38.5 us -> 7.56 us
    pallas_call x1, Pallas kernels: 33.8 us -> 2.85 us  [body(): pl.pallas_call(parcel_kernel, out_shape=array(user_rows // CORES + classe...]
  transfers between devices with their start and end apart: 1 -> 1, of which waited for: 1 -> 1; matrix products, arithmetic and copies ran while one was open for 0% -> 0% of each run, Pallas kernels for 0% -> 1%
where the time goes in v6:
time: 172 us
  blocking collectives  153 us (89%)
  starting transfers between devices  8.79 us (5%)
  Pallas kernels  7.56 us (4%)
    all_to_all x9, blocking collectives, swap(): return lax.all_to_all(block, axis, 0, 0, tiled=True)  148 us
    ppermute x1, starting transfers between devices, body(): parcel = lax.ppermute(parcel, 'c', [(0, 1), (1, 0)])  8.79 us
    all_gather x1, blocking collectives, body(): parts = lax.all_gather(part, 'c', axis=0)  5.19 us
    pallas_call x12, Pallas kernels, kernel_call(): pl.pallas_call(body, out_shape=out_shape, in_specs=[pl.BlockSpec(memory_s...  4.7 us
  transfers between devices with their start and end apart: 1, of which 1 were waited for; matrix products, arithmetic and copies ran while one was open for 0% of the time, Pallas kernels for 1%

profile of v6, /device:TPU:1, one launch (start us, length us, event | category | flops | bytes accessed | tf_op | source)
XLA Modules:
  0.0 171.7 jit_solution(11673630020788083816)
XLA Ops:
  0.6 0.0 copy-start.1
  0.6 0.0 copy-start
  0.6 0.0 copy-start.3
  0.7 2.9 %shard_map.60 = bf16[4112,128]{1,0:T(8,128)(2,1)} custom-call(f32[16,128]{1,0:T(8,128)} %weights.5, bf16[8192,128]{1,0:T(8,128)(2,1)} %rows_hbm.1), custom_call_target="tpu_custom_call" | custom-call | tf_op jit(solution)/shard_map/pallas_call | solution.py:270
  3.5 8.8 %collective-permute-start = (bf16[4112,128]{1,0:T(8,128)(2,1)}, bf16[4112,128]{1,0:T(8,128)(2,1)S(1)}, u32[]{:S(2)}, u32[]{:S(2)}) collective-permute-start(bf16[4112,128]{1,0:T(8,128)(2,1)} %shard_map.60), channel_id=1, source_target_pairs={{0,1},{1,0},{2,3},{3,2},{4,5},{5,4},{6,7},{7,6},{8,9},{9,8},{10,11... | collective-permute-start | bytes 3158024 | tf_op jit(solution)/shard_map/ppermute | solution.py:283
  12.3 0.0 copy-done.1
  12.3 0.0 copy-done
  12.3 0.0 copy-done.3
  12.3 0.9 shard_map.59
  13.3 0.0 copy-start.2
  13.3 1.5 collective-permute-done.parcel
  14.8 0.4 shard_map.61
  15.2 21.5 %all_to_all.45.came = s16[16,16,256]{2,1,0:T(8,128)(2,1)S(1)} all-to-all(s16[16,16,256]{2,1,0:T(8,128)(2,1)S(1)} %shard_map.61), channel_id=1, replica_groups=mesh['row'=16,'z'=16,'c'=2] {'z'}, dimensions={0} | all-to-all | bytes 262144 | tf_op jit(solution)/shard_map/all_to_all | solution.py:250
  36.7 0.0 copy-done.2
  36.7 0.1 shard_map.62
  36.8 18.3 %all_to_all.46.came = bf16[16,16,256]{2,1,0:T(8,128)(2,1)S(1)} all-to-all(bf16[16,16,256]{2,1,0:T(8,128)(2,1)S(1)} %get-tuple-element.16), channel_id=1, replica_groups=mesh['row'=16,'z'=16,'c'=2] {'z'}, dimensions={0} | all-to-all | bytes 262144 | tf_op jit(solution)/shard_map/all_to_all | solution.py:250
  55.1 0.4 shard_map.63
  55.5 5.2 %all-gather = f32[32,256]{1,0:T(8,128)S(1)} all-gather(f32[16,256]{1,0:T(8,128)S(1)} %shard_map.63), channel_id=2, replica_groups=mesh['row'=16,'z'=16,'c'=2] {'c'}, dimensions={0}, use_global_device_ids=true | all-gather | bytes 49152 | tf_op jit(solution)/shard_map/all_gather | solution.py:294
  60.7 14.1 %all_to_all.47.came = f32[16,16,256]{2,1,0:T(8,128)S(1)} all-to-all(f32[16,16,256]{2,1,0:T(8,128)S(1)} %shard_map.64), channel_id=1, replica_groups=mesh['row'=16,'z'=16,'c'=2] {'row'}, dimensions={0} | all-to-all | bytes 524288 | tf_op jit(solution)/shard_map/all_to_all | solution.py:250
  74.8 0.6 shard_map.65
  75.5 15.3 %all_to_all.48.came = bf16[16,16,256]{2,1,0:T(8,128)(2,1)S(1)} all-to-all(bf16[16,16,256]{2,1,0:T(8,128)(2,1)S(1)} %get-tuple-element.17), channel_id=1, replica_groups=mesh['row'=16,'z'=16,'c'=2] {'z'}, dimensions={0} | all-to-all | bytes 262144 | tf_op jit(solution)/shard_map/all_to_all | solution.py:250
  90.8 16.9 %all_to_all.49.came = bf16[16,16,256]{2,1,0:T(8,128)(2,1)S(1)} all-to-all(bf16[16,16,256]{2,1,0:T(8,128)(2,1)S(1)} %get-tuple-element.20), channel_id=1, replica_groups=mesh['row'=16,'z'=16,'c'=2] {'z'}, dimensions={0} | all-to-all | bytes 262144 | tf_op jit(solution)/shard_map/all_to_all | solution.py:250
  107.7 0.4 shard_map.67
  108.1 17.2 %all_to_all.50.came = bf16[32,16,256]{2,1,0:T(8,128)(2,1)S(1)} all-to-all(bf16[32,16,256]{2,1,0:T(8,128)(2,1)S(1)} %shard_map.67), channel_id=1, replica_groups=mesh['row'=16,'z'=16,'c'=2] {'row','c'}, dimensions={0} | all-to-all | bytes 524288 | tf_op jit(solution)/shard_map/all_to_all | solution.py:250
  125.3 0.7 shard_map.68
  126.0 15.0 %all_to_all.51.came = bf16[16,16,256]{2,1,0:T(8,128)(2,1)S(1)} all-to-all(bf16[16,16,256]{2,1,0:T(8,128)(2,1)S(1)} %get-tuple-element.22), channel_id=1, replica_groups=mesh['row'=16,'z'=16,'c'=2] {'z'}, dimensions={0} | all-to-all | bytes 262144 | tf_op jit(solution)/shard_map/all_to_all | solution.py:250
  141.0 0.2 shard_map.69
  141.2 17.5 %all_to_all.52.came = f32[16,1,128]{2,1,0:T(1,128)S(1)} all-to-all(f32[16,1,128]{2,1,0:T(1,128)S(1)} %get-tuple-element.25), channel_id=1, replica_groups=mesh['row'=16,'z'=16,'c'=2] {'z'}, dimensions={0} | all-to-all | bytes 16384 | tf_op jit(solution)/shard_map/all_to_all | solution.py:250
  158.8 12.0 %all_to_all.53.came = f32[32,1,128]{2,1,0:T(1,128)S(1)} all-to-all(f32[32,1,128]{2,1,0:T(1,128)S(1)} %shard_map.70), channel_id=1, replica_groups=mesh['row'=16,'z'=16,'c'=2] {'row','c'}, dimensions={0} | all-to-all | bytes 32768 | tf_op jit(solution)/shard_map/all_to_all | solution.py:250
  170.8 0.8 shard_map.71
  (3 shorter events, 0.1 us)
Async XLA Ops:
  0.6 11.7 %copy-start.1 = (f32[16,128]{1,0:T(8,128)S(1)}, f32[16,128]{1,0:T(8,128)}, u32[]{:S(2)}) copy-start(f32[16,128]{1,0:T(8,128)} %weights.5) | copy-start | bytes 24580
  0.6 11.7 %copy-start = (bf16[8192,128]{1,0:T(8,128)(2,1)S(1)}, bf16[8192,128]{1,0:T(8,128)(2,1)}, u32[]{:S(2)}) copy-start(bf16[8192,128]{1,0:T(8,128)(2,1)} %rows_hbm.1) | copy-start | bytes 6291460
  0.6 11.7 %copy-start.3 = (s32[4096]{0:T(1024)S(1)}, s32[4096]{0:T(1024)}, u32[]{:S(2)}) copy-start(s32[4096]{0:T(1024)} %param.7) | copy-start | bytes 49156
  3.5 11.3 %collective-permute-start = (bf16[4112,128]{1,0:T(8,128)(2,1)}, bf16[4112,128]{1,0:T(8,128)(2,1)S(1)}, u32[]{:S(2)}, u32[]{:S(2)}) collective-permute-start(bf16[4112,128]{1,0:T(8,128)(2,1)} %shard_map.60), channel_id=1, source_target_pairs={{0,1},{1,0},{2,3},{3,2},{4,5},{5,4},{6,7},{7,6},{8,9},{9,8},{10,11... | collective-permute-start | bytes 3158024 | tf_op jit(solution)/shard_map/ppermute | solution.py:283
  13.3 23.4 %copy-start.2 = (s32[8192]{0:T(1024)S(1)}, s32[8192]{0:T(1024)}, u32[]{:S(2)}) copy-start(s32[8192]{0:T(1024)} %param.5) | copy-start | bytes 98308

commit v7 on v5

--- a/solution.py
+++ b/solution.py
@@ -12,7 +12,7 @@
 LANES, SUBLANES = 128, 8
 PIECES = 3
 CORES = 2
-GROUPS = 4
+LIMIT = 24 * 1024 * 1024
 TOP, REACH = 32767.0, 768.0
 
 
@@ -22,7 +22,7 @@
         out_shape=out_shape,
         in_specs=[pl.BlockSpec(memory_space=pltpu.VMEM)] * len(operands),
         out_specs=jax.tree.map(lambda _: pl.BlockSpec(memory_space=pltpu.VMEM), out_shape),
-        compiler_params=pltpu.CompilerParams(vmem_limit_bytes=24 * 1024 * 1024),
+        compiler_params=pltpu.CompilerParams(vmem_limit_bytes=LIMIT),
     )(*operands)
 
 
@@ -50,21 +50,9 @@
     return jnp.sum(jnp.sum(block, axis=1, keepdims=True), axis=0, keepdims=True)
 
 
-def parcel_kernel(weights, rows_hbm, parcel_hbm, rounded, weights_sem, row_sems):
-    half = rows_hbm.shape[0] // CORES
-    first = (1 - lax.axis_index("c")) * half
-    step = half // GROUPS
-    copies = []
-    for group in range(GROUPS):
-        source = rows_hbm.at[pl.ds(first + group * step, step)]
-        target = parcel_hbm.at[pl.ds(group * step, step)]
-        copies.append(pltpu.make_async_copy(source, target, row_sems.at[group]))
-        copies[-1].start()
+def round_kernel(weights, far, rounded):
+    del far
     rounded[...] = weights[...].astype(BF16)
-    copies.append(pltpu.make_async_copy(rounded, parcel_hbm.at[pl.ds(half, weights.shape[0])], weights_sem))
-    copies[-1].start()
-    for copy in copies:
-        copy.wait()
 
 
 def keep_kernel(weights, rows, index, mine, count):
@@ -136,27 +124,19 @@
     part[:, width:] = far
 
 
-def image_columns_kernel(came, rows, parcel, sent):
-    repeat(sent, jnp.concatenate(columns(came, rows, parcel), axis=1).astype(BF16))
+def image_columns_kernel(came, rows, parcel, part):
+    own, far = columns(came, rows, parcel)
+    width = own.shape[1]
+    part[:, :width] = own
+    part[:, width:] = far
 
 
 def pair_kernel(parts, sent):
     core = lax.axis_index("c")
-    repeat(sent, parts[core] + turned(parts[1 - core]))
-
-
-def turned(block):
-    width = block.shape[1] // CORES
-    return jnp.concatenate([block[:, width:], block[:, :width]], axis=1)
-
-
-def arrived_pair(ref):
-    core = lax.axis_index("c")
-    near, far = ref[core].astype(F32), ref[1 - core].astype(F32)
-    for row in range(1, ref.shape[0] // CORES):
-        near = near + ref[row * CORES + core].astype(F32)
-        far = far + ref[row * CORES + 1 - core].astype(F32)
-    return near + turned(far)
+    mine, far = parts[core], parts[1 - core]
+    width = mine.shape[1] // CORES
+    both = mine + jnp.concatenate([far[:, width:], far[:, :width]], axis=1)
+    repeat(sent, both.astype(sent.dtype))
 
 
 def respond(vector, rows, parcel, depth):
@@ -184,7 +164,7 @@
 
 def image_kernel(sub_total, came, residual, rows, parcel, image, sent):
     start = residual[...]
-    value = arrived_pair(came) / sub_total + RIDGE_WEIGHT * start
+    value = arrived(came) / sub_total + RIDGE_WEIGHT * start
     image[...] = value
     _, classes, own = sent.shape
     lane = lax.broadcasted_iota(jnp.int32, (1, own), 1)
@@ -262,17 +242,16 @@
     labels = labels.reshape(-1, LANES)
     sample_index = sample_index.reshape(-1, LANES)
 
-    parcel = pl.pallas_call(
-        parcel_kernel,
-        out_shape=array(user_rows // CORES + classes, width, dtype=BF16),
+    half = user_rows // CORES
+    far = lax.dynamic_slice_in_dim(covariates, (1 - lax.axis_index("c")) * half, half, 0)
+    rounded = pl.pallas_call(
+        round_kernel,
+        out_shape=array(classes, width, dtype=BF16),
         in_specs=[pl.BlockSpec(memory_space=pltpu.VMEM), pl.BlockSpec(memory_space=pl.ANY)],
-        out_specs=pl.BlockSpec(memory_space=pl.ANY),
-        scratch_shapes=[
-            pltpu.VMEM(weights.shape, BF16),
-            pltpu.SemaphoreType.DMA,
-            pltpu.SemaphoreType.DMA((GROUPS,)),
-        ],
-    )(weights, covariates)
+        out_specs=pl.BlockSpec(memory_space=pltpu.VMEM),
+        compiler_params=pltpu.CompilerParams(vmem_limit_bytes=LIMIT),
+    )(weights, far)
+    parcel = jnp.concatenate([far, rounded], axis=0)
     parcel = lax.ppermute(parcel, "c", [(0, 1), (1, 0)])
     mine, count = kernel_call(keep_kernel, (array(*blocks), array(1, own)), weights, rows, sample_index)
     sent = kernel_call(code_kernel, array(*blocks, dtype=jnp.int16), mine, parcel)
@@ -280,27 +259,27 @@
         misfit_kernel, (array(classes, own), array(*blocks, dtype=BF16)), swap(sent, "z"), labels
     )
 
+    def add_pair(part, dtype):
+        parts = lax.all_gather(part, "c", axis=0)
+        return swap(kernel_call(pair_kernel, array(row_count, classes, wide, dtype=dtype), parts), "row")
+
     ridge = RIDGE_WEIGHT * users / row_count
     part = kernel_call(
         functools.partial(misfit_columns_kernel, ridge), array(classes, wide), swap(sent, "z"), rows, parcel, weights
     )
-    parts = lax.all_gather(part, "c", axis=0)
-    sent = kernel_call(pair_kernel, array(row_count, classes, wide), parts)
     residual, sent = kernel_call(
         functools.partial(gradient_kernel, users),
         (array(classes, wide), array(*blocks, dtype=BF16)),
-        swap(sent, "row"), rows, parcel,
+        add_pair(part, F32), rows, parcel,
     )
     response, sent = kernel_call(
         weigh_kernel, (array(classes, own), array(*blocks, dtype=BF16)), swap(sent, "z"), shares, count
     )
-    sent = kernel_call(
-        image_columns_kernel, array(row_count * CORES, classes, wide, dtype=BF16), swap(sent, "z"), rows, parcel
-    )
+    part = kernel_call(image_columns_kernel, array(classes, wide), swap(sent, "z"), rows, parcel)
     image, sent = kernel_call(
         functools.partial(image_kernel, sub_total),
         (array(classes, wide), array(*blocks, dtype=BF16)),
-        swap(sent, ("row", "c")), residual, rows, parcel,
+        add_pair(part, BF16), residual, rows, parcel,
     )
     base, direction, sent = kernel_call(
         direction_kernel,

time: 203 us -> 170 us (0.84)
  Pallas kernels: 38.5 us -> 4.65 us
    pallas_call x1, Pallas kernels: 33.8 us -> 0.01 us  [body(): pl.pallas_call(round_kernel, out_shape=array(classes, width, dtype=BF16),...]
    all_to_all x9, blocking collectives: 148 us -> 142 us  [swap(): return lax.all_to_all(block, axis, 0, 0, tiled=True)]
    all_gather x1 -> x2, blocking collectives: 5.19 us -> 10.5 us  [add_pair(): parts = lax.all_gather(part, 'c', axis=0)]
    pallas_call x12 -> x13, Pallas kernels: 4.7 us -> 4.65 us  [kernel_call(): pl.pallas_call(body, out_shape=out_shape, in_specs=[pl.BlockSpec(memory_s...]
  transfers between devices with their start and end apart: 1 -> 1, of which waited for: 1 -> 1; matrix products, arithmetic and copies ran while one was open for 0% -> 0% of each run, Pallas kernels for 0% -> 1%
where the time goes in v7:
time: 170 us
  blocking collectives  153 us (90%)
  starting transfers between devices  8.92 us (5%)
  Pallas kernels  4.65 us (3%)
    all_to_all x9, blocking collectives, swap(): return lax.all_to_all(block, axis, 0, 0, tiled=True)  142 us
    all_gather x2, blocking collectives, add_pair(): parts = lax.all_gather(part, 'c', axis=0)  10.5 us
    ppermute x1, starting transfers between devices, body(): parcel = lax.ppermute(parcel, 'c', [(0, 1), (1, 0)])  8.92 us
    pallas_call x13, Pallas kernels, kernel_call(): pl.pallas_call(body, out_shape=out_shape, in_specs=[pl.BlockSpec(memory_s...  4.65 us
  transfers between devices with their start and end apart: 1, of which 1 were waited for; matrix products, arithmetic and copies ran while one was open for 0% of the time, Pallas kernels for 1%

profile of v7, /device:TPU:1, one launch (start us, length us, event | category | flops | bytes accessed | tf_op | source)
XLA Modules:
  0.0 169.7 jit_solution(9391209716396377381)
XLA Ops:
  0.6 0.0 copy-start.1
  0.6 1.3 constant_dynamic-slice_fusion.far
  1.9 0.0 copy-done.1
  2.0 0.0 copy-start
  2.0 0.0 copy-start.3
  2.0 0.1 pad_maximum_fusion
  2.1 0.0 copy-start.2
  2.1 8.9 %collective-permute-start = (bf16[4112,128]{1,0:T(8,128)(2,1)S(1)}, bf16[4112,128]{1,0:T(8,128)(2,1)S(1)}, u32[]{:S(2)}, u32[]{:S(2)}) collective-permute-start(bf16[4112,128]{1,0:T(8,128)(2,1)S(1)} %pad_maximum_fusion), channel_id=1, source_target_pairs={{0,1},{1,0},{2,3},{3,2},{4,5},{5,4},{6,7},{7,6},{8,9},{9,8},{10,11... | collective-permute-start | bytes 3158024 | tf_op jit(solution)/shard_map/ppermute | solution.py:255
  11.0 0.0 copy-done
  11.0 0.0 copy-done.3
  11.0 0.9 shard_map.59
  11.9 1.3 collective-permute-done.parcel
  13.3 0.4 shard_map.61
  13.7 21.5 %all_to_all.45.came = s16[16,16,256]{2,1,0:T(8,128)(2,1)S(1)} all-to-all(s16[16,16,256]{2,1,0:T(8,128)(2,1)S(1)} %shard_map.61), channel_id=1, replica_groups=mesh['row'=16,'z'=16,'c'=2] {'z'}, dimensions={0} | all-to-all | bytes 262144 | tf_op jit(solution)/shard_map/all_to_all | solution.py:225
  35.2 0.0 copy-done.2
  35.2 0.1 shard_map.62
  35.3 18.3 %all_to_all.46.came = bf16[16,16,256]{2,1,0:T(8,128)(2,1)S(1)} all-to-all(bf16[16,16,256]{2,1,0:T(8,128)(2,1)S(1)} %get-tuple-element.16), channel_id=1, replica_groups=mesh['row'=16,'z'=16,'c'=2] {'z'}, dimensions={0} | all-to-all | bytes 262144 | tf_op jit(solution)/shard_map/all_to_all | solution.py:225
  53.5 0.4 shard_map.63
  53.9 5.2 %all-gather = f32[32,256]{1,0:T(8,128)S(1)} all-gather(f32[16,256]{1,0:T(8,128)S(1)} %shard_map.63), channel_id=2, replica_groups=mesh['row'=16,'z'=16,'c'=2] {'c'}, dimensions={0}, use_global_device_ids=true | all-gather | bytes 49152 | tf_op jit(solution)/shard_map/all_gather | solution.py:263
  59.1 14.1 %all_to_all.47.came = f32[16,16,256]{2,1,0:T(8,128)S(1)} all-to-all(f32[16,16,256]{2,1,0:T(8,128)S(1)} %shard_map.64), channel_id=1, replica_groups=mesh['row'=16,'z'=16,'c'=2] {'row'}, dimensions={0} | all-to-all | bytes 524288 | tf_op jit(solution)/shard_map/all_to_all | solution.py:225
  73.3 0.7 shard_map.65
  73.9 15.3 %all_to_all.48.came = bf16[16,16,256]{2,1,0:T(8,128)(2,1)S(1)} all-to-all(bf16[16,16,256]{2,1,0:T(8,128)(2,1)S(1)} %get-tuple-element.17), channel_id=1, replica_groups=mesh['row'=16,'z'=16,'c'=2] {'z'}, dimensions={0} | all-to-all | bytes 262144 | tf_op jit(solution)/shard_map/all_to_all | solution.py:225
  89.3 16.9 %all_to_all.49.came = bf16[16,16,256]{2,1,0:T(8,128)(2,1)S(1)} all-to-all(bf16[16,16,256]{2,1,0:T(8,128)(2,1)S(1)} %get-tuple-element.20), channel_id=1, replica_groups=mesh['row'=16,'z'=16,'c'=2] {'z'}, dimensions={0} | all-to-all | bytes 262144 | tf_op jit(solution)/shard_map/all_to_all | solution.py:225
  106.2 0.4 shard_map.67
  106.5 5.3 %all-gather.1 = f32[32,256]{1,0:T(8,128)S(1)} all-gather(f32[16,256]{1,0:T(8,128)S(1)} %shard_map.67), channel_id=3, replica_groups=mesh['row'=16,'z'=16,'c'=2] {'c'}, dimensions={0}, use_global_device_ids=true | all-gather | bytes 49152 | tf_op jit(solution)/shard_map/all_gather | solution.py:263
  111.9 10.8 %all_to_all.50.came = bf16[16,16,256]{2,1,0:T(8,128)(2,1)S(1)} all-to-all(bf16[16,16,256]{2,1,0:T(8,128)(2,1)S(1)} %shard_map.68), channel_id=1, replica_groups=mesh['row'=16,'z'=16,'c'=2] {'row'}, dimensions={0} | all-to-all | bytes 262144 | tf_op jit(solution)/shard_map/all_to_all | solution.py:225
  122.6 0.6 shard_map.69
  123.3 14.9 %all_to_all.51.came = bf16[16,16,256]{2,1,0:T(8,128)(2,1)S(1)} all-to-all(bf16[16,16,256]{2,1,0:T(8,128)(2,1)S(1)} %get-tuple-element.22), channel_id=1, replica_groups=mesh['row'=16,'z'=16,'c'=2] {'z'}, dimensions={0} | all-to-all | bytes 262144 | tf_op jit(solution)/shard_map/all_to_all | solution.py:225
  138.1 0.2 shard_map.70
  138.3 16.2 %all_to_all.52.came = f32[16,1,128]{2,1,0:T(1,128)S(1)} all-to-all(f32[16,1,128]{2,1,0:T(1,128)S(1)} %get-tuple-element.25), channel_id=1, replica_groups=mesh['row'=16,'z'=16,'c'=2] {'z'}, dimensions={0} | all-to-all | bytes 16384 | tf_op jit(solution)/shard_map/all_to_all | solution.py:225
  154.6 14.2 %all_to_all.53.came = f32[32,1,128]{2,1,0:T(1,128)S(1)} all-to-all(f32[32,1,128]{2,1,0:T(1,128)S(1)} %shard_map.71), channel_id=1, replica_groups=mesh['row'=16,'z'=16,'c'=2] {'row','c'}, dimensions={0} | all-to-all | bytes 32768 | tf_op jit(solution)/shard_map/all_to_all | solution.py:225
  168.8 0.8 shard_map.72
  (5 shorter events, 0.1 us)
Async XLA Ops:
  0.6 1.3 copy-start.1
  2.0 9.1 %copy-start = (bf16[8192,128]{1,0:T(8,128)(2,1)S(1)}, bf16[8192,128]{1,0:T(8,128)(2,1)}, u32[]{:S(2)}) copy-start(bf16[8192,128]{1,0:T(8,128)(2,1)} %param.4) | copy-start | bytes 6291460
  2.0 9.1 %copy-start.3 = (s32[4096]{0:T(1024)S(1)}, s32[4096]{0:T(1024)}, u32[]{:S(2)}) copy-start(s32[4096]{0:T(1024)} %param.7) | copy-start | bytes 49156
  2.1 33.1 %copy-start.2 = (s32[8192]{0:T(1024)S(1)}, s32[8192]{0:T(1024)}, u32[]{:S(2)}) copy-start(s32[8192]{0:T(1024)} %param.5) | copy-start | bytes 98308
  2.1 11.2 %collective-permute-start = (bf16[4112,128]{1,0:T(8,128)(2,1)S(1)}, bf16[4112,128]{1,0:T(8,128)(2,1)S(1)}, u32[]{:S(2)}, u32[]{:S(2)}) collective-permute-start(bf16[4112,128]{1,0:T(8,128)(2,1)S(1)} %pad_maximum_fusion), channel_id=1, source_target_pairs={{0,1},{1,0},{2,3},{3,2},{4,5},{5,4},{6,7},{7,6},{8,9},{9,8},{10,11... | collective-permute-start | bytes 3158024 | tf_op jit(solution)/shard_map/ppermute | solution.py:255

commit v8 on v7

--- a/solution.py
+++ b/solution.py
@@ -283,14 +283,14 @@
     )
     base, direction, sent = kernel_call(
         direction_kernel,
-        (array(classes, width), array(classes, width), array(depth, 1, LANES)),
+        (array(classes, width), array(classes, width), array(depth * CORES, 1, LANES)),
         swap(sent, "z"), response, shares, count, residual, image,
     )
-    sent = kernel_call(relay_kernel, array(row_count * CORES, 1, LANES), swap(sent, "z"))
+    sent = kernel_call(relay_kernel, array(row_count, 1, LANES), swap(sent, ("z", "c")))
     return kernel_call(
         functools.partial(step_kernel, sub_total, row_count * CORES),
         (array(classes, width), array(classes, width)),
-        swap(sent, ("row", "c")), residual, base, direction,
+        swap(sent, "row"), residual, base, direction,
     )
 
 

time: 170 us -> 169 us (level)
  blocking collectives: 153 us -> 151 us
where the time goes in v8:
time: 169 us; the launch traced here: 168 us
  blocking collectives  151 us (89%)
  starting transfers between devices  8.92 us (5%)
  Pallas kernels  4.65 us (3%)
    all_to_all x9, blocking collectives, swap(): return lax.all_to_all(block, axis, 0, 0, tiled=True)  141 us
    all_gather x2, blocking collectives, add_pair(): parts = lax.all_gather(part, 'c', axis=0)  10.5 us
    ppermute x1, starting transfers between devices, body(): parcel = lax.ppermute(parcel, 'c', [(0, 1), (1, 0)])  8.92 us
    pallas_call x13, Pallas kernels, kernel_call(): pl.pallas_call(body, out_shape=out_shape, in_specs=[pl.BlockSpec(memory_s...  4.65 us
  transfers between devices with their start and end apart: 1, of which 1 were waited for; matrix products, arithmetic and copies ran while one was open for 0% of the time, Pallas kernels for 1%

profile of v8, /device:TPU:1, one launch (start us, length us, event | category | flops | bytes accessed | tf_op | source)
XLA Modules:
  0.0 168.2 jit_solution(4713075744932883490)
XLA Ops:
  0.6 0.0 copy-start.1
  0.6 1.3 constant_dynamic-slice_fusion.far
  1.9 0.0 copy-done.1
  2.0 0.0 copy-start
  2.0 0.0 copy-start.3
  2.0 0.1 pad_maximum_fusion
  2.1 0.0 copy-start.2
  2.1 8.9 %collective-permute-start = (bf16[4112,128]{1,0:T(8,128)(2,1)S(1)}, bf16[4112,128]{1,0:T(8,128)(2,1)S(1)}, u32[]{:S(2)}, u32[]{:S(2)}) collective-permute-start(bf16[4112,128]{1,0:T(8,128)(2,1)S(1)} %pad_maximum_fusion), channel_id=1, source_target_pairs={{0,1},{1,0},{2,3},{3,2},{4,5},{5,4},{6,7},{7,6},{8,9},{9,8},{10,11... | collective-permute-start | bytes 3158024 | tf_op jit(solution)/shard_map/ppermute | solution.py:255
  11.0 0.0 copy-done
  11.0 0.0 copy-done.3
  11.0 0.9 shard_map.59
  11.9 1.3 collective-permute-done.parcel
  13.3 0.4 shard_map.61
  13.7 21.5 %all_to_all.45.came = s16[16,16,256]{2,1,0:T(8,128)(2,1)S(1)} all-to-all(s16[16,16,256]{2,1,0:T(8,128)(2,1)S(1)} %shard_map.61), channel_id=1, replica_groups=mesh['row'=16,'z'=16,'c'=2] {'z'}, dimensions={0} | all-to-all | bytes 262144 | tf_op jit(solution)/shard_map/all_to_all | solution.py:225
  35.2 0.0 copy-done.2
  35.2 0.1 shard_map.62
  35.3 18.3 %all_to_all.46.came = bf16[16,16,256]{2,1,0:T(8,128)(2,1)S(1)} all-to-all(bf16[16,16,256]{2,1,0:T(8,128)(2,1)S(1)} %get-tuple-element.16), channel_id=1, replica_groups=mesh['row'=16,'z'=16,'c'=2] {'z'}, dimensions={0} | all-to-all | bytes 262144 | tf_op jit(solution)/shard_map/all_to_all | solution.py:225
  53.5 0.4 shard_map.63
  53.9 5.2 %all-gather = f32[32,256]{1,0:T(8,128)S(1)} all-gather(f32[16,256]{1,0:T(8,128)S(1)} %shard_map.63), channel_id=2, replica_groups=mesh['row'=16,'z'=16,'c'=2] {'c'}, dimensions={0}, use_global_device_ids=true | all-gather | bytes 49152 | tf_op jit(solution)/shard_map/all_gather | solution.py:263
  59.1 14.1 %all_to_all.47.came = f32[16,16,256]{2,1,0:T(8,128)S(1)} all-to-all(f32[16,16,256]{2,1,0:T(8,128)S(1)} %shard_map.64), channel_id=1, replica_groups=mesh['row'=16,'z'=16,'c'=2] {'row'}, dimensions={0} | all-to-all | bytes 524288 | tf_op jit(solution)/shard_map/all_to_all | solution.py:225
  73.3 0.7 shard_map.65
  73.9 15.3 %all_to_all.48.came = bf16[16,16,256]{2,1,0:T(8,128)(2,1)S(1)} all-to-all(bf16[16,16,256]{2,1,0:T(8,128)(2,1)S(1)} %get-tuple-element.17), channel_id=1, replica_groups=mesh['row'=16,'z'=16,'c'=2] {'z'}, dimensions={0} | all-to-all | bytes 262144 | tf_op jit(solution)/shard_map/all_to_all | solution.py:225
  89.3 16.9 %all_to_all.49.came = bf16[16,16,256]{2,1,0:T(8,128)(2,1)S(1)} all-to-all(bf16[16,16,256]{2,1,0:T(8,128)(2,1)S(1)} %get-tuple-element.20), channel_id=1, replica_groups=mesh['row'=16,'z'=16,'c'=2] {'z'}, dimensions={0} | all-to-all | bytes 262144 | tf_op jit(solution)/shard_map/all_to_all | solution.py:225
  106.2 0.4 shard_map.67
  106.5 5.3 %all-gather.1 = f32[32,256]{1,0:T(8,128)S(1)} all-gather(f32[16,256]{1,0:T(8,128)S(1)} %shard_map.67), channel_id=3, replica_groups=mesh['row'=16,'z'=16,'c'=2] {'c'}, dimensions={0}, use_global_device_ids=true | all-gather | bytes 49152 | tf_op jit(solution)/shard_map/all_gather | solution.py:263
  111.9 10.8 %all_to_all.50.came = bf16[16,16,256]{2,1,0:T(8,128)(2,1)S(1)} all-to-all(bf16[16,16,256]{2,1,0:T(8,128)(2,1)S(1)} %shard_map.68), channel_id=1, replica_groups=mesh['row'=16,'z'=16,'c'=2] {'row'}, dimensions={0} | all-to-all | bytes 262144 | tf_op jit(solution)/shard_map/all_to_all | solution.py:225
  122.6 0.6 shard_map.69
  123.3 14.9 %all_to_all.51.came = bf16[16,16,256]{2,1,0:T(8,128)(2,1)S(1)} all-to-all(bf16[16,16,256]{2,1,0:T(8,128)(2,1)S(1)} %get-tuple-element.22), channel_id=1, replica_groups=mesh['row'=16,'z'=16,'c'=2] {'z'}, dimensions={0} | all-to-all | bytes 262144 | tf_op jit(solution)/shard_map/all_to_all | solution.py:225
  138.1 0.2 shard_map.70
  138.4 19.1 %all_to_all.52.came = f32[32,1,128]{2,1,0:T(1,128)S(1)} all-to-all(f32[32,1,128]{2,1,0:T(1,128)S(1)} %get-tuple-element.25), channel_id=1, replica_groups=mesh['row'=16,'z'=16,'c'=2] {'z','c'}, dimensions={0} | all-to-all | bytes 32768 | tf_op jit(solution)/shard_map/all_to_all | solution.py:225
  157.5 9.8 %all_to_all.53.came = f32[16,1,128]{2,1,0:T(1,128)S(1)} all-to-all(f32[16,1,128]{2,1,0:T(1,128)S(1)} %shard_map.71), channel_id=1, replica_groups=mesh['row'=16,'z'=16,'c'=2] {'row'}, dimensions={0} | all-to-all | bytes 16384 | tf_op jit(solution)/shard_map/all_to_all | solution.py:225
  167.4 0.8 shard_map.72
  (5 shorter events, 0.1 us)
Async XLA Ops:
  0.6 1.3 copy-start.1
  2.0 9.1 %copy-start = (bf16[8192,128]{1,0:T(8,128)(2,1)S(1)}, bf16[8192,128]{1,0:T(8,128)(2,1)}, u32[]{:S(2)}) copy-start(bf16[8192,128]{1,0:T(8,128)(2,1)} %param.4) | copy-start | bytes 6291460
  2.0 9.1 %copy-start.3 = (s32[4096]{0:T(1024)S(1)}, s32[4096]{0:T(1024)}, u32[]{:S(2)}) copy-start(s32[4096]{0:T(1024)} %param.7) | copy-start | bytes 49156
  2.1 33.1 %copy-start.2 = (s32[8192]{0:T(1024)S(1)}, s32[8192]{0:T(1024)}, u32[]{:S(2)}) copy-start(s32[8192]{0:T(1024)} %param.5) | copy-start | bytes 98308
  2.1 11.2 %collective-permute-start = (bf16[4112,128]{1,0:T(8,128)(2,1)S(1)}, bf16[4112,128]{1,0:T(8,128)(2,1)S(1)}, u32[]{:S(2)}, u32[]{:S(2)}) collective-permute-start(bf16[4112,128]{1,0:T(8,128)(2,1)S(1)} %pad_maximum_fusion), channel_id=1, source_target_pairs={{0,1},{1,0},{2,3},{3,2},{4,5},{5,4},{6,7},{7,6},{8,9},{9,8},{10,11... | collective-permute-start | bytes 3158024 | tf_op jit(solution)/shard_map/ppermute | solution.py:255

commit v9 on v8

--- a/solution.py
+++ b/solution.py
@@ -14,6 +14,7 @@
 CORES = 2
 LIMIT = 24 * 1024 * 1024
 TOP, REACH = 32767.0, 768.0
+STEPS, SMALLEST = 128.0, 1e-30
 
 
 def kernel_call(body, out_shape, *operands):
@@ -117,11 +118,13 @@
     return near, far
 
 
-def misfit_columns_kernel(ridge, came, rows, parcel, weights, part):
+def misfit_columns_kernel(came, rows, parcel, weights, part):
     own, far = columns(came, rows, parcel)
     width = own.shape[1]
-    part[:, :width] = own + ridge * weights[...]
-    part[:, width:] = far
+    part[0, :, :width] = own
+    part[0, :, width:] = far
+    part[1, :, :width] = weights[...]
+    part[1, :, width:] = jnp.zeros_like(far)
 
 
 def image_columns_kernel(came, rows, parcel, part):
@@ -131,12 +134,29 @@
     part[:, width:] = far
 
 
-def pair_kernel(parts, sent):
-    core = lax.axis_index("c")
-    mine, far = parts[core], parts[1 - core]
+def add_cores(mine, far):
     width = mine.shape[1] // CORES
-    both = mine + jnp.concatenate([far[:, width:], far[:, :width]], axis=1)
-    repeat(sent, both.astype(sent.dtype))
+    return mine + jnp.concatenate([far[:, width:], far[:, :width]], axis=1)
+
+
+def column_scale(code):
+    return jnp.exp2(code * (1.0 / STEPS))
+
+
+def gradient_pair_kernel(parts, weights, sent):
+    core = lax.axis_index("c")
+    both = add_cores(parts[core, 0], parts[1 - core, 0])
+    weights[...] = add_cores(parts[core, 1], parts[1 - core, 1])
+    largest = jnp.maximum(jnp.max(jnp.abs(both), axis=0, keepdims=True), SMALLEST)
+    scale = jnp.floor(jnp.log2(largest) * STEPS) + 2.0
+    code = jnp.clip(jnp.floor(both * (TOP / column_scale(scale)) + 0.5), -TOP, TOP)
+    last = lax.broadcasted_iota(jnp.int32, both.shape, 0) == both.shape[0] - 1
+    repeat(sent, jnp.where(last, scale, code).astype(jnp.int32).astype(jnp.int16))
+
+
+def image_pair_kernel(parts, sent):
+    core = lax.axis_index("c")
+    repeat(sent, add_cores(parts[core], parts[1 - core]).astype(sent.dtype))
 
 
 def respond(vector, rows, parcel, depth):
@@ -148,8 +168,15 @@
         yield near + times_transposed(far, parcel[level * users : (level + 1) * users])
 
 
-def gradient_kernel(users, came, rows, parcel, residual, sent):
-    value = arrived(came) / -users
+def gradient_kernel(users, came, weights, rows, parcel, residual, sent):
+    value = jnp.zeros(weights.shape, F32)
+    for sender in range(came.shape[0]):
+        code = came[sender].astype(jnp.int32).astype(F32)
+        value = value + code * (column_scale(code[-1:]) * (1.0 / TOP))
+    last = lax.broadcasted_iota(jnp.int32, value.shape, 0) == value.shape[0] - 1
+    value = jnp.where(last, 0.0, value)
+    value = jnp.where(last, -jnp.sum(value, axis=0, keepdims=True), value)
+    value = -(value / users + RIDGE_WEIGHT * weights[...])
     residual[...] = value
     for level, answer in enumerate(respond(value, rows, parcel, sent.shape[0])):
         sent[level] = answer.astype(BF16)
@@ -259,27 +286,30 @@
         misfit_kernel, (array(classes, own), array(*blocks, dtype=BF16)), swap(sent, "z"), labels
     )
 
-    def add_pair(part, dtype):
-        parts = lax.all_gather(part, "c", axis=0)
-        return swap(kernel_call(pair_kernel, array(row_count, classes, wide, dtype=dtype), parts), "row")
-
-    ridge = RIDGE_WEIGHT * users / row_count
     part = kernel_call(
-        functools.partial(misfit_columns_kernel, ridge), array(classes, wide), swap(sent, "z"), rows, parcel, weights
+        misfit_columns_kernel, array(CORES, classes, wide), swap(sent, "z"), rows, parcel, weights
+    )
+    wide_weights, sent = kernel_call(
+        gradient_pair_kernel,
+        (array(classes, wide), array(row_count, classes, wide, dtype=jnp.int16)),
+        lax.all_gather(part, "c", axis=0),
     )
     residual, sent = kernel_call(
         functools.partial(gradient_kernel, users),
         (array(classes, wide), array(*blocks, dtype=BF16)),
-        add_pair(part, F32), rows, parcel,
+        swap(sent, "row"), wide_weights, rows, parcel,
     )
     response, sent = kernel_call(
         weigh_kernel, (array(classes, own), array(*blocks, dtype=BF16)), swap(sent, "z"), shares, count
     )
     part = kernel_call(image_columns_kernel, array(classes, wide), swap(sent, "z"), rows, parcel)
+    sent = kernel_call(
+        image_pair_kernel, array(row_count, classes, wide, dtype=BF16), lax.all_gather(part, "c", axis=0)
+    )
     image, sent = kernel_call(
         functools.partial(image_kernel, sub_total),
         (array(classes, wide), array(*blocks, dtype=BF16)),
-        add_pair(part, BF16), residual, rows, parcel,
+        swap(sent, "row"), residual, rows, parcel,
     )
     base, direction, sent = kernel_call(
         direction_kernel,

time: 169 us -> 168 us (level)
  no operation moved by 1% of the time
where the time goes in v9:
time: 168 us; the launch traced here: 167 us
  blocking collectives  150 us (89%)
  starting transfers between devices  8.92 us (5%)
  Pallas kernels  4.69 us (3%)
    all_to_all x9, blocking collectives, swap(): return lax.all_to_all(block, axis, 0, 0, tiled=True)  140 us
    all_gather x2, blocking collectives, body(): lax.all_gather(part, 'c', axis=0)  10.5 us
    ppermute x1, starting transfers between devices, body(): parcel = lax.ppermute(parcel, 'c', [(0, 1), (1, 0)])  8.92 us
    pallas_call x13, Pallas kernels, kernel_call(): pl.pallas_call(body, out_shape=out_shape, in_specs=[pl.BlockSpec(memory_s...  4.69 us
  transfers between devices with their start and end apart: 1, of which 1 were waited for; matrix products, arithmetic and copies ran while one was open for 0% of the time, Pallas kernels for 1%

profile of v9, /device:TPU:1, one launch (start us, length us, event | category | flops | bytes accessed | tf_op | source)
XLA Modules:
  0.0 167.2 jit_solution(17467305112311765742)
XLA Ops:
  0.6 0.0 copy-start.1
  0.6 1.3 constant_dynamic-slice_fusion.far
  1.9 0.0 copy-done.1
  2.0 0.0 copy-start
  2.0 0.0 copy-start.3
  2.0 0.1 pad_maximum_fusion
  2.1 0.0 copy-start.2
  2.1 8.9 %collective-permute-start = (bf16[4112,128]{1,0:T(8,128)(2,1)S(1)}, bf16[4112,128]{1,0:T(8,128)(2,1)S(1)}, u32[]{:S(2)}, u32[]{:S(2)}) collective-permute-start(bf16[4112,128]{1,0:T(8,128)(2,1)S(1)} %pad_maximum_fusion), channel_id=1, source_target_pairs={{0,1},{1,0},{2,3},{3,2},{4,5},{5,4},{6,7},{7,6},{8,9},{9,8},{10,11... | collective-permute-start | bytes 3158024 | tf_op jit(solution)/shard_map/ppermute | solution.py:282
  11.0 0.0 copy-done
  11.0 0.0 copy-done.3
  11.0 0.9 shard_map.59
  11.9 1.3 collective-permute-done.parcel
  13.3 0.4 shard_map.61
  13.7 21.5 %all_to_all.45.came = s16[16,16,256]{2,1,0:T(8,128)(2,1)S(1)} all-to-all(s16[16,16,256]{2,1,0:T(8,128)(2,1)S(1)} %shard_map.61), channel_id=1, replica_groups=mesh['row'=16,'z'=16,'c'=2] {'z'}, dimensions={0} | all-to-all | bytes 262144 | tf_op jit(solution)/shard_map/all_to_all | solution.py:252
  35.2 0.0 copy-done.2
  35.2 0.1 shard_map.62
  35.3 18.3 %all_to_all.46.came = bf16[16,16,256]{2,1,0:T(8,128)(2,1)S(1)} all-to-all(bf16[16,16,256]{2,1,0:T(8,128)(2,1)S(1)} %get-tuple-element.18), channel_id=1, replica_groups=mesh['row'=16,'z'=16,'c'=2] {'z'}, dimensions={0} | all-to-all | bytes 262144 | tf_op jit(solution)/shard_map/all_to_all | solution.py:252
  53.5 0.4 shard_map.63
  53.9 5.2 %all-gather = f32[4,16,256]{2,1,0:T(8,128)S(1)} all-gather(f32[2,16,256]{2,1,0:T(8,128)S(1)} %shard_map.63), channel_id=2, replica_groups=mesh['row'=16,'z'=16,'c'=2] {'c'}, dimensions={0}, use_global_device_ids=true | all-gather | bytes 98304 | tf_op jit(solution)/shard_map/all_gather | solution.py:295
  59.1 0.1 shard_map.64
  59.2 13.2 %all_to_all.47.came = s16[16,16,256]{2,1,0:T(8,128)(2,1)S(1)} all-to-all(s16[16,16,256]{2,1,0:T(8,128)(2,1)S(1)} %get-tuple-element.19), channel_id=1, replica_groups=mesh['row'=16,'z'=16,'c'=2] {'row'}, dimensions={0} | all-to-all | bytes 262144 | tf_op jit(solution)/shard_map/all_to_all | solution.py:252
  72.4 0.7 shard_map.65
  73.1 15.3 %all_to_all.48.came = bf16[16,16,256]{2,1,0:T(8,128)(2,1)S(1)} all-to-all(bf16[16,16,256]{2,1,0:T(8,128)(2,1)S(1)} %get-tuple-element.21), channel_id=1, replica_groups=mesh['row'=16,'z'=16,'c'=2] {'z'}, dimensions={0} | all-to-all | bytes 262144 | tf_op jit(solution)/shard_map/all_to_all | solution.py:252
  88.5 16.9 %all_to_all.49.came = bf16[16,16,256]{2,1,0:T(8,128)(2,1)S(1)} all-to-all(bf16[16,16,256]{2,1,0:T(8,128)(2,1)S(1)} %get-tuple-element.24), channel_id=1, replica_groups=mesh['row'=16,'z'=16,'c'=2] {'z'}, dimensions={0} | all-to-all | bytes 262144 | tf_op jit(solution)/shard_map/all_to_all | solution.py:252
  105.4 0.4 shard_map.67
  105.7 5.3 %all-gather.1 = f32[32,256]{1,0:T(8,128)S(1)} all-gather(f32[16,256]{1,0:T(8,128)S(1)} %shard_map.67), channel_id=3, replica_groups=mesh['row'=16,'z'=16,'c'=2] {'c'}, dimensions={0}, use_global_device_ids=true | all-gather | bytes 49152 | tf_op jit(solution)/shard_map/all_gather | solution.py:307
  111.1 10.6 %all_to_all.50.came = bf16[16,16,256]{2,1,0:T(8,128)(2,1)S(1)} all-to-all(bf16[16,16,256]{2,1,0:T(8,128)(2,1)S(1)} %shard_map.68), channel_id=1, replica_groups=mesh['row'=16,'z'=16,'c'=2] {'row'}, dimensions={0} | all-to-all | bytes 262144 | tf_op jit(solution)/shard_map/all_to_all | solution.py:252
  121.7 0.6 shard_map.69
  122.3 14.9 %all_to_all.51.came = bf16[16,16,256]{2,1,0:T(8,128)(2,1)S(1)} all-to-all(bf16[16,16,256]{2,1,0:T(8,128)(2,1)S(1)} %get-tuple-element.26), channel_id=1, replica_groups=mesh['row'=16,'z'=16,'c'=2] {'z'}, dimensions={0} | all-to-all | bytes 262144 | tf_op jit(solution)/shard_map/all_to_all | solution.py:252
  137.2 0.2 shard_map.70
  137.4 19.1 %all_to_all.52.came = f32[32,1,128]{2,1,0:T(1,128)S(1)} all-to-all(f32[32,1,128]{2,1,0:T(1,128)S(1)} %get-tuple-element.29), channel_id=1, replica_groups=mesh['row'=16,'z'=16,'c'=2] {'z','c'}, dimensions={0} | all-to-all | bytes 32768 | tf_op jit(solution)/shard_map/all_to_all | solution.py:252
  156.6 9.8 %all_to_all.53.came = f32[16,1,128]{2,1,0:T(1,128)S(1)} all-to-all(f32[16,1,128]{2,1,0:T(1,128)S(1)} %shard_map.71), channel_id=1, replica_groups=mesh['row'=16,'z'=16,'c'=2] {'row'}, dimensions={0} | all-to-all | bytes 16384 | tf_op jit(solution)/shard_map/all_to_all | solution.py:252
  166.4 0.8 shard_map.72
  (4 shorter events, 0.1 us)
Async XLA Ops:
  0.6 1.3 copy-start.1
  2.0 9.1 %copy-start = (bf16[8192,128]{1,0:T(8,128)(2,1)S(1)}, bf16[8192,128]{1,0:T(8,128)(2,1)}, u32[]{:S(2)}) copy-start(bf16[8192,128]{1,0:T(8,128)(2,1)} %param.4) | copy-start | bytes 6291460
  2.0 9.1 %copy-start.3 = (s32[4096]{0:T(1024)S(1)}, s32[4096]{0:T(1024)}, u32[]{:S(2)}) copy-start(s32[4096]{0:T(1024)} %param.7) | copy-start | bytes 49156
  2.1 33.1 %copy-start.2 = (s32[8192]{0:T(1024)S(1)}, s32[8192]{0:T(1024)}, u32[]{:S(2)}) copy-start(s32[8192]{0:T(1024)} %param.5) | copy-start | bytes 98308
  2.1 11.2 %collective-permute-start = (bf16[4112,128]{1,0:T(8,128)(2,1)S(1)}, bf16[4112,128]{1,0:T(8,128)(2,1)S(1)}, u32[]{:S(2)}, u32[]{:S(2)}) collective-permute-start(bf16[4112,128]{1,0:T(8,128)(2,1)S(1)} %pad_maximum_fusion), channel_id=1, source_target_pairs={{0,1},{1,0},{2,3},{3,2},{4,5},{5,4},{6,7},{7,6},{8,9},{9,8},{10,11... | collective-permute-start | bytes 3158024 | tf_op jit(solution)/shard_map/ppermute | solution.py:282

commit v10 on v9

--- a/solution.py
+++ b/solution.py
@@ -139,19 +139,29 @@
     return mine + jnp.concatenate([far[:, width:], far[:, :width]], axis=1)
 
 
-def column_scale(code):
+def scale_of(code):
     return jnp.exp2(code * (1.0 / STEPS))
+
+
+def halves(shape):
+    width = shape[1] // CORES
+    column = lax.broadcasted_iota(jnp.int32, shape, 1)
+    last = lax.broadcasted_iota(jnp.int32, shape, 0) == shape[0] - 1
+    start = jnp.logical_or(column == 0, column == width)
+    return jnp.logical_and(last, start), lax.broadcasted_iota(jnp.int32, (1, shape[1]), 1) < width
 
 
 def gradient_pair_kernel(parts, weights, sent):
     core = lax.axis_index("c")
     both = add_cores(parts[core, 0], parts[1 - core, 0])
     weights[...] = add_cores(parts[core, 1], parts[1 - core, 1])
-    largest = jnp.maximum(jnp.max(jnp.abs(both), axis=0, keepdims=True), SMALLEST)
-    scale = jnp.floor(jnp.log2(largest) * STEPS) + 2.0
-    code = jnp.clip(jnp.floor(both * (TOP / column_scale(scale)) + 0.5), -TOP, TOP)
-    last = lax.broadcasted_iota(jnp.int32, both.shape, 0) == both.shape[0] - 1
-    repeat(sent, jnp.where(last, scale, code).astype(jnp.int32).astype(jnp.int16))
+    spot, first = halves(both.shape)
+    size = jnp.max(jnp.abs(both), axis=0, keepdims=True)
+    left = jnp.max(jnp.where(first, size, SMALLEST), axis=1, keepdims=True)
+    right = jnp.max(jnp.where(first, SMALLEST, size), axis=1, keepdims=True)
+    scale = jnp.floor(jnp.log2(jnp.maximum(jnp.where(first, left, right), SMALLEST)) * STEPS) + 2.0
+    code = jnp.clip(jnp.floor(both * (TOP / scale_of(scale)) + 0.5), -TOP, TOP)
+    repeat(sent, jnp.where(spot, scale, code).astype(jnp.int32).astype(jnp.int16))
 
 
 def image_pair_kernel(parts, sent):
@@ -170,12 +180,14 @@
 
 def gradient_kernel(users, came, weights, rows, parcel, residual, sent):
     value = jnp.zeros(weights.shape, F32)
+    spot, first = halves(value.shape)
+    width = value.shape[1] // CORES
     for sender in range(came.shape[0]):
         code = came[sender].astype(jnp.int32).astype(F32)
-        value = value + code * (column_scale(code[-1:]) * (1.0 / TOP))
-    last = lax.broadcasted_iota(jnp.int32, value.shape, 0) == value.shape[0] - 1
-    value = jnp.where(last, 0.0, value)
-    value = jnp.where(last, -jnp.sum(value, axis=0, keepdims=True), value)
+        scale = jnp.where(first, code[-1:, :1], code[-1:, width : width + 1])
+        value = value + code * (scale_of(scale) * (1.0 / TOP))
+    value = jnp.where(spot, 0.0, value)
+    value = jnp.where(spot, -jnp.sum(value, axis=0, keepdims=True), value)
     value = -(value / users + RIDGE_WEIGHT * weights[...])
     residual[...] = value
     for level, answer in enumerate(respond(value, rows, parcel, sent.shape[0])):

time: 168 us -> 168 us (level)
  no operation moved by 1% of the time
where the time goes in v10:
time: 168 us; the launch traced here: 167 us
  blocking collectives  150 us (89%)
  starting transfers between devices  8.92 us (5%)
  Pallas kernels  4.82 us (3%)
    all_to_all x9, blocking collectives, swap(): return lax.all_to_all(block, axis, 0, 0, tiled=True)  140 us
    all_gather x2, blocking collectives, body(): lax.all_gather(part, 'c', axis=0)  10.5 us
    ppermute x1, starting transfers between devices, body(): parcel = lax.ppermute(parcel, 'c', [(0, 1), (1, 0)])  8.92 us
    pallas_call x13, Pallas kernels, kernel_call(): pl.pallas_call(body, out_shape=out_shape, in_specs=[pl.BlockSpec(memory_s...  4.82 us
  transfers between devices with their start and end apart: 1, of which 1 were waited for; matrix products, arithmetic and copies ran while one was open for 0% of the time, Pallas kernels for 1%

profile of v10, /device:TPU:1, one launch (start us, length us, event | category | flops | bytes accessed | tf_op | source)
XLA Modules:
  0.0 167.4 jit_solution(12637109848465208222)
XLA Ops:
  0.6 0.0 copy-start.1
  0.6 1.3 constant_dynamic-slice_fusion.far
  1.9 0.0 copy-done.1
  2.0 0.0 copy-start
  2.0 0.0 copy-start.3
  2.0 0.1 pad_maximum_fusion
  2.1 0.0 copy-start.2
  2.1 8.9 %collective-permute-start = (bf16[4112,128]{1,0:T(8,128)(2,1)S(1)}, bf16[4112,128]{1,0:T(8,128)(2,1)S(1)}, u32[]{:S(2)}, u32[]{:S(2)}) collective-permute-start(bf16[4112,128]{1,0:T(8,128)(2,1)S(1)} %pad_maximum_fusion), channel_id=1, source_target_pairs={{0,1},{1,0},{2,3},{3,2},{4,5},{5,4},{6,7},{7,6},{8,9},{9,8},{10,11... | collective-permute-start | bytes 3158024 | tf_op jit(solution)/shard_map/ppermute | solution.py:294
  11.0 0.0 copy-done
  11.0 0.0 copy-done.3
  11.0 0.9 shard_map.59
  11.9 1.3 collective-permute-done.parcel
  13.3 0.4 shard_map.61
  13.7 21.5 %all_to_all.45.came = s16[16,16,256]{2,1,0:T(8,128)(2,1)S(1)} all-to-all(s16[16,16,256]{2,1,0:T(8,128)(2,1)S(1)} %shard_map.61), channel_id=1, replica_groups=mesh['row'=16,'z'=16,'c'=2] {'z'}, dimensions={0} | all-to-all | bytes 262144 | tf_op jit(solution)/shard_map/all_to_all | solution.py:264
  35.2 0.0 copy-done.2
  35.2 0.1 shard_map.62
  35.3 18.3 %all_to_all.46.came = bf16[16,16,256]{2,1,0:T(8,128)(2,1)S(1)} all-to-all(bf16[16,16,256]{2,1,0:T(8,128)(2,1)S(1)} %get-tuple-element.18), channel_id=1, replica_groups=mesh['row'=16,'z'=16,'c'=2] {'z'}, dimensions={0} | all-to-all | bytes 262144 | tf_op jit(solution)/shard_map/all_to_all | solution.py:264
  53.5 0.4 shard_map.63
  53.9 5.2 %all-gather = f32[4,16,256]{2,1,0:T(8,128)S(1)} all-gather(f32[2,16,256]{2,1,0:T(8,128)S(1)} %shard_map.63), channel_id=2, replica_groups=mesh['row'=16,'z'=16,'c'=2] {'c'}, dimensions={0}, use_global_device_ids=true | all-gather | bytes 98304 | tf_op jit(solution)/shard_map/all_gather | solution.py:307
  59.1 0.1 shard_map.64
  59.3 13.2 %all_to_all.47.came = s16[16,16,256]{2,1,0:T(8,128)(2,1)S(1)} all-to-all(s16[16,16,256]{2,1,0:T(8,128)(2,1)S(1)} %get-tuple-element.19), channel_id=1, replica_groups=mesh['row'=16,'z'=16,'c'=2] {'row'}, dimensions={0} | all-to-all | bytes 262144 | tf_op jit(solution)/shard_map/all_to_all | solution.py:264
  72.5 0.7 shard_map.65
  73.2 15.3 %all_to_all.48.came = bf16[16,16,256]{2,1,0:T(8,128)(2,1)S(1)} all-to-all(bf16[16,16,256]{2,1,0:T(8,128)(2,1)S(1)} %get-tuple-element.21), channel_id=1, replica_groups=mesh['row'=16,'z'=16,'c'=2] {'z'}, dimensions={0} | all-to-all | bytes 262144 | tf_op jit(solution)/shard_map/all_to_all | solution.py:264
  88.6 16.9 %all_to_all.49.came = bf16[16,16,256]{2,1,0:T(8,128)(2,1)S(1)} all-to-all(bf16[16,16,256]{2,1,0:T(8,128)(2,1)S(1)} %get-tuple-element.24), channel_id=1, replica_groups=mesh['row'=16,'z'=16,'c'=2] {'z'}, dimensions={0} | all-to-all | bytes 262144 | tf_op jit(solution)/shard_map/all_to_all | solution.py:264
  105.5 0.4 shard_map.67
  105.9 5.3 %all-gather.1 = f32[32,256]{1,0:T(8,128)S(1)} all-gather(f32[16,256]{1,0:T(8,128)S(1)} %shard_map.67), channel_id=3, replica_groups=mesh['row'=16,'z'=16,'c'=2] {'c'}, dimensions={0}, use_global_device_ids=true | all-gather | bytes 49152 | tf_op jit(solution)/shard_map/all_gather | solution.py:319
  111.2 10.6 %all_to_all.50.came = bf16[16,16,256]{2,1,0:T(8,128)(2,1)S(1)} all-to-all(bf16[16,16,256]{2,1,0:T(8,128)(2,1)S(1)} %shard_map.68), channel_id=1, replica_groups=mesh['row'=16,'z'=16,'c'=2] {'row'}, dimensions={0} | all-to-all | bytes 262144 | tf_op jit(solution)/shard_map/all_to_all | solution.py:264
  121.8 0.6 shard_map.69
  122.4 14.9 %all_to_all.51.came = bf16[16,16,256]{2,1,0:T(8,128)(2,1)S(1)} all-to-all(bf16[16,16,256]{2,1,0:T(8,128)(2,1)S(1)} %get-tuple-element.26), channel_id=1, replica_groups=mesh['row'=16,'z'=16,'c'=2] {'z'}, dimensions={0} | all-to-all | bytes 262144 | tf_op jit(solution)/shard_map/all_to_all | solution.py:264
  137.3 0.2 shard_map.70
  137.5 19.1 %all_to_all.52.came = f32[32,1,128]{2,1,0:T(1,128)S(1)} all-to-all(f32[32,1,128]{2,1,0:T(1,128)S(1)} %get-tuple-element.29), channel_id=1, replica_groups=mesh['row'=16,'z'=16,'c'=2] {'z','c'}, dimensions={0} | all-to-all | bytes 32768 | tf_op jit(solution)/shard_map/all_to_all | solution.py:264
  156.7 9.8 %all_to_all.53.came = f32[16,1,128]{2,1,0:T(1,128)S(1)} all-to-all(f32[16,1,128]{2,1,0:T(1,128)S(1)} %shard_map.71), channel_id=1, replica_groups=mesh['row'=16,'z'=16,'c'=2] {'row'}, dimensions={0} | all-to-all | bytes 16384 | tf_op jit(solution)/shard_map/all_to_all | solution.py:264
  166.5 0.8 shard_map.72
  (4 shorter events, 0.1 us)
Async XLA Ops:
  0.6 1.3 copy-start.1
  2.0 9.1 %copy-start = (bf16[8192,128]{1,0:T(8,128)(2,1)S(1)}, bf16[8192,128]{1,0:T(8,128)(2,1)}, u32[]{:S(2)}) copy-start(bf16[8192,128]{1,0:T(8,128)(2,1)} %param.4) | copy-start | bytes 6291460
  2.0 9.1 %copy-start.3 = (s32[4096]{0:T(1024)S(1)}, s32[4096]{0:T(1024)}, u32[]{:S(2)}) copy-start(s32[4096]{0:T(1024)} %param.7) | copy-start | bytes 49156
  2.1 33.1 %copy-start.2 = (s32[8192]{0:T(1024)S(1)}, s32[8192]{0:T(1024)}, u32[]{:S(2)}) copy-start(s32[8192]{0:T(1024)} %param.5) | copy-start | bytes 98308
  2.1 11.2 %collective-permute-start = (bf16[4112,128]{1,0:T(8,128)(2,1)S(1)}, bf16[4112,128]{1,0:T(8,128)(2,1)S(1)}, u32[]{:S(2)}, u32[]{:S(2)}) collective-permute-start(bf16[4112,128]{1,0:T(8,128)(2,1)S(1)} %pad_maximum_fusion), channel_id=1, source_target_pairs={{0,1},{1,0},{2,3},{3,2},{4,5},{5,4},{6,7},{7,6},{8,9},{9,8},{10,11... | collective-permute-start | bytes 3158024 | tf_op jit(solution)/shard_map/ppermute | solution.py:294

commit v11 on v9

--- a/solution.py
+++ b/solution.py
@@ -139,19 +139,23 @@
     return mine + jnp.concatenate([far[:, width:], far[:, :width]], axis=1)
 
 
-def column_scale(code):
+def scale_of(code):
     return jnp.exp2(code * (1.0 / STEPS))
+
+
+def scale_spot(shape):
+    row, column = (lax.broadcasted_iota(jnp.int32, shape, axis) for axis in range(2))
+    return jnp.logical_and(row == shape[0] - 1, column == 0)
 
 
 def gradient_pair_kernel(parts, weights, sent):
     core = lax.axis_index("c")
     both = add_cores(parts[core, 0], parts[1 - core, 0])
     weights[...] = add_cores(parts[core, 1], parts[1 - core, 1])
-    largest = jnp.maximum(jnp.max(jnp.abs(both), axis=0, keepdims=True), SMALLEST)
-    scale = jnp.floor(jnp.log2(largest) * STEPS) + 2.0
-    code = jnp.clip(jnp.floor(both * (TOP / column_scale(scale)) + 0.5), -TOP, TOP)
-    last = lax.broadcasted_iota(jnp.int32, both.shape, 0) == both.shape[0] - 1
-    repeat(sent, jnp.where(last, scale, code).astype(jnp.int32).astype(jnp.int16))
+    largest = jnp.max(jnp.max(jnp.abs(both), axis=0, keepdims=True), axis=1, keepdims=True)
+    scale = jnp.floor(jnp.log2(jnp.maximum(largest, SMALLEST)) * STEPS) + 2.0
+    code = jnp.clip(jnp.floor(both * (TOP / scale_of(scale)) + 0.5), -TOP, TOP)
+    repeat(sent, jnp.where(scale_spot(both.shape), scale, code).astype(jnp.int32).astype(jnp.int16))
 
 
 def image_pair_kernel(parts, sent):
@@ -170,12 +174,12 @@
 
 def gradient_kernel(users, came, weights, rows, parcel, residual, sent):
     value = jnp.zeros(weights.shape, F32)
+    spot = scale_spot(value.shape)
     for sender in range(came.shape[0]):
         code = came[sender].astype(jnp.int32).astype(F32)
-        value = value + code * (column_scale(code[-1:]) * (1.0 / TOP))
-    last = lax.broadcasted_iota(jnp.int32, value.shape, 0) == value.shape[0] - 1
-    value = jnp.where(last, 0.0, value)
-    value = jnp.where(last, -jnp.sum(value, axis=0, keepdims=True), value)
+        value = value + code * (scale_of(code[-1:, :1]) * (1.0 / TOP))
+    value = jnp.where(spot, 0.0, value)
+    value = jnp.where(spot, -jnp.sum(value, axis=0, keepdims=True), value)
     value = -(value / users + RIDGE_WEIGHT * weights[...])
     residual[...] = value
     for level, answer in enumerate(respond(value, rows, parcel, sent.shape[0])):
@@ -313,14 +317,14 @@
     )
     base, direction, sent = kernel_call(
         direction_kernel,
-        (array(classes, width), array(classes, width), array(depth * CORES, 1, LANES)),
+        (array(classes, width), array(classes, width), array(row_count * CORES, 1, LANES)),
         swap(sent, "z"), response, shares, count, residual, image,
     )
-    sent = kernel_call(relay_kernel, array(row_count, 1, LANES), swap(sent, ("z", "c")))
+    sent = kernel_call(relay_kernel, array(depth, 1, LANES), swap(sent, ("row", "c")))
     return kernel_call(
         functools.partial(step_kernel, sub_total, row_count * CORES),
         (array(classes, width), array(classes, width)),
-        swap(sent, "row"), residual, base, direction,
+        swap(sent, "z"), residual, base, direction,
     )
 
 

time: 168 us -> 168 us (level)
  no operation moved by 1% of the time
where the time goes in v11:
time: 168 us; the launch traced here: 167 us
  blocking collectives  150 us (89%)
  starting transfers between devices  8.92 us (5%)
  Pallas kernels  4.78 us (3%)
    all_to_all x9, blocking collectives, swap(): return lax.all_to_all(block, axis, 0, 0, tiled=True)  140 us
    all_gather x2, blocking collectives, body(): lax.all_gather(part, 'c', axis=0)  10.5 us
    ppermute x1, starting transfers between devices, body(): parcel = lax.ppermute(parcel, 'c', [(0, 1), (1, 0)])  8.92 us
    pallas_call x13, Pallas kernels, kernel_call(): pl.pallas_call(body, out_shape=out_shape, in_specs=[pl.BlockSpec(memory_s...  4.78 us
  transfers between devices with their start and end apart: 1, of which 1 were waited for; matrix products, arithmetic and copies ran while one was open for 0% of the time, Pallas kernels for 1%

profile of v11, /device:TPU:1, one launch (start us, length us, event | category | flops | bytes accessed | tf_op | source)
XLA Modules:
  0.0 167.4 jit_solution(5500851794486045326)
XLA Ops:
  0.6 0.0 copy-start.1
  0.6 1.3 constant_dynamic-slice_fusion.far
  1.9 0.0 copy-done.1
  2.0 0.0 copy-start
  2.0 0.0 copy-start.3
  2.0 0.1 pad_maximum_fusion
  2.1 0.0 copy-start.2
  2.1 8.9 %collective-permute-start = (bf16[4112,128]{1,0:T(8,128)(2,1)S(1)}, bf16[4112,128]{1,0:T(8,128)(2,1)S(1)}, u32[]{:S(2)}, u32[]{:S(2)}) collective-permute-start(bf16[4112,128]{1,0:T(8,128)(2,1)S(1)} %pad_maximum_fusion), channel_id=1, source_target_pairs={{0,1},{1,0},{2,3},{3,2},{4,5},{5,4},{6,7},{7,6},{8,9},{9,8},{10,11... | collective-permute-start | bytes 3158024 | tf_op jit(solution)/shard_map/ppermute | solution.py:286
  11.0 0.0 copy-done
  11.0 0.0 copy-done.3
  11.0 0.9 shard_map.59
  11.9 1.3 collective-permute-done.parcel
  13.3 0.4 shard_map.61
  13.7 21.5 %all_to_all.45.came = s16[16,16,256]{2,1,0:T(8,128)(2,1)S(1)} all-to-all(s16[16,16,256]{2,1,0:T(8,128)(2,1)S(1)} %shard_map.61), channel_id=1, replica_groups=mesh['row'=16,'z'=16,'c'=2] {'z'}, dimensions={0} | all-to-all | bytes 262144 | tf_op jit(solution)/shard_map/all_to_all | solution.py:256
  35.2 0.0 copy-done.2
  35.2 0.1 shard_map.62
  35.3 18.3 %all_to_all.46.came = bf16[16,16,256]{2,1,0:T(8,128)(2,1)S(1)} all-to-all(bf16[16,16,256]{2,1,0:T(8,128)(2,1)S(1)} %get-tuple-element.18), channel_id=1, replica_groups=mesh['row'=16,'z'=16,'c'=2] {'z'}, dimensions={0} | all-to-all | bytes 262144 | tf_op jit(solution)/shard_map/all_to_all | solution.py:256
  53.5 0.4 shard_map.63
  53.9 5.2 %all-gather = f32[4,16,256]{2,1,0:T(8,128)S(1)} all-gather(f32[2,16,256]{2,1,0:T(8,128)S(1)} %shard_map.63), channel_id=2, replica_groups=mesh['row'=16,'z'=16,'c'=2] {'c'}, dimensions={0}, use_global_device_ids=true | all-gather | bytes 98304 | tf_op jit(solution)/shard_map/all_gather | solution.py:299
  59.1 0.1 shard_map.64
  59.3 13.2 %all_to_all.47.came = s16[16,16,256]{2,1,0:T(8,128)(2,1)S(1)} all-to-all(s16[16,16,256]{2,1,0:T(8,128)(2,1)S(1)} %get-tuple-element.19), channel_id=1, replica_groups=mesh['row'=16,'z'=16,'c'=2] {'row'}, dimensions={0} | all-to-all | bytes 262144 | tf_op jit(solution)/shard_map/all_to_all | solution.py:256
  72.5 0.7 shard_map.65
  73.2 15.3 %all_to_all.48.came = bf16[16,16,256]{2,1,0:T(8,128)(2,1)S(1)} all-to-all(bf16[16,16,256]{2,1,0:T(8,128)(2,1)S(1)} %get-tuple-element.21), channel_id=1, replica_groups=mesh['row'=16,'z'=16,'c'=2] {'z'}, dimensions={0} | all-to-all | bytes 262144 | tf_op jit(solution)/shard_map/all_to_all | solution.py:256
  88.5 16.9 %all_to_all.49.came = bf16[16,16,256]{2,1,0:T(8,128)(2,1)S(1)} all-to-all(bf16[16,16,256]{2,1,0:T(8,128)(2,1)S(1)} %get-tuple-element.24), channel_id=1, replica_groups=mesh['row'=16,'z'=16,'c'=2] {'z'}, dimensions={0} | all-to-all | bytes 262144 | tf_op jit(solution)/shard_map/all_to_all | solution.py:256
  105.4 0.4 shard_map.67
  105.8 5.3 %all-gather.1 = f32[32,256]{1,0:T(8,128)S(1)} all-gather(f32[16,256]{1,0:T(8,128)S(1)} %shard_map.67), channel_id=3, replica_groups=mesh['row'=16,'z'=16,'c'=2] {'c'}, dimensions={0}, use_global_device_ids=true | all-gather | bytes 49152 | tf_op jit(solution)/shard_map/all_gather | solution.py:311
  111.1 10.6 %all_to_all.50.came = bf16[16,16,256]{2,1,0:T(8,128)(2,1)S(1)} all-to-all(bf16[16,16,256]{2,1,0:T(8,128)(2,1)S(1)} %shard_map.68), channel_id=1, replica_groups=mesh['row'=16,'z'=16,'c'=2] {'row'}, dimensions={0} | all-to-all | bytes 262144 | tf_op jit(solution)/shard_map/all_to_all | solution.py:256
  121.8 0.6 shard_map.69
  122.4 14.9 %all_to_all.51.came = bf16[16,16,256]{2,1,0:T(8,128)(2,1)S(1)} all-to-all(bf16[16,16,256]{2,1,0:T(8,128)(2,1)S(1)} %get-tuple-element.26), channel_id=1, replica_groups=mesh['row'=16,'z'=16,'c'=2] {'z'}, dimensions={0} | all-to-all | bytes 262144 | tf_op jit(solution)/shard_map/all_to_all | solution.py:256
  137.3 0.2 shard_map.70
  137.5 14.4 %all_to_all.52.came = f32[32,1,128]{2,1,0:T(1,128)S(1)} all-to-all(f32[32,1,128]{2,1,0:T(1,128)S(1)} %get-tuple-element.29), channel_id=1, replica_groups=mesh['row'=16,'z'=16,'c'=2] {'row','c'}, dimensions={0} | all-to-all | bytes 32768 | tf_op jit(solution)/shard_map/all_to_all | solution.py:256
  151.9 14.6 %all_to_all.53.came = f32[16,1,128]{2,1,0:T(1,128)S(1)} all-to-all(f32[16,1,128]{2,1,0:T(1,128)S(1)} %shard_map.71), channel_id=1, replica_groups=mesh['row'=16,'z'=16,'c'=2] {'z'}, dimensions={0} | all-to-all | bytes 16384 | tf_op jit(solution)/shard_map/all_to_all | solution.py:256
  166.5 0.8 shard_map.72
  (4 shorter events, 0.1 us)
Async XLA Ops:
  0.6 1.3 copy-start.1
  2.0 9.1 %copy-start = (bf16[8192,128]{1,0:T(8,128)(2,1)S(1)}, bf16[8192,128]{1,0:T(8,128)(2,1)}, u32[]{:S(2)}) copy-start(bf16[8192,128]{1,0:T(8,128)(2,1)} %param.4) | copy-start | bytes 6291460
  2.0 9.1 %copy-start.3 = (s32[4096]{0:T(1024)S(1)}, s32[4096]{0:T(1024)}, u32[]{:S(2)}) copy-start(s32[4096]{0:T(1024)} %param.7) | copy-start | bytes 49156
  2.1 33.1 %copy-start.2 = (s32[8192]{0:T(1024)S(1)}, s32[8192]{0:T(1024)}, u32[]{:S(2)}) copy-start(s32[8192]{0:T(1024)} %param.5) | copy-start | bytes 98308
  2.1 11.2 %collective-permute-start = (bf16[4112,128]{1,0:T(8,128)(2,1)S(1)}, bf16[4112,128]{1,0:T(8,128)(2,1)S(1)}, u32[]{:S(2)}, u32[]{:S(2)}) collective-permute-start(bf16[4112,128]{1,0:T(8,128)(2,1)S(1)} %pad_maximum_fusion), channel_id=1, source_target_pairs={{0,1},{1,0},{2,3},{3,2},{4,5},{5,4},{6,7},{7,6},{8,9},{9,8},{10,11... | collective-permute-start | bytes 3158024 | tf_op jit(solution)/shard_map/ppermute | solution.py:286

commit v12 on v11

--- a/solution.py
+++ b/solution.py
@@ -317,14 +317,14 @@
     )
     base, direction, sent = kernel_call(
         direction_kernel,
-        (array(classes, width), array(classes, width), array(row_count * CORES, 1, LANES)),
+        (array(classes, width), array(classes, width), array(depth * CORES, 1, LANES)),
         swap(sent, "z"), response, shares, count, residual, image,
     )
-    sent = kernel_call(relay_kernel, array(depth, 1, LANES), swap(sent, ("row", "c")))
+    sent = kernel_call(relay_kernel, array(row_count, 1, LANES), swap(sent, ("z", "c")))
     return kernel_call(
         functools.partial(step_kernel, sub_total, row_count * CORES),
         (array(classes, width), array(classes, width)),
-        swap(sent, "z"), residual, base, direction,
+        swap(sent, "row"), residual, base, direction,
     )
 
 

time: 168 us -> 168 us (level)
  no operation moved by 1% of the time
where the time goes in v12:
time: 168 us; the launch traced here: 167 us
  blocking collectives  150 us (89%)
  starting transfers between devices  8.92 us (5%)
  Pallas kernels  4.78 us (3%)
    all_to_all x9, blocking collectives, swap(): return lax.all_to_all(block, axis, 0, 0, tiled=True)  140 us
    all_gather x2, blocking collectives, body(): lax.all_gather(part, 'c', axis=0)  10.5 us
    ppermute x1, starting transfers between devices, body(): parcel = lax.ppermute(parcel, 'c', [(0, 1), (1, 0)])  8.92 us
    pallas_call x13, Pallas kernels, kernel_call(): pl.pallas_call(body, out_shape=out_shape, in_specs=[pl.BlockSpec(memory_s...  4.78 us
  transfers between devices with their start and end apart: 1, of which 1 were waited for; matrix products, arithmetic and copies ran while one was open for 0% of the time, Pallas kernels for 1%

profile of v12, /device:TPU:1, one launch (start us, length us, event | category | flops | bytes accessed | tf_op | source)
XLA Modules:
  0.0 167.3 jit_solution(10298446857564479372)
XLA Ops:
  0.6 0.0 copy-start.1
  0.6 1.3 constant_dynamic-slice_fusion.far
  1.9 0.0 copy-done.1
  2.0 0.0 copy-start
  2.0 0.0 copy-start.3
  2.0 0.1 pad_maximum_fusion
  2.1 0.0 copy-start.2
  2.1 8.9 %collective-permute-start = (bf16[4112,128]{1,0:T(8,128)(2,1)S(1)}, bf16[4112,128]{1,0:T(8,128)(2,1)S(1)}, u32[]{:S(2)}, u32[]{:S(2)}) collective-permute-start(bf16[4112,128]{1,0:T(8,128)(2,1)S(1)} %pad_maximum_fusion), channel_id=1, source_target_pairs={{0,1},{1,0},{2,3},{3,2},{4,5},{5,4},{6,7},{7,6},{8,9},{9,8},{10,11... | collective-permute-start | bytes 3158024 | tf_op jit(solution)/shard_map/ppermute | solution.py:286
  11.0 0.0 copy-done
  11.0 0.0 copy-done.3
  11.0 0.9 shard_map.59
  11.9 1.3 collective-permute-done.parcel
  13.3 0.4 shard_map.61
  13.7 21.5 %all_to_all.45.came = s16[16,16,256]{2,1,0:T(8,128)(2,1)S(1)} all-to-all(s16[16,16,256]{2,1,0:T(8,128)(2,1)S(1)} %shard_map.61), channel_id=1, replica_groups=mesh['row'=16,'z'=16,'c'=2] {'z'}, dimensions={0} | all-to-all | bytes 262144 | tf_op jit(solution)/shard_map/all_to_all | solution.py:256
  35.2 0.0 copy-done.2
  35.2 0.1 shard_map.62
  35.3 18.3 %all_to_all.46.came = bf16[16,16,256]{2,1,0:T(8,128)(2,1)S(1)} all-to-all(bf16[16,16,256]{2,1,0:T(8,128)(2,1)S(1)} %get-tuple-element.18), channel_id=1, replica_groups=mesh['row'=16,'z'=16,'c'=2] {'z'}, dimensions={0} | all-to-all | bytes 262144 | tf_op jit(solution)/shard_map/all_to_all | solution.py:256
  53.5 0.4 shard_map.63
  53.9 5.2 %all-gather = f32[4,16,256]{2,1,0:T(8,128)S(1)} all-gather(f32[2,16,256]{2,1,0:T(8,128)S(1)} %shard_map.63), channel_id=2, replica_groups=mesh['row'=16,'z'=16,'c'=2] {'c'}, dimensions={0}, use_global_device_ids=true | all-gather | bytes 98304 | tf_op jit(solution)/shard_map/all_gather | solution.py:299
  59.1 0.1 shard_map.64
  59.3 13.2 %all_to_all.47.came = s16[16,16,256]{2,1,0:T(8,128)(2,1)S(1)} all-to-all(s16[16,16,256]{2,1,0:T(8,128)(2,1)S(1)} %get-tuple-element.19), channel_id=1, replica_groups=mesh['row'=16,'z'=16,'c'=2] {'row'}, dimensions={0} | all-to-all | bytes 262144 | tf_op jit(solution)/shard_map/all_to_all | solution.py:256
  72.5 0.7 shard_map.65
  73.2 15.3 %all_to_all.48.came = bf16[16,16,256]{2,1,0:T(8,128)(2,1)S(1)} all-to-all(bf16[16,16,256]{2,1,0:T(8,128)(2,1)S(1)} %get-tuple-element.21), channel_id=1, replica_groups=mesh['row'=16,'z'=16,'c'=2] {'z'}, dimensions={0} | all-to-all | bytes 262144 | tf_op jit(solution)/shard_map/all_to_all | solution.py:256
  88.5 16.9 %all_to_all.49.came = bf16[16,16,256]{2,1,0:T(8,128)(2,1)S(1)} all-to-all(bf16[16,16,256]{2,1,0:T(8,128)(2,1)S(1)} %get-tuple-element.24), channel_id=1, replica_groups=mesh['row'=16,'z'=16,'c'=2] {'z'}, dimensions={0} | all-to-all | bytes 262144 | tf_op jit(solution)/shard_map/all_to_all | solution.py:256
  105.4 0.4 shard_map.67
  105.8 5.3 %all-gather.1 = f32[32,256]{1,0:T(8,128)S(1)} all-gather(f32[16,256]{1,0:T(8,128)S(1)} %shard_map.67), channel_id=3, replica_groups=mesh['row'=16,'z'=16,'c'=2] {'c'}, dimensions={0}, use_global_device_ids=true | all-gather | bytes 49152 | tf_op jit(solution)/shard_map/all_gather | solution.py:311
  111.1 10.6 %all_to_all.50.came = bf16[16,16,256]{2,1,0:T(8,128)(2,1)S(1)} all-to-all(bf16[16,16,256]{2,1,0:T(8,128)(2,1)S(1)} %shard_map.68), channel_id=1, replica_groups=mesh['row'=16,'z'=16,'c'=2] {'row'}, dimensions={0} | all-to-all | bytes 262144 | tf_op jit(solution)/shard_map/all_to_all | solution.py:256
  121.8 0.6 shard_map.69
  122.4 14.9 %all_to_all.51.came = bf16[16,16,256]{2,1,0:T(8,128)(2,1)S(1)} all-to-all(bf16[16,16,256]{2,1,0:T(8,128)(2,1)S(1)} %get-tuple-element.26), channel_id=1, replica_groups=mesh['row'=16,'z'=16,'c'=2] {'z'}, dimensions={0} | all-to-all | bytes 262144 | tf_op jit(solution)/shard_map/all_to_all | solution.py:256
  137.3 0.2 shard_map.70
  137.5 19.1 %all_to_all.52.came = f32[32,1,128]{2,1,0:T(1,128)S(1)} all-to-all(f32[32,1,128]{2,1,0:T(1,128)S(1)} %get-tuple-element.29), channel_id=1, replica_groups=mesh['row'=16,'z'=16,'c'=2] {'z','c'}, dimensions={0} | all-to-all | bytes 32768 | tf_op jit(solution)/shard_map/all_to_all | solution.py:256
  156.7 9.8 %all_to_all.53.came = f32[16,1,128]{2,1,0:T(1,128)S(1)} all-to-all(f32[16,1,128]{2,1,0:T(1,128)S(1)} %shard_map.71), channel_id=1, replica_groups=mesh['row'=16,'z'=16,'c'=2] {'row'}, dimensions={0} | all-to-all | bytes 16384 | tf_op jit(solution)/shard_map/all_to_all | solution.py:256
  166.5 0.8 shard_map.72
  (4 shorter events, 0.1 us)
Async XLA Ops:
  0.6 1.3 copy-start.1
  2.0 9.1 %copy-start = (bf16[8192,128]{1,0:T(8,128)(2,1)S(1)}, bf16[8192,128]{1,0:T(8,128)(2,1)}, u32[]{:S(2)}) copy-start(bf16[8192,128]{1,0:T(8,128)(2,1)} %param.4) | copy-start | bytes 6291460
  2.0 9.1 %copy-start.3 = (s32[4096]{0:T(1024)S(1)}, s32[4096]{0:T(1024)}, u32[]{:S(2)}) copy-start(s32[4096]{0:T(1024)} %param.7) | copy-start | bytes 49156
  2.1 33.1 %copy-start.2 = (s32[8192]{0:T(1024)S(1)}, s32[8192]{0:T(1024)}, u32[]{:S(2)}) copy-start(s32[8192]{0:T(1024)} %param.5) | copy-start | bytes 98308
  2.1 11.2 %collective-permute-start = (bf16[4112,128]{1,0:T(8,128)(2,1)S(1)}, bf16[4112,128]{1,0:T(8,128)(2,1)S(1)}, u32[]{:S(2)}, u32[]{:S(2)}) collective-permute-start(bf16[4112,128]{1,0:T(8,128)(2,1)S(1)} %pad_maximum_fusion), channel_id=1, source_target_pairs={{0,1},{1,0},{2,3},{3,2},{4,5},{5,4},{6,7},{7,6},{8,9},{9,8},{10,11... | collective-permute-start | bytes 3158024 | tf_op jit(solution)/shard_map/ppermute | solution.py:286
